TPU v7x, 256 devices: a whole 4x4x8 slice. The times are simulated.
256 devices in a mesh: dp: 32 (over z_hi, x, core), section: 8 (over z_lo, y).
Axes of the slice: x: 4, y: 4, z: 8 (z_hi: 4, z_lo: 2; z = z_hi * 2 + z_lo), core: 2. Of those that a mesh axis runs over, the one named last changes fastest.
Arguments:
- layer_inputs: bfloat16 [8, 8192, 4096], P('section', 'dp'), may hold values from -120 to 120
- output_grads: bfloat16 [8, 8192, 4096], P('section', 'dp'), may hold values from -120 to 120
- proj_in: bfloat16 [8, 4096, 64], P('section'), may hold values from -0.09375 to 0.09375
- proj_out: bfloat16 [8, 4096, 64], P('section'), may hold values from -0.09375 to 0.09375
- train_log: bfloat16 [8, 24576, 4096], P('section', 'dp'), may hold values from -6 to 6
- queries: bfloat16 [8, 1024, 4096], P('section', 'dp'), may hold values from -6 to 6
- query_owner: int32 [32], replicated, may hold values from 0 to 31, each once
Outputs:
- fresh_grads: bfloat16 [8, 32, 4096], P('section', 'dp')
- scores: float32 [1024, 24576], P('section', 'dp')
Inputs may be any that keep to these rules, and one draw needn't show every extreme that they name: `query_owner`: each stored block holds exactly one query block.
All inputs are finite; a program needn't handle non-finite values.
Results may differ from a plain program's by a relative error of at most 0.0065.
Values may be sent and summed in bfloat16 or wider, within the bound.
No kernel may reach another device: no remote copies, remote signals or barrier semaphores. Data moves between devices by JAX's collectives and lax.ppermute only.
A program may use at most 128 MiB of HBM per device.

v0:
```python
import jax
import jax.numpy as jnp
from jax import lax
from jax.sharding import PartitionSpec as P

SEQ = 256


def damped_inverse(factor):
    size = factor.shape[0]
    eye = jnp.eye(size, dtype=factor.dtype)
    damped = factor + 0.1 * jnp.trace(factor) / size * eye
    lower = jnp.linalg.cholesky(damped)
    solved = lax.linalg.triangular_solve(lower, eye, left_side=True, lower=True)
    return jnp.dot(solved.T, solved, precision=lax.Precision.HIGHEST)


def condition(block, out_half, in_half):
    rank = out_half.shape[0]
    matrices = block.reshape(block.shape[0], rank, rank)
    left = jnp.einsum("ok,qki->qoi", out_half, matrices, preferred_element_type=jnp.float32).astype(
        jnp.bfloat16
    )
    both = jnp.einsum("qok,ki->qoi", left, in_half, preferred_element_type=jnp.float32)
    return both.reshape(block.shape[0], rank * rank).astype(jnp.bfloat16)


def on_device(layer_inputs, output_grads, proj_in, proj_out, train_log, queries, query_owner):
    rank = proj_in.shape[2]
    local_tokens = layer_inputs.shape[1]
    total_tokens = local_tokens * lax.axis_size("dp")
    examples = local_tokens // SEQ
    layer = 0
    acts = jnp.dot(layer_inputs[layer], proj_in[layer], preferred_element_type=jnp.float32).astype(
        jnp.bfloat16
    )
    grads = jnp.dot(
        output_grads[layer], proj_out[layer], preferred_element_type=jnp.float32
    ).astype(jnp.bfloat16)
    per_example = lax.dot_general(
        grads.reshape(examples, SEQ, rank),
        acts.reshape(examples, SEQ, rank),
        (((1,), (1,)), ((0,), (0,))),
        preferred_element_type=jnp.float32,
    )
    fresh_list = [(per_example / SEQ).reshape(examples, rank * rank).astype(jnp.bfloat16)]
    in_list = [
        lax.dot_general(acts, acts, (((0,), (0,)), ((), ())), preferred_element_type=jnp.float32)
    ]
    out_list = [
        lax.dot_general(grads, grads, (((0,), (0,)), ((), ())), preferred_element_type=jnp.float32)
    ]
    fresh_grads = jnp.stack(fresh_list)
    in_sums, out_sums = lax.psum((jnp.stack(in_list), jnp.stack(out_list)), "dp")
    in_half = damped_inverse(in_sums[0] / total_tokens).astype(jnp.bfloat16)
    out_half = damped_inverse(out_sums[0] / total_tokens).astype(jnp.bfloat16)
    block_rows = queries.shape[1]
    dp_count = lax.axis_size("dp")
    conditioned = jnp.stack([condition(queries[0], out_half, in_half)])
    block = lax.all_gather(conditioned, "dp", axis=1, tiled=True)
    layer = 0
    total = lax.dot_general(
        block[layer], train_log[layer], (((1,), (1,)), ((), ())), preferred_element_type=jnp.float32
    )
    ordered = jnp.take(
        total.reshape(dp_count, block_rows, total.shape[1]), query_owner, axis=0
    ).reshape(total.shape)
    scores = lax.psum_scatter(ordered, "section", scatter_dimension=0, tiled=True)
    return (fresh_grads, scores)


def solution(mesh):
    placed = (
        P("section", "dp", None),
        P("section", "dp", None),
        P("section", None, None),
        P("section", None, None),
        P("section", "dp", None),
        P("section", "dp", None),
        P(),
    )
    return jax.shard_map(
        on_device,
        mesh=mesh,
        in_specs=placed,
        out_specs=(P("section", "dp", None), P("section", "dp")),
        check_vma=False,
    )
```

profile of v0, /device:TPU:1, one launch (start us, length us, event | category | flops | bytes accessed | tf_op | source)
XLA Modules:
  0.0 334.3 jit_solution(2542016616693476619)
XLA Ops:
  7.2 1.5 copy-done
  8.8 1.8 fusion.10
  10.7 2.5 fusion.7
  13.3 141.0 %all-reduce = (f32[1,64,64]{1,2,0:T(8,128)S(1)}, f32[1,64,64]{1,2,0:T(8,128)S(1)}) all-reduce(f32[1,64,64]{1,2,0:T(8,128)S(1)} %convolution_bitcast_fusion, f32[1,64,64]{1,2,0:T(8,128)S(1)} %convolution_bitcast_fusion.1), channel_id=1, replica_groups=mesh['dp'=32,'section'=8] {'dp'}, use_global_device_ids=true, to_apply=%region_4.7 | all-reduce | flops 8192 | bytes 65536 | tf_op jit(solution)/shard_map/psum | solution.py:54
  154.3 0.6 fusion.26
  154.9 0.6 fusion.29
  157.0 5.8 %cholesky.55 = f32[64,64]{1,0:T(8,128)S(1)} custom-call(f32[64,64]{1,0:T(8,128)S(1)} %fusion.25), custom_call_target="Cholesky" | custom-call | tf_op jit(solution)/shard_map/jit(cholesky)/cholesky | solution.py:13
  162.8 0.6 compare_reduce_fusion
  163.5 0.7 fusion.23
  164.1 4.9 %custom-call.7 = f32[1,64,64]{1,2,0:T(8,128)S(1)} custom-call(f32[1,64,64]{2,1,0:T(8,128)S(1)} %fusion.23), custom_call_target="InvertDiagBlocksLowerTriangular" | custom-call | tf_op jit(solution)/shard_map/triangular_solve/custom-call.0 | solution.py:14
  169.0 0.3 fusion.18
  169.6 5.8 %cholesky.44 = f32[64,64]{1,0:T(8,128)S(1)} custom-call(f32[64,64]{1,0:T(8,128)S(1)} %fusion.28), custom_call_target="Cholesky" | custom-call | tf_op jit(solution)/shard_map/jit(cholesky)/cholesky | solution.py:13
  175.5 0.6 compare_reduce_fusion.1
  176.2 0.7 fusion.22
  176.8 4.9 %custom-call.6 = f32[1,64,64]{1,2,0:T(8,128)S(1)} custom-call(f32[1,64,64]{2,1,0:T(8,128)S(1)} %fusion.22), custom_call_target="InvertDiagBlocksLowerTriangular" | custom-call | tf_op jit(solution)/shard_map/triangular_solve/custom-call.0 | solution.py:14
  182.2 0.5 reshape_squeeze.3
  182.8 0.5 convolution_convert_fusion
  183.2 1.2 convert_element_type.62
  184.7 76.8 %all-gather.2.cloned.1.call-done = bf16[1,1024,4096]{2,1,0:T(8,128)(2,1)} async-done(((bf16[1,32,4096]{2,1,0:T(8,128)(2,1)}), bf16[1,1024,4096]{2,1,0:T(8,128)(2,1)}) %all-gather.2.cloned.1.call-update) | async-done | bytes 8388624 | tf_op jit(solution)/shard_map/all_gather | solution.py:60
  261.4 12.2 %fusion = f32[32,32,768]{2,1,0:T(8,128)} fusion(bf16[32,32,4096]{2,1,0:T(8,128)(2,1)} %bitcast.77, bf16[1,768,4096]{2,1,0:T(8,128)(2,1)} %param.14), kind=kOutput, calls=%fused_computation.1 | convolution fusion | flops 6442450944 | bytes 17825792 | tf_op jit(solution)/shard_map/dot_general | solution.py:62
  273.6 4.3 %gather_fusion = f32[32,32,768]{2,1,0:T(8,128)} fusion(f32[32,32,768]{2,1,0:T(8,128)} %fusion, s32[1024]{0:T(1024)S(1)} %pad_clamp_fusion), kind=kCustom, calls=%fused_computation | custom fusion | bytes 6291584 | tf_op jit(solution)/shard_map/jit(_take)/gather | solution.py:65
  277.9 3.9 %bitcast_select_fusion = f32[1024,768]{1,0:T(8,128)} fusion(f32[32,32,768]{2,1,0:T(8,128)} %gather_fusion, pred[1024]{0:T(1024)(128)(4,1)S(1)} %broadcast_in_dim.23), kind=kLoop, calls=%fused_computation.3 | loop fusion | flops 786432 | bytes 6292480 | tf_op jit(solution)/shard_map/jit(_take)/select_n | solution.py:65
  281.9 0.7 convert_element_type.55
  282.7 44.8 %reduce-scatter.2.cloned.1.call-done = f32[128,768]{1,0:T(8,128)} async-done(((f32[1024,768]{1,0:T(8,128)}), f32[128,768]{1,0:T(8,128)}) %reduce-scatter.2.cloned.1.call-update) | async-done | bytes 393232 | tf_op jit(solution)/shard_map/reduce_scatter | solution.py:68
  (27 shorter events, 1.6 us)
Async XLA Ops:
  7.2 1.6 copy-start
  7.2 175.0 %copy-start.1 = (bf16[1,32,4096]{2,1,0:T(8,128)(2,1)S(1)}, bf16[1,32,4096]{2,1,0:T(8,128)(2,1)}, u32[]{:S(2)}) copy-start(bf16[1,32,4096]{2,1,0:T(8,128)(2,1)} %param.15) | copy-start | bytes 786436
  7.2 254.3 %all-gather.2.cloned.1.call-start = ((), (), s32[]{:S(2)}) async-start(), calls=%async_computation.1 | async-start | bytes 8650752 | tf_op jit(solution)/shard_map/all_gather | solution.py:60
  10.7 173.8 %copy-start.2 = (s32[32]{0:T(128)S(1)}, s32[32]{0:T(128)}, u32[]{:S(2)}) copy-start(s32[32]{0:T(128)} %param.16) | copy-start | bytes 388
  184.4 143.0 %reduce-scatter.2.cloned.1.call-start = ((), (), s32[]{:S(2)}) async-start(), calls=%async_computation.2 | async-start | bytes 3538944 | tf_op jit(solution)/shard_map/reduce_scatter | solution.py:68
Sparse Core Ops, SparseCore 0:
  184.6 76.8 all-gather.1
  281.9 45.4 reduce-scatter.1
where the time goes:
time: 337 us; the launch traced here: 334 us
  blocking collectives  141 us (42%)
  waiting for transfers between devices  122 us (36%)
  other arithmetic  29.3 us (9%)
  matrix products  18.2 us (5%)
  between operations  15.5 us (5%)
  local copies, waits for them, and re-layouts  8.57 us (3%)
    psum x1, blocking collectives, on_device(): lax.psum((jnp.stack(in_list), jnp.stack(out_list)), 'dp')  141 us
    all_gather x1, waiting for transfers between devices, on_device(): block = lax.all_gather(conditioned, 'dp', axis=1, tiled=True)  76.8 us
    reduce_scatter x1, waiting for transfers between devices, on_device(): lax.psum_scatter(ordered, 'section', scatter_dimension=0, tiled=True)  44.8 us
    another operation x6, other arithmetic, damped_inverse(): lower = jnp.linalg.cholesky(damped)  13 us
    dot_general x1, matrix products, on_device(): lax.dot_general(block[layer], train_log[layer], (((1,), (1,)), ((), ())),...  12.2 us
    another operation x4, other arithmetic, damped_inverse(): solved = lax.linalg.triangular_solve(lower, eye, left_side=True, lower=True)  11.1 us
  transfers between devices with their start and end apart: 2, of which 2 were waited for; matrix products, arithmetic and copies ran while one was open for 0% of the time, Pallas kernels for 0%

commit v1 on v0

--- a/solution.py
+++ b/solution.py
@@ -4,6 +4,8 @@
 from jax.sharding import PartitionSpec as P
 
 SEQ = 256
+DP = ("zh", "x", "core")
+SECTION = ("zl", "y")
 
 
 def damped_inverse(factor):
@@ -28,7 +30,7 @@
 def on_device(layer_inputs, output_grads, proj_in, proj_out, train_log, queries, query_owner):
     rank = proj_in.shape[2]
     local_tokens = layer_inputs.shape[1]
-    total_tokens = local_tokens * lax.axis_size("dp")
+    total_tokens = local_tokens * lax.axis_size(DP)
     examples = local_tokens // SEQ
     layer = 0
     acts = jnp.dot(layer_inputs[layer], proj_in[layer], preferred_element_type=jnp.float32).astype(
@@ -51,38 +53,50 @@
         lax.dot_general(grads, grads, (((0,), (0,)), ((), ())), preferred_element_type=jnp.float32)
     ]
     fresh_grads = jnp.stack(fresh_list)
-    in_sums, out_sums = lax.psum((jnp.stack(in_list), jnp.stack(out_list)), "dp")
-    in_half = damped_inverse(in_sums[0] / total_tokens).astype(jnp.bfloat16)
-    out_half = damped_inverse(out_sums[0] / total_tokens).astype(jnp.bfloat16)
+    sums = jnp.concatenate([in_list[0], out_list[0]], axis=1)
+    for axis in ("core", "x", "zh"):
+        size = lax.axis_size(axis)
+        stride = 1
+        while stride < size:
+            sums = sums + lax.ppermute(sums, axis, [(i, i ^ stride) for i in range(size)])
+            stride *= 2
+    in_half = damped_inverse(sums[:, :rank] / total_tokens).astype(jnp.bfloat16)
+    out_half = damped_inverse(sums[:, rank:] / total_tokens).astype(jnp.bfloat16)
     block_rows = queries.shape[1]
-    dp_count = lax.axis_size("dp")
+    dp_count = lax.axis_size(DP)
     conditioned = jnp.stack([condition(queries[0], out_half, in_half)])
-    block = lax.all_gather(conditioned, "dp", axis=1, tiled=True)
+    block = lax.all_gather(conditioned, DP, axis=1, tiled=True)
     layer = 0
     total = lax.dot_general(
         block[layer], train_log[layer], (((1,), (1,)), ((), ())), preferred_element_type=jnp.float32
     )
     ordered = jnp.take(
-        total.reshape(dp_count, block_rows, total.shape[1]), query_owner, axis=0
-    ).reshape(total.shape)
-    scores = lax.psum_scatter(ordered, "section", scatter_dimension=0, tiled=True)
+        total.astype(jnp.bfloat16).reshape(dp_count, block_rows, total.shape[1]), query_owner, axis=0
+    )
+    parts = lax.axis_size(SECTION)
+    ordered = ordered.reshape(parts, total.shape[0] // parts, total.shape[1])
+    arrived = lax.all_to_all(ordered, SECTION, split_axis=0, concat_axis=0, tiled=True)
+    scores = jnp.sum(arrived.astype(jnp.float32), axis=0)
     return (fresh_grads, scores)
 
 
 def solution(mesh):
+    fine = jax.sharding.Mesh(
+        mesh.devices.reshape(4, 4, 2, 2, 4), ("zh", "x", "core", "zl", "y")
+    )
     placed = (
-        P("section", "dp", None),
-        P("section", "dp", None),
-        P("section", None, None),
-        P("section", None, None),
-        P("section", "dp", None),
-        P("section", "dp", None),
+        P(SECTION, DP, None),
+        P(SECTION, DP, None),
+        P(SECTION, None, None),
+        P(SECTION, None, None),
+        P(SECTION, DP, None),
+        P(SECTION, DP, None),
         P(),
     )
     return jax.shard_map(
         on_device,
-        mesh=mesh,
+        mesh=fine,
         in_specs=placed,
-        out_specs=(P("section", "dp", None), P("section", "dp")),
+        out_specs=(P(SECTION, DP, None), P(SECTION, DP)),
         check_vma=False,
     )

time: 337 us -> 203 us (0.60)
  blocking collectives: 141 us -> 0 us
  starting transfers between devices: 0.08 us -> 18.9 us
  waiting for transfers between devices: 122 us -> 114 us
    psum x1 -> x0, blocking collectives: 141 us -> none  [on_device(): lax.psum((jnp.stack(in_list), jnp.stack(out_list)), 'dp')]
    reduce_scatter x1 -> x0, waiting for transfers between devices: 44.8 us -> none  [on_device(): lax.psum_scatter(ordered, 'section', scatter_dimension=0, tiled=True)]
    all_to_all x0 -> x1, waiting for transfers between devices: none -> 19.9 us  [on_device(): lax.all_to_all(ordered, SECTION, split_axis=0, concat_axis=0, tiled=True)]
    ppermute x0 -> x5, waiting for transfers between devices: none -> 12.4 us  [on_device(): lax.ppermute(sums, axis, [(i, i ^ stride) for i in range(size)])]
    ppermute x0 -> x5, starting transfers between devices: none -> 11.3 us  [on_device(): lax.ppermute(sums, axis, [(i, i ^ stride) for i in range(size)])]
    all_to_all x0 -> x1, starting transfers between devices: none -> 7.6 us  [on_device(): lax.all_to_all(ordered, SECTION, split_axis=0, concat_axis=0, tiled=True)]
    all_gather x1, waiting for transfers between devices: 76.8 us -> 81.9 us  [on_device(): block = lax.all_gather(conditioned, DP, axis=1, tiled=True)]
  transfers between devices with their start and end apart: 2 -> 7, of which waited for: 2 -> 7; matrix products, arithmetic and copies ran while one was open for 0% -> 1% of each run, Pallas kernels for 0% -> 0%
where the time goes in v1:
time: 203 us
  waiting for transfers between devices  114 us (56%)
  other arithmetic  30.1 us (15%)
  starting transfers between devices  18.9 us (9%)
  matrix products  16.4 us (8%)
  between operations  15.5 us (8%)
  local copies, waits for them, and re-layouts  7.58 us (4%)
    all_gather x1, waiting for transfers between devices, on_device(): block = lax.all_gather(conditioned, DP, axis=1, tiled=True)  81.9 us
    all_to_all x1, waiting for transfers between devices, on_device(): lax.all_to_all(ordered, SECTION, split_axis=0, concat_axis=0, tiled=True)  19.9 us
    another operation x6, other arithmetic, damped_inverse(): lower = jnp.linalg.cholesky(damped)  13 us
    ppermute x5, waiting for transfers between devices, on_device(): lax.ppermute(sums, axis, [(i, i ^ stride) for i in range(size)])  12.4 us
    dot_general x1, matrix products, on_device(): lax.dot_general(block[layer], train_log[layer], (((1,), (1,)), ((), ())),...  11.9 us
    ppermute x5, starting transfers between devices, on_device(): lax.ppermute(sums, axis, [(i, i ^ stride) for i in range(size)])  11.3 us
    another operation x4, other arithmetic, damped_inverse(): solved = lax.linalg.triangular_solve(lower, eye, left_side=True, lower=True)  11.1 us
    all_to_all x1, starting transfers between devices, on_device(): lax.all_to_all(ordered, SECTION, split_axis=0, concat_axis=0, tiled=True)  7.6 us
  transfers between devices with their start and end apart: 7, of which 7 were waited for; matrix products, arithmetic and copies ran while one was open for 1% of the time, Pallas kernels for 0%

profile of v1, /device:TPU:1, one launch (start us, length us, event | category | flops | bytes accessed | tf_op | source)
XLA Modules:
  0.0 202.6 jit_solution(6440971390388660692)
XLA Ops:
  7.2 1.5 copy-done
  8.8 1.9 fusion.13
  10.9 0.8 fusion.16
  11.8 3.3 %collective-permute-start = (f32[64,128]{0,1:T(8,128)S(1)}, f32[64,128]{0,1:T(8,128)S(1)}, u32[]{:S(2)}, u32[]{:S(2)}) collective-permute-start(f32[64,128]{0,1:T(8,128)S(1)} %pad_maximum_fusion), channel_id=1, source_target_pairs={{0,8},{8,0},{1,9},{9,1},{2,10},{10,2},{3,11},{11,3},{4,12},{12,4},... | collective-permute-start | bytes 98312 | tf_op jit(solution)/shard_map/ppermute | solution.py:61
  15.1 0.9 collective-permute-done
  16.1 3.1 %collective-permute-done.1 = f32[64,128]{0,1:T(8,128)S(1)} collective-permute-done((f32[64,128]{0,1:T(8,128)S(1)}, f32[64,128]{0,1:T(8,128)S(1)}, u32[]{:S(2)}, u32[]{:S(2)}) %collective-permute-start.1) | collective-permute-done | bytes 32800 | tf_op jit(solution)/shard_map/ppermute | solution.py:61
  19.2 1.1 collective-permute-start.2
  20.3 3.6 %collective-permute-done.2 = f32[64,128]{0,1:T(8,128)S(1)} collective-permute-done((f32[64,128]{0,1:T(8,128)S(1)}, f32[64,128]{0,1:T(8,128)S(1)}, u32[]{:S(2)}, u32[]{:S(2)}) %collective-permute-start.2) | collective-permute-done | bytes 32800 | tf_op jit(solution)/shard_map/ppermute | solution.py:61
  24.0 1.3 collective-permute-start.3
  25.3 3.5 %collective-permute-done.3 = f32[64,128]{0,1:T(8,128)S(1)} collective-permute-done((f32[64,128]{0,1:T(8,128)S(1)}, f32[64,128]{0,1:T(8,128)S(1)}, u32[]{:S(2)}, u32[]{:S(2)}) %collective-permute-start.3) | collective-permute-done | bytes 32800 | tf_op jit(solution)/shard_map/ppermute | solution.py:61
  28.8 5.4 %collective-permute-start.4 = (f32[64,128]{0,1:T(8,128)S(1)}, f32[64,128]{0,1:T(8,128)S(1)}, u32[]{:S(2)}, u32[]{:S(2)}) collective-permute-start(f32[64,128]{0,1:T(8,128)S(1)} %add.42), channel_id=1, source_target_pairs={{0,128},{64,192},{128,0},{192,64},{1,129},{65,193},{129,1},{193,65... | collective-permute-start | bytes 98312 | tf_op jit(solution)/shard_map/ppermute | solution.py:61
  34.8 1.3 collective-permute-done.4
  38.2 5.8 %cholesky.55 = f32[64,64]{1,0:T(8,128)S(1)} custom-call(f32[64,64]{1,0:T(8,128)S(1)} %get-tuple-element.8), custom_call_target="Cholesky" | custom-call | tf_op jit(solution)/shard_map/jit(cholesky)/cholesky | solution.py:15
  45.4 4.9 %custom-call.7 = f32[1,64,64]{1,2,0:T(8,128)S(1)} custom-call(f32[1,64,64]{2,1,0:T(8,128)S(1)} %fusion.29), custom_call_target="InvertDiagBlocksLowerTriangular" | custom-call | tf_op jit(solution)/shard_map/triangular_solve/custom-call.0 | solution.py:16
  50.8 5.8 %cholesky.44 = f32[64,64]{1,0:T(8,128)S(1)} custom-call(f32[64,64]{1,0:T(8,128)S(1)} %get-tuple-element.9), custom_call_target="Cholesky" | custom-call | tf_op jit(solution)/shard_map/jit(cholesky)/cholesky | solution.py:15
  58.0 4.9 %custom-call.6 = f32[1,64,64]{1,2,0:T(8,128)S(1)} custom-call(f32[1,64,64]{2,1,0:T(8,128)S(1)} %fusion.28), custom_call_target="InvertDiagBlocksLowerTriangular" | custom-call | tf_op jit(solution)/shard_map/triangular_solve/custom-call.0 | solution.py:16
  63.9 1.2 convert_element_type.68
  65.4 81.9 %all-gather.2.cloned.1.call-done = bf16[1,1024,4096]{2,1,0:T(8,128)(2,1)} async-done(((bf16[1,32,4096]{2,1,0:T(8,128)(2,1)}), bf16[1,1024,4096]{2,1,0:T(8,128)(2,1)}) %all-gather.2.cloned.1.call-update) | async-done | bytes 8388624 | tf_op jit(solution)/shard_map/all_gather | solution.py:68
  147.2 11.9 %fusion.7 = bf16[1024,768]{1,0:T(8,128)(2,1)} fusion(bf16[1,768,4096]{2,1,0:T(8,128)(2,1)} %param.14, bf16[1,1024,4096]{2,1,0:T(8,128)(2,1)} %all-gather.2.cloned.1.call-done), kind=kOutput, calls=%fused_computation.9 | convolution fusion | flops 6443237376 | bytes 16252928 | tf_op jit(solution)/shard_map/dot_general | solution.py:70
  159.1 3.2 %gather_fusion = bf16[32,32,768]{2,1,0:T(8,128)(2,1)} fusion(bf16[32,32,768]{2,1,0:T(8,128)(2,1)} %bitcast.70, s32[1024]{0:T(1024)S(1)} %pad_clamp_fusion), kind=kCustom, calls=%fused_computation | custom fusion | bytes 3145856 | tf_op jit(solution)/shard_map/jit(_take)/gather | solution.py:73
  162.3 2.8 %bitcast_select_fusion = bf16[8,128,768]{2,1,0:T(8,128)(2,1)} fusion(pred[8,128]{1,0:T(8,128)(4,1)S(1)} %broadcast_in_dim.26, bf16[8,128,768]{2,1,0:T(8,128)(2,1)} %bitcast.69), kind=kLoop, calls=%fused_computation.10 | loop fusion | flops 786432 | bytes 3146752 | tf_op jit(solution)/shard_map/jit(_take)/select_n | solution.py:73
  165.1 7.6 %all-to-all-start = ((bf16[8,128,768]{2,1,0:T(8,128)(2,1)}), bf16[8,128,768]{2,1,0:T(8,128)(2,1)}, u32[]{:S(2)}, u32[]{:S(2)}) async-start(bf16[8,128,768]{2,1,0:T(8,128)(2,1)} %bitcast_select_fusion), calls=%async_computation | async-start | bytes 3145728 | tf_op jit(solution)/shard_map/all_to_all | solution.py:78
  173.5 19.9 %all-to-all-done = bf16[8,128,768]{2,1,0:T(8,128)(2,1)} async-done(((bf16[8,128,768]{2,1,0:T(8,128)(2,1)}), bf16[8,128,768]{2,1,0:T(8,128)(2,1)}, u32[]{:S(2)}, u32[]{:S(2)}) %all-to-all-start) | async-done | bytes 1572896 | tf_op jit(solution)/shard_map/all_to_all | solution.py:78
  193.4 2.4 %convert_reduce_fusion = f32[128,768]{1,0:T(8,128)} fusion(bf16[8,128,768]{2,1,0:T(8,128)(2,1)} %all-to-all-done), kind=kLoop, calls=%fused_computation.4 | loop fusion | flops 1474560 | bytes 1966080 | tf_op jit(solution)/shard_map/reduce_sum | solution.py:79
  (45 shorter events, 7.0 us)
Async XLA Ops:
  7.2 1.6 copy-start
  7.2 3.7 %copy-start.2 = (bf16[1,4096,64]{1,2,0:T(8,128)(2,1)S(1)}, bf16[1,4096,64]{1,2,0:T(8,128)(2,1)}, u32[]{:S(2)}) copy-start(bf16[1,4096,64]{1,2,0:T(8,128)(2,1)} %param.12) | copy-start | bytes 1572868
  7.2 140.1 %all-gather.2.cloned.1.call-start = ((), (), s32[]{:S(2)}) async-start(), calls=%async_computation.1 | async-start | bytes 8650752 | tf_op jit(solution)/shard_map/all_gather | solution.py:68
  8.8 2.1 %copy-start.1 = (bf16[1,256,4096]{2,1,0:T(8,128)(2,1)S(1)}, bf16[1,256,4096]{2,1,0:T(8,128)(2,1)}, u32[]{:S(2)}) copy-start(bf16[1,256,4096]{2,1,0:T(8,128)(2,1)} %param.10) | copy-start | bytes 6291460
  10.7 23.5 %copy-start.3 = (bf16[1,32,4096]{2,1,0:T(8,128)(2,1)S(1)}, bf16[1,32,4096]{2,1,0:T(8,128)(2,1)}, u32[]{:S(2)}) copy-start(bf16[1,32,4096]{2,1,0:T(8,128)(2,1)} %param.15) | copy-start | bytes 786436
  11.8 4.2 %collective-permute-start = (f32[64,128]{0,1:T(8,128)S(1)}, f32[64,128]{0,1:T(8,128)S(1)}, u32[]{:S(2)}, u32[]{:S(2)}) collective-permute-start(f32[64,128]{0,1:T(8,128)S(1)} %pad_maximum_fusion), channel_id=1, source_target_pairs={{0,8},{8,0},{1,9},{9,1},{2,10},{10,2},{3,11},{11,3},{4,12},{12,4},... | collective-permute-start | bytes 98312 | tf_op jit(solution)/shard_map/ppermute | solution.py:61
  16.0 3.2 %collective-permute-start.1 = (f32[64,128]{0,1:T(8,128)S(1)}, f32[64,128]{0,1:T(8,128)S(1)}, u32[]{:S(2)}, u32[]{:S(2)}) collective-permute-start(f32[64,128]{0,1:T(8,128)S(1)} %fusion.34), channel_id=1, source_target_pairs={{0,16},{16,0},{32,48},{48,32},{1,17},{17,1},{33,49},{49,33},{2,18}... | collective-permute-start | bytes 98312 | tf_op jit(solution)/shard_map/ppermute | solution.py:61
  19.2 4.7 %collective-permute-start.2 = (f32[64,128]{0,1:T(8,128)S(1)}, f32[64,128]{0,1:T(8,128)S(1)}, u32[]{:S(2)}, u32[]{:S(2)}) collective-permute-start(f32[64,128]{0,1:T(8,128)S(1)} %add.40), channel_id=1, source_target_pairs={{0,32},{16,48},{32,0},{48,16},{1,33},{17,49},{33,1},{49,17},{2,34}... | collective-permute-start | bytes 98312 | tf_op jit(solution)/shard_map/ppermute | solution.py:61
  24.0 4.8 %collective-permute-start.3 = (f32[64,128]{0,1:T(8,128)S(1)}, f32[64,128]{0,1:T(8,128)S(1)}, u32[]{:S(2)}, u32[]{:S(2)}) collective-permute-start(f32[64,128]{0,1:T(8,128)S(1)} %add.41), channel_id=1, source_target_pairs={{0,64},{64,0},{128,192},{192,128},{1,65},{65,1},{129,193},{193,129... | collective-permute-start | bytes 98312 | tf_op jit(solution)/shard_map/ppermute | solution.py:61
  28.8 36.3 %copy-start.4 = (s32[32]{0:T(128)S(1)}, s32[32]{0:T(128)}, u32[]{:S(2)}) copy-start(s32[32]{0:T(128)} %param.16) | copy-start | bytes 388
  28.8 7.3 %collective-permute-start.4 = (f32[64,128]{0,1:T(8,128)S(1)}, f32[64,128]{0,1:T(8,128)S(1)}, u32[]{:S(2)}, u32[]{:S(2)}) collective-permute-start(f32[64,128]{0,1:T(8,128)S(1)} %add.42), channel_id=1, source_target_pairs={{0,128},{64,192},{128,0},{192,64},{1,129},{65,193},{129,1},{193,65... | collective-permute-start | bytes 98312 | tf_op jit(solution)/shard_map/ppermute | solution.py:61
  165.1 28.3 %all-to-all-start = ((bf16[8,128,768]{2,1,0:T(8,128)(2,1)}), bf16[8,128,768]{2,1,0:T(8,128)(2,1)}, u32[]{:S(2)}, u32[]{:S(2)}) async-start(bf16[8,128,768]{2,1,0:T(8,128)(2,1)} %bitcast_select_fusion), calls=%async_computation | async-start | bytes 3145728 | tf_op jit(solution)/shard_map/all_to_all | solution.py:78
Sparse Core Ops, SparseCore 0:
  65.2 82.0 all-gather.1

commit v2 on v1

v2 whole, which is shorter than its diff:
```python
import functools

import jax
import jax.numpy as jnp
from jax import lax
from jax.experimental import pallas as pl
from jax.experimental.pallas import tpu as pltpu
from jax.sharding import PartitionSpec as P

SEQ = 256
RANK = 64
DP = ("zh", "x", "core")
SECTION = ("zl", "y")

def shuffle_kernel(t_ref, x_ref, wide):
    rows = t_ref.shape[0]
    width = t_ref.shape[1]
    for j in range(width // 128):
        wide[128*j:128*j+128, :] = t_ref[:, 128*j:128*j+128].astype(jnp.float32).T
    for i in range(RANK):
        x_ref[RANK*i:RANK*i+RANK, :] = wide[pl.ds(i, RANK, stride=RANK), :].astype(jnp.bfloat16)
def shuffle(t):
    n,w=t.shape
    return pl.pallas_call(shuffle_kernel, grid=(n//128,),
        in_specs=[pl.BlockSpec((128,w),lambda j:(j,0))],
        out_specs=pl.BlockSpec((w,128),lambda j:(0,j)),
        out_shape=jax.ShapeDtypeStruct((w,n),jnp.bfloat16),
        scratch_shapes=[pltpu.VMEM((w,128),jnp.float32)],
        compiler_params=pltpu.CompilerParams(vmem_limit_bytes=32*2**20),
        cost_estimate=pl.CostEstimate(flops=2*n*w*64,bytes_accessed=4*n*w,transcendentals=0),
    )(t)
def weigh_kernel(x_ref, a_ref, b_ref, y_ref, lo, hi):
    halves=(lo,hi)
    a=a_ref[...]; b=b_ref[...]
    w=x_ref.shape[0]
    for g in range(w//256):
        y=jnp.dot(a, x_ref[256*g:256*g+256,:], preferred_element_type=jnp.float32)
        lo[256*g:256*g+256,:]=y[:,:128]
        hi[256*g:256*g+256,:]=y[:,128:]
    for g in range(w//256):
        parts=[]
        for k in range(4*g,4*g+4):
            parts.append(jnp.concatenate([h[pl.ds(k,RANK,stride=RANK),:] for h in halves],axis=1).astype(jnp.bfloat16))
        z=jnp.concatenate(parts,axis=0)
        y_ref[256*g:256*g+256,:]=jnp.dot(b,z,preferred_element_type=jnp.float32).astype(jnp.bfloat16)
def weigh(x,a,b):
    w,n=x.shape
    return pl.pallas_call(weigh_kernel, grid=(n//256,),
        in_specs=[pl.BlockSpec((w,256),lambda j:(0,j)),pl.BlockSpec((256,256),lambda j:(0,0)),pl.BlockSpec((256,256),lambda j:(0,0))],
        out_specs=pl.BlockSpec((w,256),lambda j:(0,j)),
        out_shape=jax.ShapeDtypeStruct((w,n),jnp.bfloat16),
        scratch_shapes=[pltpu.VMEM((w,128),jnp.float32)]*2,
        compiler_params=pltpu.CompilerParams(vmem_limit_bytes=32*2**20),
        cost_estimate=pl.CostEstimate(flops=4*n*w*256,bytes_accessed=4*n*w,transcendentals=0),
    )(x,a,b)
def blocks(m):
    four=jnp.concatenate([m]*4,axis=1)
    four=jnp.concatenate([four]*4,axis=0)
    r=lax.broadcasted_iota(jnp.int32,four.shape,0)//RANK
    c=lax.broadcasted_iota(jnp.int32,four.shape,1)//RANK
    return jnp.where(r==c,four,0.0).astype(jnp.bfloat16)
def inverse_kernel(tokens, s_ref, a_ref, b_ref):
    m=s_ref[...]/tokens
    row=lax.broadcasted_iota(jnp.int32,m.shape,0)
    lane=lax.broadcasted_iota(jnp.int32,m.shape,1)
    left=lane<RANK
    lcol=jnp.where(left,lane,lane-RANK)
    diag=jnp.where(row==lcol,m,0.0)
    tl=jnp.sum(jnp.where(left,diag,0.0)); tr=jnp.sum(jnp.where(left,0.0,diag))
    m=m+jnp.where(row==lcol,jnp.where(left,tl,tr)*(0.1/RANK),0.0)
    for k in range(RANK):
        pr=m[k:k+1,:]
        l1=left[:1]
        piv=jnp.where(l1,pr[:,k:k+1],pr[:,RANK+k:RANK+k+1])
        at=lcol==k
        scaled=jnp.where(at[:1],1.0,pr)/piv
        col=jnp.where(left,m[:,k:k+1],m[:,RANK+k:RANK+k+1])
        m=jnp.where(row==k,scaled,jnp.where(at,0.0,m)-col*scaled)
    inb=m[:,:RANK]; outb=m[:,RANK:]
    a_ref[...]=blocks(outb.T)
    b_ref[...]=blocks(inb)
def inverses(s,tokens):
    return pl.pallas_call(functools.partial(inverse_kernel,tokens),
        out_shape=[jax.ShapeDtypeStruct((256,256),jnp.bfloat16)]*2,
        cost_estimate=pl.CostEstimate(flops=64*64*128*2,bytes_accessed=300000,transcendentals=0),
    )(s)


def dp_sum(value):
    for axis in ("core", "x", "zh"):
        last = lax.axis_size(axis) - 1
        value = value + lax.ppermute(value, axis, [(i, i ^ 1) for i in range(last + 1)])
        if last > 1:
            value = value + lax.ppermute(value, axis, [(i, last - i) for i in range(last + 1)])
    return value


def on_device(layer_inputs, output_grads, proj_in, proj_out, train_log, queries, query_owner):
    local_tokens = layer_inputs.shape[1]
    total_tokens = local_tokens * lax.axis_size(DP)
    block = lax.all_gather(queries[0], DP, axis=0, tiled=True)
    acts = jnp.dot(layer_inputs[0], proj_in[0], preferred_element_type=jnp.float32).astype(
        jnp.bfloat16
    )
    grads = jnp.dot(output_grads[0], proj_out[0], preferred_element_type=jnp.float32).astype(
        jnp.bfloat16
    )
    down = (((0,), (0,)), ((), ()))
    in_sum = lax.dot_general(acts, acts, down, preferred_element_type=jnp.float32)
    out_sum = lax.dot_general(grads, grads, down, preferred_element_type=jnp.float32)
    sums = dp_sum(jnp.concatenate([in_sum, out_sum], axis=1))
    examples = local_tokens // SEQ
    per_example = lax.dot_general(
        grads.reshape(examples, SEQ, RANK),
        acts.reshape(examples, SEQ, RANK),
        (((1,), (1,)), ((0,), (0,))),
        preferred_element_type=jnp.float32,
    )
    fresh_grads = (per_example / SEQ).reshape(1, examples, RANK * RANK).astype(jnp.bfloat16)
    turned = shuffle(train_log[0])
    out_blocks, in_blocks = inverses(sums, total_tokens)
    weighed = weigh(turned, out_blocks, in_blocks)
    total = jnp.dot(block, weighed, preferred_element_type=jnp.float32).astype(jnp.bfloat16)
    count = query_owner.shape[0]
    ordered = jnp.take(
        total.reshape(count, total.shape[0] // count, total.shape[1]), query_owner, axis=0
    )
    parts = lax.axis_size(SECTION)
    ordered = ordered.reshape(parts, total.shape[0] // parts, total.shape[1])
    arrived = lax.all_to_all(ordered, SECTION, split_axis=0, concat_axis=0, tiled=True)
    scores = jnp.sum(arrived.astype(jnp.float32), axis=0)
    return (fresh_grads, scores)


def solution(mesh):
    fine = jax.sharding.Mesh(
        mesh.devices.reshape(4, 4, 2, 2, 4), ("zh", "x", "core", "zl", "y")
    )
    placed = (
        P(SECTION, DP, None),
        P(SECTION, DP, None),
        P(SECTION, None, None),
        P(SECTION, None, None),
        P(SECTION, DP, None),
        P(SECTION, DP, None),
        P(),
    )
    return jax.shard_map(
        on_device,
        mesh=fine,
        in_specs=placed,
        out_specs=(P(SECTION, DP, None), P(SECTION, DP)),
        check_vma=False,
    )
```

time: 203 us -> 154 us (0.76)
  waiting for transfers between devices: 114 us -> 53.5 us
  Pallas kernels: 0 us -> 27.4 us
  other arithmetic: 30.1 us -> 6.03 us
  local copies, waits for them, and re-layouts: 7.58 us -> 20.5 us
    all_gather x1, waiting for transfers between devices: 81.9 us -> 23.6 us  [on_device(): block = lax.all_gather(queries[0], DP, axis=0, tiled=True)]
    pallas_call x0 -> x3, Pallas kernels: none -> 27.4 us  [the longest x1 10.6 us: weigh(): pl.pallas_call(weigh_kernel, grid=(n // 256,), in_specs=[pl.BlockSpec((w,...]
    another operation x10 -> x0, other arithmetic: 24.1 us -> none  [the longest x6 13 us: damped_inverse(): lower = jnp.linalg.cholesky(damped)]
    unnamed x10 -> x20, local copies, waits for them, and re-layouts: 1.55 us -> 13.7 us
    ppermute x5, waiting for transfers between devices: 12.4 us -> 9.32 us  [the longest x3 6.09 us: dp_sum(): lax.ppermute(value, axis, [(i, i ^ 1) for i in range(last + 1)])]
    ppermute x5, starting transfers between devices: 11.3 us -> 9.24 us  [the longest x2 4.67 us: dp_sum(): lax.ppermute(value, axis, [(i, last - i) for i in range(last + 1)])]
    dot_general x9 -> x6, matrix products: 15.9 us -> 15.3 us  [the longest x1 12.2 us: on_device(): jnp.dot(block, weighed, preferred_element_type=jnp.float32)]
  transfers between devices with their start and end apart: 7 -> 7, of which waited for: 7 -> 6; matrix products, arithmetic and copies ran while one was open for 1% -> 3% of each run, Pallas kernels for 0% -> 18%
where the time goes in v2:
time: 154 us
  waiting for transfers between devices  53.5 us (35%)
  Pallas kernels  27.4 us (18%)
  local copies, waits for them, and re-layouts  20.5 us (13%)
  starting transfers between devices  17 us (11%)
  matrix products  15.3 us (10%)
  between operations  14.1 us (9%)
  other arithmetic  6.03 us (4%)
    all_gather x1, waiting for transfers between devices, on_device(): block = lax.all_gather(queries[0], DP, axis=0, tiled=True)  23.6 us
    all_to_all x1, waiting for transfers between devices, on_device(): lax.all_to_all(ordered, SECTION, split_axis=0, concat_axis=0, tiled=True)  19.9 us
    unnamed x20, local copies, waits for them, and re-layouts  13.7 us
    dot_general x1, matrix products, on_device(): jnp.dot(block, weighed, preferred_element_type=jnp.float32)  12.2 us
    pallas_call x1, Pallas kernels, weigh(): pl.pallas_call(weigh_kernel, grid=(n // 256,), in_specs=[pl.BlockSpec((w,...  10.6 us
    pallas_call x1, Pallas kernels, shuffle(): pl.pallas_call(shuffle_kernel, grid=(n // 128,), in_specs=[pl.BlockSpec((...  9.45 us
    all_to_all x1, starting transfers between devices, on_device(): lax.all_to_all(ordered, SECTION, split_axis=0, concat_axis=0, tiled=True)  7.69 us
    pallas_call x1, Pallas kernels, inverses(): pl.pallas_call(functools.partial(inverse_kernel, tokens), out_shape=[jax....  7.43 us
  transfers between devices with their start and end apart: 7, of which 6 were waited for; matrix products, arithmetic and copies ran while one was open for 3% of the time, Pallas kernels for 18%

profile of v2, /device:TPU:1, one launch (start us, length us, event | category | flops | bytes accessed | tf_op | source)
XLA Modules:
  0.0 153.8 jit_solution(2918516853692424893)
XLA Ops:
  8.8 1.9 %fusion.12 = bf16[256,64]{0,1:T(8,128)(2,1)S(1)} fusion(bf16[1,256,4096]{2,1,0:T(8,128)(2,1)S(1)} %copy-done, bf16[1,4096,64]{1,2,0:T(8,128)(2,1)} %param.10), kind=kOutput, calls=%fused_computation.11 | convolution fusion | flops 134234112 | bytes 2654208 | tf_op jit(solution)/shard_map/dot_general | solution.py:105
  11.8 3.3 %collective-permute-start = (f32[64,128]{1,0:T(8,128)S(1)}, f32[64,128]{1,0:T(8,128)S(1)}, u32[]{:S(2)}, u32[]{:S(2)}) collective-permute-start(f32[64,128]{1,0:T(8,128)S(1)} %pad_maximum_fusion), channel_id=1, source_target_pairs={{0,8},{8,0},{1,9},{9,1},{2,10},{10,2},{3,11},{11,3},{4,12},{12,4},... | collective-permute-start | bytes 98312 | tf_op jit(solution)/shard_map/ppermute | solution.py:92
  16.1 2.7 %collective-permute-done.1 = f32[64,128]{1,0:T(8,128)S(1)} collective-permute-done((f32[64,128]{1,0:T(8,128)S(1)}, f32[64,128]{1,0:T(8,128)S(1)}, u32[]{:S(2)}, u32[]{:S(2)}) %collective-permute-start.1) | collective-permute-done | bytes 32800 | tf_op jit(solution)/shard_map/ppermute | solution.py:92
  19.6 3.2 %collective-permute-done.2 = f32[64,128]{1,0:T(8,128)S(1)} collective-permute-done((f32[64,128]{1,0:T(8,128)S(1)}, f32[64,128]{1,0:T(8,128)S(1)}, u32[]{:S(2)}, u32[]{:S(2)}) %collective-permute-start.2) | collective-permute-done | bytes 32800 | tf_op jit(solution)/shard_map/ppermute | solution.py:94
  22.8 1.3 collective-permute-start.3
  24.4 2.5 %collective-permute-done.3 = f32[64,128]{1,0:T(8,128)S(1)} collective-permute-done((f32[64,128]{1,0:T(8,128)S(1)}, f32[64,128]{1,0:T(8,128)S(1)}, u32[]{:S(2)}, u32[]{:S(2)}) %collective-permute-start.3) | collective-permute-done | bytes 32800 | tf_op jit(solution)/shard_map/ppermute | solution.py:92
  26.9 3.9 %collective-permute-start.4 = (f32[64,128]{1,0:T(8,128)S(1)}, f32[64,128]{1,0:T(8,128)S(1)}, u32[]{:S(2)}, u32[]{:S(2)}) collective-permute-start(f32[64,128]{1,0:T(8,128)S(1)} %add.28), channel_id=1, source_target_pairs={{0,192},{64,128},{128,64},{192,0},{1,193},{65,129},{129,65},{193,1... | collective-permute-start | bytes 98312 | tf_op jit(solution)/shard_map/ppermute | solution.py:94
  30.8 2.8 %copy-done.3 = bf16[1,768,4096]{2,1,0:T(8,128)(2,1)S(1)} copy-done((bf16[1,768,4096]{2,1,0:T(8,128)(2,1)S(1)}, bf16[1,768,4096]{2,1,0:T(8,128)(2,1)}, u32[]{:S(2)}) %copy-start.3) | copy-done | bytes 6291480
  33.6 9.4 %shard_map.86.x_ref = bf16[4096,768]{1,0:T(8,128)(2,1)S(1)} custom-call(bf16[768,4096]{1,0:T(8,128)(2,1)S(1)} %bitcast.37), custom_call_target="tpu_custom_call" | custom-call | flops 402653184 | bytes 12582912 | tf_op jit(solution)/shard_map/pallas_call | solution.py:24
  43.1 2.7 %copy-done.1 = bf16[4096,768]{1,0:T(8,128)(2,1)} copy-done((bf16[4096,768]{1,0:T(8,128)(2,1)}, bf16[4096,768]{1,0:T(8,128)(2,1)S(1)}, u32[]{:S(2)}) %copy-start.1) | copy-done | bytes 6291480
  46.4 7.4 %shard_map.87 = (bf16[256,256]{1,0:T(8,128)(2,1)}, bf16[256,256]{1,0:T(8,128)(2,1)}) custom-call(f32[64,128]{1,0:T(8,128)} %add.29.s_ref), custom_call_target="tpu_custom_call" | custom-call | flops 1048576 | bytes 300000 | tf_op jit(solution)/shard_map/pallas_call | solution.py:83
  53.8 2.8 %copy-done.2 = bf16[4096,768]{1,0:T(8,128)(2,1)S(1)} copy-done((bf16[4096,768]{1,0:T(8,128)(2,1)S(1)}, bf16[4096,768]{1,0:T(8,128)(2,1)}, u32[]{:S(2)}) %copy-start.2) | copy-done | bytes 6291480
  56.6 0.9 copy-done.5
  57.5 1.0 copy-done.6
  58.5 10.6 %shard_map.88 = bf16[4096,768]{1,0:T(8,128)(2,1)S(1)} custom-call(bf16[4096,768]{1,0:T(8,128)(2,1)S(1)} %copy-done.2, bf16[256,256]{1,0:T(8,128)(2,1)S(1)} %copy-done.5, bf16[256,256]{1,0:T(8,128)(2,1)S(1)} %copy-done.6), custom_call_target="tpu_custom_call" | custom-call | flops 3221225472 | bytes 12582912 | tf_op jit(solution)/shard_map/pallas_call | solution.py:48
  69.1 2.7 %copy-done.4 = bf16[4096,768]{1,0:T(8,128)(2,1)} copy-done((bf16[4096,768]{1,0:T(8,128)(2,1)}, bf16[4096,768]{1,0:T(8,128)(2,1)S(1)}, u32[]{:S(2)}) %copy-start.4) | copy-done | bytes 6291480
  71.8 23.6 %all-gather.3.cloned.1.call-done = bf16[1,1024,4096]{2,1,0:T(8,128)(2,1)} async-done(((bf16[1,32,4096]{2,1,0:T(8,128)(2,1)}), bf16[1,1024,4096]{2,1,0:T(8,128)(2,1)}) %all-gather.3.cloned.1.call-update) | async-done | bytes 8388624 | tf_op jit(solution)/shard_map/all_gather | solution.py:101
  95.4 12.2 %fusion.9 = bf16[1024,768]{0,1:T(8,128)(2,1)} fusion(bf16[4096,768]{1,0:T(8,128)(2,1)} %copy-done.4, bf16[1,1024,4096]{2,1,0:T(8,128)(2,1)} %all-gather.3.cloned.1.call-done), kind=kOutput, calls=%fused_computation.10 | convolution fusion | flops 6443237376 | bytes 16252928 | tf_op jit(solution)/shard_map/dot_general | solution.py:123
  107.6 2.6 %copy.9 = bf16[1024,768]{1,0:T(8,128)(2,1)} copy(bf16[1024,768]{0,1:T(8,128)(2,1)} %fusion.9) | data formatting | bytes 3145728 | tf_op jit(solution)/shard_map/convert_element_type | solution.py:123
  110.2 3.2 %gather_fusion = bf16[32,32,768]{2,1,0:T(8,128)(2,1)} fusion(bf16[32,32,768]{2,1,0:T(8,128)(2,1)} %bitcast.39, s32[1024]{0:T(1024)S(1)} %pad_clamp_fusion), kind=kCustom, calls=%fused_computation | custom fusion | bytes 3145856 | tf_op jit(solution)/shard_map/jit(_take)/gather | solution.py:125
  113.4 2.8 %bitcast_select_fusion = bf16[8,128,768]{2,1,0:T(8,128)(2,1)} fusion(pred[8,128]{1,0:T(8,128)(4,1)S(1)} %broadcast_in_dim.20, bf16[8,128,768]{2,1,0:T(8,128)(2,1)} %bitcast.38), kind=kLoop, calls=%fused_computation.9 | loop fusion | flops 786432 | bytes 3146752 | tf_op jit(solution)/shard_map/jit(_take)/select_n | solution.py:125
  116.2 7.7 %all-to-all-start = ((bf16[8,128,768]{2,1,0:T(8,128)(2,1)}), bf16[8,128,768]{2,1,0:T(8,128)(2,1)}, u32[]{:S(2)}, u32[]{:S(2)}) async-start(bf16[8,128,768]{2,1,0:T(8,128)(2,1)} %bitcast_select_fusion), calls=%async_computation | async-start | bytes 3145728 | tf_op jit(solution)/shard_map/all_to_all | solution.py:130
  124.7 19.9 %all-to-all-done = bf16[8,128,768]{2,1,0:T(8,128)(2,1)} async-done(((bf16[8,128,768]{2,1,0:T(8,128)(2,1)}), bf16[8,128,768]{2,1,0:T(8,128)(2,1)}, u32[]{:S(2)}, u32[]{:S(2)}) %all-to-all-start) | async-done | bytes 1572896 | tf_op jit(solution)/shard_map/all_to_all | solution.py:130
  144.6 2.4 %convert_reduce_fusion = f32[128,768]{1,0:T(8,128)} fusion(bf16[8,128,768]{2,1,0:T(8,128)(2,1)} %all-to-all-done), kind=kLoop, calls=%fused_computation.3 | loop fusion | flops 1474560 | bytes 1966080 | tf_op jit(solution)/shard_map/reduce_sum | solution.py:131
  (37 shorter events, 6.2 us)
Async XLA Ops:
  7.2 1.6 %copy-start = (bf16[1,256,4096]{2,1,0:T(8,128)(2,1)S(1)}, bf16[1,256,4096]{2,1,0:T(8,128)(2,1)}, u32[]{:S(2)}) copy-start(bf16[1,256,4096]{2,1,0:T(8,128)(2,1)} %param.8) | copy-start | bytes 6291460
  7.2 3.7 %copy-start.8 = (bf16[1,4096,64]{1,2,0:T(8,128)(2,1)S(1)}, bf16[1,4096,64]{1,2,0:T(8,128)(2,1)}, u32[]{:S(2)}) copy-start(bf16[1,4096,64]{1,2,0:T(8,128)(2,1)} %param.9) | copy-start | bytes 1572868
  7.2 88.2 %all-gather.3.cloned.1.call-start = ((), (), s32[]{:S(2)}) async-start(), calls=%async_computation.1 | async-start | bytes 8650752 | tf_op jit(solution)/shard_map/all_gather | solution.py:101
  8.8 2.1 %copy-start.7 = (bf16[1,256,4096]{2,1,0:T(8,128)(2,1)S(1)}, bf16[1,256,4096]{2,1,0:T(8,128)(2,1)}, u32[]{:S(2)}) copy-start(bf16[1,256,4096]{2,1,0:T(8,128)(2,1)} %param.7) | copy-start | bytes 6291460
  10.7 5.4 %copy-start.9 = (s32[32]{0:T(128)S(1)}, s32[32]{0:T(128)}, u32[]{:S(2)}) copy-start(s32[32]{0:T(128)} %param.13) | copy-start | bytes 388
  11.8 4.1 %collective-permute-start = (f32[64,128]{1,0:T(8,128)S(1)}, f32[64,128]{1,0:T(8,128)S(1)}, u32[]{:S(2)}, u32[]{:S(2)}) collective-permute-start(f32[64,128]{1,0:T(8,128)S(1)} %pad_maximum_fusion), channel_id=1, source_target_pairs={{0,8},{8,0},{1,9},{9,1},{2,10},{10,2},{3,11},{11,3},{4,12},{12,4},... | collective-permute-start | bytes 98312 | tf_op jit(solution)/shard_map/ppermute | solution.py:92
  16.1 2.8 %collective-permute-start.1 = (f32[64,128]{1,0:T(8,128)S(1)}, f32[64,128]{1,0:T(8,128)S(1)}, u32[]{:S(2)}, u32[]{:S(2)}) collective-permute-start(f32[64,128]{1,0:T(8,128)S(1)} %fusion.30), channel_id=1, source_target_pairs={{0,16},{16,0},{32,48},{48,32},{1,17},{17,1},{33,49},{49,33},{2,18}... | collective-permute-start | bytes 98312 | tf_op jit(solution)/shard_map/ppermute | solution.py:92
  18.9 4.0 %collective-permute-start.2 = (f32[64,128]{1,0:T(8,128)S(1)}, f32[64,128]{1,0:T(8,128)S(1)}, u32[]{:S(2)}, u32[]{:S(2)}) collective-permute-start(f32[64,128]{1,0:T(8,128)S(1)} %add.26), channel_id=1, source_target_pairs={{0,48},{16,32},{32,16},{48,0},{1,49},{17,33},{33,17},{49,1},{2,50}... | collective-permute-start | bytes 98312 | tf_op jit(solution)/shard_map/ppermute | solution.py:94
  22.8 4.0 %collective-permute-start.3 = (f32[64,128]{1,0:T(8,128)S(1)}, f32[64,128]{1,0:T(8,128)S(1)}, u32[]{:S(2)}, u32[]{:S(2)}) collective-permute-start(f32[64,128]{1,0:T(8,128)S(1)} %add.27), channel_id=1, source_target_pairs={{0,64},{64,0},{128,192},{192,128},{1,65},{65,1},{129,193},{193,129... | collective-permute-start | bytes 98312 | tf_op jit(solution)/shard_map/ppermute | solution.py:92
  26.9 18.9 %collective-permute-start.4 = (f32[64,128]{1,0:T(8,128)S(1)}, f32[64,128]{1,0:T(8,128)S(1)}, u32[]{:S(2)}, u32[]{:S(2)}) collective-permute-start(f32[64,128]{1,0:T(8,128)S(1)} %add.28), channel_id=1, source_target_pairs={{0,192},{64,128},{128,64},{192,0},{1,193},{65,129},{129,65},{193,1... | collective-permute-start | bytes 98312 | tf_op jit(solution)/shard_map/ppermute | solution.py:94
  30.8 2.8 %copy-start.3 = (bf16[1,768,4096]{2,1,0:T(8,128)(2,1)S(1)}, bf16[1,768,4096]{2,1,0:T(8,128)(2,1)}, u32[]{:S(2)}) copy-start(bf16[1,768,4096]{2,1,0:T(8,128)(2,1)} %param.11) | copy-start | bytes 18874372
  43.1 2.7 %copy-start.1 = (bf16[4096,768]{1,0:T(8,128)(2,1)}, bf16[4096,768]{1,0:T(8,128)(2,1)S(1)}, u32[]{:S(2)}) copy-start(bf16[4096,768]{1,0:T(8,128)(2,1)S(1)} %shard_map.86.x_ref) | copy-start | bytes 18874372
  53.8 2.8 %copy-start.2 = (bf16[4096,768]{1,0:T(8,128)(2,1)S(1)}, bf16[4096,768]{1,0:T(8,128)(2,1)}, u32[]{:S(2)}) copy-start(bf16[4096,768]{1,0:T(8,128)(2,1)} %copy-done.1) | copy-start | bytes 18874372
  56.6 0.9 copy-start.5
  57.5 1.0 copy-start.6
  69.0 2.7 %copy-start.4 = (bf16[4096,768]{1,0:T(8,128)(2,1)}, bf16[4096,768]{1,0:T(8,128)(2,1)S(1)}, u32[]{:S(2)}) copy-start(bf16[4096,768]{1,0:T(8,128)(2,1)S(1)} %shard_map.88) | copy-start | bytes 18874372
  116.2 28.4 %all-to-all-start = ((bf16[8,128,768]{2,1,0:T(8,128)(2,1)}), bf16[8,128,768]{2,1,0:T(8,128)(2,1)}, u32[]{:S(2)}, u32[]{:S(2)}) async-start(bf16[8,128,768]{2,1,0:T(8,128)(2,1)} %bitcast_select_fusion), calls=%async_computation | async-start | bytes 3145728 | tf_op jit(solution)/shard_map/all_to_all | solution.py:130
Sparse Core Ops, SparseCore 0:
  10.6 84.7 all-gather.2

commit v3 on v2

v3 whole, which is shorter than its diff:
```python
import functools

import jax
import jax.numpy as jnp
from jax import lax
from jax.experimental import pallas as pl
from jax.experimental.pallas import tpu as pltpu
from jax.sharding import PartitionSpec as P

SEQ = 256
RANK = 64
DP = ("zh", "x", "core")
SECTION = ("zl", "y")

VMEM_BYTES = 60 * 2**20
LIGHT = pl.CostEstimate(flops=0, bytes_accessed=1024, transcendentals=0)


def params():
    return pltpu.CompilerParams(vmem_limit_bytes=VMEM_BYTES)


def shuffle_kernel(t_ref, *refs):
    x_ref, wide = refs[-2:]
    for j in range(t_ref.shape[1] // 128):
        lanes = slice(128 * j, 128 * j + 128)
        wide[lanes, :] = t_ref[:, lanes].astype(jnp.float32).T
    for i in range(RANK):
        x_ref[RANK * i : RANK * i + RANK, :] = wide[pl.ds(i, RANK, stride=RANK), :].astype(
            jnp.bfloat16
        )


def shuffle(t, first, count, held=None):
    n, width = t.shape
    specs = [pl.BlockSpec((128, width), lambda j: (j + first, 0))]
    return pl.pallas_call(
        shuffle_kernel,
        grid=(count,),
        in_specs=specs + ([] if held is None else [pl.BlockSpec(memory_space=pl.ANY)]),
        out_specs=pl.BlockSpec((width, 128), lambda j: (0, j + first)),
        out_shape=jax.ShapeDtypeStruct((width, n), jnp.bfloat16),
        input_output_aliases={} if held is None else {1: 0},
        scratch_shapes=[pltpu.VMEM((width, 128), jnp.float32)],
        compiler_params=params(),
        cost_estimate=LIGHT,
    )(*((t,) if held is None else (t, held)))


def score_kernel(moves, count, pos_ref, x_ref, a_ref, b_ref, *refs):
    pieces, y_ref = refs[:count], refs[count]
    rows, low, high, weighed, sems = refs[count + 1 :]
    copies = []
    for n, (piece, start, size, slot, half) in enumerate(moves):
        place = pl.multiple_of(pos_ref[slot] * 32 + half * 16, 16)
        copies.append(
            pltpu.make_async_copy(
                pieces[piece].at[pl.ds(start, size)], rows.at[pl.ds(place, size)], sems.at[n]
            )
        )
    first = pl.program_id(0) == 0

    @pl.when(first)
    def _():
        for copy in copies:
            copy.start()

    a, b = a_ref[...], b_ref[...]
    width = x_ref.shape[0]
    for g in range(width // 256):
        band = slice(256 * g, 256 * g + 256)
        y = jnp.dot(a, x_ref[band, :], preferred_element_type=jnp.float32)
        low[band, :] = y[:, :128]
        high[band, :] = y[:, 128:]
    for g in range(width // 256):
        parts = []
        for k in range(4 * g, 4 * g + 4):
            pair = [half[pl.ds(k, RANK, stride=RANK), :] for half in (low, high)]
            parts.append(jnp.concatenate(pair, axis=1).astype(jnp.bfloat16))
        z = jnp.concatenate(parts, axis=0)
        weighed[256 * g : 256 * g + 256, :] = jnp.dot(
            b, z, preferred_element_type=jnp.float32
        ).astype(jnp.bfloat16)

    @pl.when(first)
    def _():
        for copy in copies:
            copy.wait()

    tall = 256
    for g in range(rows.shape[0] // tall):
        band = slice(tall * g, tall * g + tall)
        y_ref[band, :] = jnp.dot(
            rows[band, :], weighed[...], preferred_element_type=jnp.float32
        ).astype(jnp.bfloat16)


def score(pieces, moves, pos, x, a, b):
    width, n = x.shape
    total = sum(piece.shape[0] for piece in pieces)
    small = pl.BlockSpec((256, 256), lambda j: (0, 0))
    return pl.pallas_call(
        functools.partial(score_kernel, moves, len(pieces)),
        grid=(n // 256,),
        in_specs=[
            pl.BlockSpec(memory_space=pltpu.SMEM),
            pl.BlockSpec((width, 256), lambda j: (0, j)),
            small,
            small,
        ]
        + [pl.BlockSpec(memory_space=pl.ANY)] * len(pieces),
        out_specs=pl.BlockSpec((total, 256), lambda j: (0, j)),
        out_shape=jax.ShapeDtypeStruct((total, n), jnp.bfloat16),
        scratch_shapes=[
            pltpu.VMEM((total, width), jnp.bfloat16),
            pltpu.VMEM((width, 128), jnp.float32),
            pltpu.VMEM((width, 128), jnp.float32),
            pltpu.VMEM((width, 256), jnp.bfloat16),
            pltpu.SemaphoreType.DMA((len(moves),)),
        ],
        compiler_params=params(),
        cost_estimate=LIGHT,
    )(pos, x, a, b, *pieces)


def blocks(m):
    four=jnp.concatenate([m]*4,axis=1)
    four=jnp.concatenate([four]*4,axis=0)
    r=lax.broadcasted_iota(jnp.int32,four.shape,0)//RANK
    c=lax.broadcasted_iota(jnp.int32,four.shape,1)//RANK
    return jnp.where(r==c,four,0.0).astype(jnp.bfloat16)
def inverse_kernel(tokens, s_ref, a_ref, b_ref):
    m=s_ref[...]/tokens
    row=lax.broadcasted_iota(jnp.int32,m.shape,0)
    lane=lax.broadcasted_iota(jnp.int32,m.shape,1)
    left=lane<RANK
    lcol=jnp.where(left,lane,lane-RANK)
    diag=jnp.where(row==lcol,m,0.0)
    tl=jnp.sum(jnp.where(left,diag,0.0)); tr=jnp.sum(jnp.where(left,0.0,diag))
    m=m+jnp.where(row==lcol,jnp.where(left,tl,tr)*(0.1/RANK),0.0)
    for k in range(RANK):
        pr=m[k:k+1,:]
        l1=left[:1]
        piv=jnp.where(l1,pr[:,k:k+1],pr[:,RANK+k:RANK+k+1])
        at=lcol==k
        scaled=jnp.where(at[:1],1.0,pr)/piv
        col=jnp.where(left,m[:,k:k+1],m[:,RANK+k:RANK+k+1])
        m=jnp.where(row==k,scaled,jnp.where(at,0.0,m)-col*scaled)
    inb=m[:,:RANK]; outb=m[:,RANK:]
    a_ref[...]=blocks(outb.T)
    b_ref[...]=blocks(inb)
def inverses(s,tokens):
    return pl.pallas_call(functools.partial(inverse_kernel,tokens),
        out_shape=[jax.ShapeDtypeStruct((256,256),jnp.bfloat16)]*2,
        cost_estimate=LIGHT,
    )(s)


def shift(value, axis, step):
    size = lax.axis_size(axis)
    return lax.ppermute(value, axis, [(i, (i + step) % size) for i in range(size)])


def swap(value, axis, way):
    last = lax.axis_size(axis) - 1
    pairs = [(i, i ^ 1 if way == 0 else last - i) for i in range(last + 1)]
    return value + lax.ppermute(value, axis, pairs)


def forward(behind, ahead, axis):
    half = behind.shape[0] // 2
    return [shift(behind[:half], axis, 1), shift(ahead[half:], axis, -1)]


def layout():
    pair = [(0, 32, 3, 0), (32, 32, 1, 0)]
    far = [(0, 32, 2, 0)]
    groups = [(turn, [(0, 32, 0, 0)]) for turn in (0, 3, 1, 2)]
    groups += [(turn, pair) for turn in (0, 3, 1)] + [(2, [(0, 32, 3, 0)]), (2, [(0, 32, 1, 0)])]
    groups += [(turn, far) for turn in (0, 3, 1)] + [(2, [(0, 16, 2, 0)]), (2, [(0, 16, 2, 1)])]
    moves = []
    for other in range(2):
        for n, (turn, runs) in enumerate(groups):
            for start, size, climb, half in runs:
                slot = (climb * 4 + turn) * 2 + other
                moves.append((other * len(groups) + n, start, size, slot, half))
    return moves


def block_ids():
    zh, x, core = (lax.axis_index(axis) for axis in DP)
    ids = []
    for climb in range(4):
        for turn in range(4):
            for other in range(2):
                ids.append((((zh + climb) % 4) * 4 + (x + turn) % 4) * 2 + (core + other) % 2)
    return jnp.stack(ids)


def on_device(layer_inputs, output_grads, proj_in, proj_out, train_log, queries, query_owner):
    local_tokens = layer_inputs.shape[1]
    total_tokens = local_tokens * lax.axis_size(DP)
    hold = lax.optimization_barrier
    own, train = queries[0], train_log[0]
    behind, ahead = shift(own, "zh", 1), shift(own, "zh", -1)
    near = [own] + [shift(own, "x", step) for step in (1, -1, 2)]

    acts = jnp.dot(layer_inputs[0], proj_in[0], preferred_element_type=jnp.float32).astype(
        jnp.bfloat16
    )
    grads = jnp.dot(output_grads[0], proj_out[0], preferred_element_type=jnp.float32).astype(
        jnp.bfloat16
    )
    down = (((0,), (0,)), ((), ()))
    in_sum = lax.dot_general(acts, acts, down, preferred_element_type=jnp.float32)
    out_sum = lax.dot_general(grads, grads, down, preferred_element_type=jnp.float32)
    sums = swap(jnp.concatenate([in_sum, out_sum], axis=1), "core", 0)
    sums, train = hold((swap(sums, "x", 0), train))
    turned = shuffle(train, 0, 2)
    sums, turned, behind, ahead = hold((swap(sums, "x", 1), turned, behind, ahead))
    far = forward(behind, ahead, "zh")
    pair = jnp.concatenate([behind, ahead], axis=0)
    pairs = [pair, shift(pair, "x", 1), shift(pair, "x", -1)]
    turned = shuffle(train, 2, 2, turned)
    sums, turned, far, near = hold((swap(sums, "zh", 0), turned, far, near))
    far = jnp.concatenate(far, axis=0)
    fars = [far, shift(far, "x", 1), shift(far, "x", -1)]
    turned = shuffle(train, 4, 2, turned)
    near_twins = [shift(piece, "core", 1) for piece in near]
    sums, turned, pairs, near, near_twins = hold(
        (swap(sums, "zh", 1), turned, pairs, near, near_twins)
    )
    pairs += forward(pairs[1], pairs[2], "x")
    out_blocks, in_blocks = inverses(sums, total_tokens)
    fars, out_blocks, pairs = hold((fars, out_blocks, pairs))
    fars += forward(fars[1], fars[2], "x")
    rest = pairs + fars
    pieces = near + rest + near_twins + [shift(piece, "core", 1) for piece in rest]

    count = query_owner.shape[0]
    here = block_ids()[:, None] == query_owner[None, :]
    pos = jnp.sum(jnp.where(here, jnp.arange(count, dtype=jnp.int32)[None, :], 0), axis=1)
    ordered = score(pieces, layout(), pos, turned, out_blocks, in_blocks)
    parts = lax.axis_size(SECTION)
    ordered = ordered.reshape(parts, ordered.shape[0] // parts, ordered.shape[1])
    arrived = lax.all_to_all(ordered, SECTION, split_axis=0, concat_axis=0, tiled=True)
    scores = jnp.sum(arrived.astype(jnp.float32), axis=0)

    examples = local_tokens // SEQ
    per_example = lax.dot_general(
        grads.reshape(examples, SEQ, RANK),
        acts.reshape(examples, SEQ, RANK),
        (((1,), (1,)), ((0,), (0,))),
        preferred_element_type=jnp.float32,
    )
    fresh_grads = (per_example / SEQ).reshape(1, examples, RANK * RANK).astype(jnp.bfloat16)
    return (fresh_grads, scores)


def solution(mesh):
    fine = jax.sharding.Mesh(
        mesh.devices.reshape(4, 4, 2, 2, 4), ("zh", "x", "core", "zl", "y")
    )
    placed = (
        P(SECTION, DP, None),
        P(SECTION, DP, None),
        P(SECTION, None, None),
        P(SECTION, None, None),
        P(SECTION, DP, None),
        P(SECTION, DP, None),
        P(),
    )
    return jax.shard_map(
        on_device,
        mesh=fine,
        in_specs=placed,
        out_specs=(P(SECTION, DP, None), P(SECTION, DP)),
        check_vma=False,
    )
```

time: 154 us -> 135 us (0.88)
  starting transfers between devices: 17 us -> 48.8 us
  waiting for transfers between devices: 53.5 us -> 26 us
  Pallas kernels: 27.4 us -> 42.8 us
  between operations: 14.1 us -> 0.96 us
  matrix products: 15.3 us -> 2.94 us
  local copies, waits for them, and re-layouts: 20.5 us -> 9.07 us
  other arithmetic: 6.03 us -> 3.94 us
    ppermute x5 -> x34, starting transfers between devices: 9.24 us -> 44 us  [the longest x29 32.4 us: shift(): lax.ppermute(value, axis, [(i, (i + step) % size) for i in range(size)])]
    all_gather x1 -> x0, waiting for transfers between devices: 23.6 us -> none  [on_device(): block = lax.all_gather(queries[0], DP, axis=0, tiled=True)]
    pallas_call x2 -> x4, Pallas kernels: 20 us -> 35.4 us  [the longest x1 20 us: score(): pl.pallas_call(functools.partial(score_kernel, moves, len(pieces)), grid=...]
    dot_general x1 -> x0, matrix products: 12.2 us -> none  [on_device(): jnp.dot(block, weighed, preferred_element_type=jnp.float32)]
    unnamed x20 -> x44, local copies, waits for them, and re-layouts: 13.7 us -> 3.48 us
    slice x0 -> x6, local copies, waits for them, and re-layouts: none -> 3.84 us  [forward(): return [shift(behind[:half], axis, 1), shift(ahead[half:], axis, -1)]]
    gather x1 -> x0, local copies, waits for them, and re-layouts: 3.19 us -> none  [on_device(): jnp.take(total.reshape(count, total.shape[0] // count, total.shape[1]), q...]
    ppermute x5 -> x34, waiting for transfers between devices: 9.32 us -> 6.16 us  [the longest x29 4.3 us: shift(): lax.ppermute(value, axis, [(i, (i + step) % size) for i in range(size)])]
  transfers between devices with their start and end apart: 7 -> 35, of which waited for: 6 -> 7; matrix products, arithmetic and copies ran while one was open for 3% -> 6% of each run, Pallas kernels for 18% -> 17%
where the time goes in v3:
time: 135 us; the launch traced here: 134 us
  starting transfers between devices  48.8 us (36%)
  Pallas kernels  42.8 us (32%)
  waiting for transfers between devices  26 us (19%)
  local copies, waits for them, and re-layouts  9.07 us (7%)
  other arithmetic  3.94 us (3%)
  matrix products  2.94 us (2%)
    ppermute x29, starting transfers between devices, shift(): lax.ppermute(value, axis, [(i, (i + step) % size) for i in range(size)])  32.4 us
    pallas_call x1, Pallas kernels, score(): pl.pallas_call(functools.partial(score_kernel, moves, len(pieces)), grid=...  20 us
    all_to_all x1, waiting for transfers between devices, on_device(): lax.all_to_all(ordered, SECTION, split_axis=0, concat_axis=0, tiled=True)  19.9 us
    pallas_call x3, Pallas kernels, shuffle(): pl.pallas_call(shuffle_kernel, grid=(count,), in_specs=specs + ([] if hel...  15.4 us
    ppermute x5, starting transfers between devices, swap(): return value + lax.ppermute(value, axis, pairs)  11.6 us
    pallas_call x1, Pallas kernels, inverses(): pl.pallas_call(functools.partial(inverse_kernel, tokens), out_shape=[jax....  7.42 us
    all_to_all x1, starting transfers between devices, on_device(): lax.all_to_all(ordered, SECTION, split_axis=0, concat_axis=0, tiled=True)  4.77 us
    ppermute x29, waiting for transfers between devices, shift(): lax.ppermute(value, axis, [(i, (i + step) % size) for i in range(size)])  4.3 us
  transfers between devices with their start and end apart: 35, of which 7 were waited for; matrix products, arithmetic and copies ran while one was open for 6% of the time, Pallas kernels for 17%

profile of v3, /device:TPU:1, one launch (start us, length us, event | category | flops | bytes accessed | tf_op | source)
XLA Modules:
  0.0 134.5 jit_solution(282156684583458823)
XLA Ops:
  2.2 1.8 %fusion.7 = bf16[256,64]{0,1:T(8,128)(2,1)S(1)} fusion(bf16[1,256,4096]{2,1,0:T(8,128)(2,1)S(1)} %copy-done, bf16[1,4096,64]{1,2,0:T(8,128)(2,1)} %param.9), kind=kOutput, calls=%fused_computation.6 | convolution fusion | flops 134234112 | bytes 2654208 | tf_op jit(solution)/shard_map/dot_general | solution.py:208
  5.2 3.3 %collective-permute-start = (f32[64,128]{1,0:T(8,128)S(1)}, f32[64,128]{1,0:T(8,128)S(1)}, u32[]{:S(2)}, u32[]{:S(2)}) collective-permute-start(f32[64,128]{1,0:T(8,128)S(1)} %pad_maximum_fusion), channel_id=1, source_target_pairs={{0,8},{8,0},{1,9},{9,1},{2,10},{10,2},{3,11},{11,3},{4,12},{12,4},... | collective-permute-start | bytes 98312 | tf_op jit(solution)/shard_map/ppermute | solution.py:167
  8.4 4.3 %collective-permute-start.4 = (bf16[32,4096]{1,0:T(8,128)(2,1)}, bf16[32,4096]{1,0:T(8,128)(2,1)S(1)}, u32[]{:S(2)}, u32[]{:S(2)}) collective-permute-start(bf16[32,4096]{1,0:T(8,128)(2,1)} %bitcast.37.refs_0_), channel_id=1, source_target_pairs={{0,192},{64,0},{128,64},{192,128},{1,193},{65,1},{129,65},{193,129... | collective-permute-start | bytes 786440 | tf_op jit(solution)/shard_map/ppermute | solution.py:161
  14.1 1.9 %collective-permute-done.1 = f32[64,128]{1,0:T(8,128)S(1)} collective-permute-done((f32[64,128]{1,0:T(8,128)S(1)}, f32[64,128]{1,0:T(8,128)S(1)}, u32[]{:S(2)}, u32[]{:S(2)}) %collective-permute-start.1) | collective-permute-done | bytes 32800 | tf_op jit(solution)/shard_map/ppermute | solution.py:167
  15.9 2.5 %collective-permute-start.2 = (f32[64,128]{1,0:T(8,128)S(1)}, f32[64,128]{1,0:T(8,128)S(1)}, u32[]{:S(2)}, u32[]{:S(2)}) collective-permute-start(f32[64,128]{1,0:T(8,128)S(1)} %add.436), channel_id=1, source_target_pairs={{0,48},{16,32},{32,16},{48,0},{1,49},{17,33},{33,17},{49,1},{2,50}... | collective-permute-start | bytes 98312 | tf_op jit(solution)/shard_map/ppermute | solution.py:167
  18.9 1.8 %collective-permute-start.9 = (bf16[32,4096]{1,0:T(8,128)(2,1)}, bf16[32,4096]{1,0:T(8,128)(2,1)}, u32[]{:S(2)}, u32[]{:S(2)}) collective-permute-start(bf16[32,4096]{1,0:T(8,128)(2,1)} %bitcast.37.refs_0_), channel_id=1, source_target_pairs={{0,48},{16,0},{32,16},{48,32},{1,49},{17,1},{33,17},{49,33},{2,50}... | collective-permute-start | bytes 786440 | tf_op jit(solution)/shard_map/ppermute | solution.py:161
  20.7 5.1 %shard_map.86.refs_0_ = bf16[4096,768]{1,0:T(8,128)(2,1)} custom-call(bf16[768,4096]{1,0:T(8,128)(2,1)} %bitcast.57), custom_call_target="tpu_custom_call" | custom-call | bytes 1024 | tf_op jit(solution)/shard_map/pallas_call | solution.py:37
  28.4 2.4 %collective-permute-start.7 = (bf16[16,4096]{1,0:T(8,128)(2,1)}, bf16[16,4096]{1,0:T(8,128)(2,1)}, u32[]{:S(2)}, u32[]{:S(2)}) collective-permute-start(bf16[16,4096]{1,0:T(8,128)(2,1)} %slice.19), channel_id=1, source_target_pairs={{0,192},{64,0},{128,64},{192,128},{1,193},{65,1},{129,65},{193,129... | collective-permute-start | bytes 393224 | tf_op jit(solution)/shard_map/ppermute | solution.py:161
  30.9 5.3 %shard_map.87.refs_0_ = bf16[4096,768]{1,0:T(8,128)(2,1)} custom-call(bf16[768,4096]{1,0:T(8,128)(2,1)} %bitcast.58, bf16[4096,768]{1,0:T(8,128)(2,1)} %shard_map.86.refs_0_), custom_call_target="tpu_custom_call", output_to_operand_aliasing={{}: (1, {})} | custom-call | bytes 1024 | tf_op jit(solution)/shard_map/pallas_call | solution.py:37
  36.2 3.2 %collective-permute-start.13 = (bf16[64,4096]{1,0:T(8,128)(2,1)S(1)}, bf16[64,4096]{1,0:T(8,128)(2,1)S(1)}, u32[]{:S(2)}, u32[]{:S(2)}) collective-permute-start(bf16[64,4096]{1,0:T(8,128)(2,1)S(1)} %constant_dynamic-update-slice_fusion.refs_4_), channel_id=1, source_target_pairs={{0,48},{16,0},{32,16},{48,32},{1,49},{17,1},{33,17},{49,33},{2,50}... | collective-permute-start | bytes 1572872 | tf_op jit(solution)/shard_map/ppermute | solution.py:161
  39.5 3.4 %collective-permute-start.11 = (f32[64,128]{1,0:T(8,128)S(1)}, f32[64,128]{1,0:T(8,128)S(1)}, u32[]{:S(2)}, u32[]{:S(2)}) collective-permute-start(f32[64,128]{1,0:T(8,128)S(1)} %add.438), channel_id=1, source_target_pairs={{0,192},{64,128},{128,64},{192,0},{1,193},{65,129},{129,65},{193,1... | collective-permute-start | bytes 98312 | tf_op jit(solution)/shard_map/ppermute | solution.py:167
  42.9 4.0 %collective-permute-start.14 = (bf16[32,4096]{1,0:T(8,128)(2,1)}, bf16[32,4096]{1,0:T(8,128)(2,1)}, u32[]{:S(2)}, u32[]{:S(2)}) collective-permute-start(bf16[32,4096]{1,0:T(8,128)(2,1)} %bitcast.37.refs_0_), channel_id=1, source_target_pairs={{0,8},{8,0},{1,9},{9,1},{2,10},{10,2},{3,11},{11,3},{4,12},{12,4},... | collective-permute-start | bytes 786440 | tf_op jit(solution)/shard_map/ppermute | solution.py:161
  47.8 5.1 %shard_map.88.x_ref = bf16[4096,768]{1,0:T(8,128)(2,1)} custom-call(bf16[768,4096]{1,0:T(8,128)(2,1)} %bitcast.59, bf16[4096,768]{1,0:T(8,128)(2,1)} %shard_map.87.refs_0_), custom_call_target="tpu_custom_call", output_to_operand_aliasing={{}: (1, {})} | custom-call | bytes 1024 | tf_op jit(solution)/shard_map/pallas_call | solution.py:37
  55.1 2.9 %collective-permute-start.19 = (bf16[32,4096]{1,0:T(8,128)(2,1)}, bf16[32,4096]{1,0:T(8,128)(2,1)S(1)}, u32[]{:S(2)}, u32[]{:S(2)}) collective-permute-start(bf16[32,4096]{1,0:T(8,128)(2,1)} %copy-done.6), channel_id=1, source_target_pairs={{0,48},{16,0},{32,16},{48,32},{1,49},{17,1},{33,17},{49,33},{2,50}... | collective-permute-start | bytes 786440 | tf_op jit(solution)/shard_map/ppermute | solution.py:161
  59.7 2.6 %collective-permute-start.21 = (bf16[32,4096]{1,0:T(8,128)(2,1)}, bf16[32,4096]{1,0:T(8,128)(2,1)}, u32[]{:S(2)}, u32[]{:S(2)}) collective-permute-start(bf16[32,4096]{1,0:T(8,128)(2,1)} %slice.21), channel_id=1, source_target_pairs={{0,48},{16,0},{32,16},{48,32},{1,49},{17,1},{33,17},{49,33},{2,50}... | collective-permute-start | bytes 786440 | tf_op jit(solution)/shard_map/ppermute | solution.py:161
  62.4 7.4 %shard_map.89 = (bf16[256,256]{1,0:T(8,128)(2,1)}, bf16[256,256]{1,0:T(8,128)(2,1)}) custom-call(f32[64,128]{1,0:T(8,128)} %add.439.s_ref), custom_call_target="tpu_custom_call" | custom-call | bytes 1024 | tf_op jit(solution)/shard_map/pallas_call | solution.py:153
  69.8 2.6 %collective-permute-done.20.refs_7_ = bf16[32,4096]{1,0:T(8,128)(2,1)} collective-permute-done((bf16[32,4096]{1,0:T(8,128)(2,1)}, bf16[32,4096]{1,0:T(8,128)(2,1)}, u32[]{:S(2)}, u32[]{:S(2)}) %collective-permute-start.20) | collective-permute-done | bytes 262176 | tf_op jit(solution)/shard_map/ppermute | solution.py:161
  74.9 2.1 %collective-permute-start.27 = (bf16[32,4096]{1,0:T(8,128)(2,1)}, bf16[32,4096]{1,0:T(8,128)(2,1)S(1)}, u32[]{:S(2)}, u32[]{:S(2)}) collective-permute-start(bf16[32,4096]{1,0:T(8,128)(2,1)} %collective-permute-done.20.refs_7_), channel_id=1, source_target_pairs={{0,8},{8,0},{1,9},{9,1},{2,10},{10,2},{3,11},{11,3},{4,12},{12,4},... | collective-permute-start | bytes 786440 | tf_op jit(solution)/shard_map/ppermute | solution.py:161
  77.1 1.9 %collective-permute-start.33 = (bf16[16,4096]{1,0:T(8,128)(2,1)S(1)}, bf16[16,4096]{1,0:T(8,128)(2,1)S(1)}, u32[]{:S(2)}, u32[]{:S(2)}) collective-permute-start(bf16[16,4096]{1,0:T(8,128)(2,1)S(1)} %collective-permute-done.23.refs_13_), channel_id=1, source_target_pairs={{0,8},{8,0},{1,9},{9,1},{2,10},{10,2},{3,11},{11,3},{4,12},{12,4},... | collective-permute-start | bytes 393224 | tf_op jit(solution)/shard_map/ppermute | solution.py:161
  79.0 2.6 %collective-permute-start.32 = (bf16[16,4096]{1,0:T(8,128)(2,1)S(1)}, bf16[16,4096]{1,0:T(8,128)(2,1)S(1)}, u32[]{:S(2)}, u32[]{:S(2)}) collective-permute-start(bf16[16,4096]{1,0:T(8,128)(2,1)S(1)} %collective-permute-done.22.refs_12_), channel_id=1, source_target_pairs={{0,8},{8,0},{1,9},{9,1},{2,10},{10,2},{3,11},{11,3},{4,12},{12,4},... | collective-permute-start | bytes 393224 | tf_op jit(solution)/shard_map/ppermute | solution.py:161
  86.7 20.0 %shard_map.90 = bf16[1024,768]{1,0:T(8,128)(2,1)} custom-call(s32[32]{0:T(128)} %select_reduce_fusion.pos_ref, bf16[4096,768]{1,0:T(8,128)(2,1)} %shard_map.88.x_ref, bf16[256,256]{1,0:T(8,128)(2,1)} %get-tuple-element.60.a_ref, bf16[256,256]{1,0:T(8,128)(2,1)} %get-tuple-element.61.b_ref, bf16[32,4096]{1,0:T(8,128)(2,1)} %bitcast.37.refs_0_, ...), custom_call_target="tpu_custom_call" | custom-call | bytes 1024 | tf_op jit(solution)/shard_map/pallas_call | solution.py:102
  106.6 4.8 %all-to-all-start = ((bf16[8,128,768]{2,1,0:T(8,128)(2,1)}), bf16[8,128,768]{2,1,0:T(8,128)(2,1)}, u32[]{:S(2)}, u32[]{:S(2)}) async-start(bf16[8,128,768]{2,1,0:T(8,128)(2,1)} %bitcast.60), calls=%async_computation | async-start | bytes 3145728 | tf_op jit(solution)/shard_map/all_to_all | solution.py:246
  112.2 19.9 %all-to-all-done = bf16[8,128,768]{2,1,0:T(8,128)(2,1)} async-done(((bf16[8,128,768]{2,1,0:T(8,128)(2,1)}), bf16[8,128,768]{2,1,0:T(8,128)(2,1)}, u32[]{:S(2)}, u32[]{:S(2)}) %all-to-all-start) | async-done | bytes 1572896 | tf_op jit(solution)/shard_map/all_to_all | solution.py:246
  132.1 2.4 %convert_reduce_fusion = f32[128,768]{1,0:T(8,128)} fusion(bf16[8,128,768]{2,1,0:T(8,128)(2,1)} %all-to-all-done), kind=kLoop, calls=%fused_computation | loop fusion | flops 1474560 | bytes 1966080 | tf_op jit(solution)/shard_map/reduce_sum | solution.py:247
  (118 shorter events, 20.5 us)
Async XLA Ops:
  5.2 7.6 %collective-permute-start = (f32[64,128]{1,0:T(8,128)S(1)}, f32[64,128]{1,0:T(8,128)S(1)}, u32[]{:S(2)}, u32[]{:S(2)}) collective-permute-start(f32[64,128]{1,0:T(8,128)S(1)} %pad_maximum_fusion), channel_id=1, source_target_pairs={{0,8},{8,0},{1,9},{9,1},{2,10},{10,2},{3,11},{11,3},{4,12},{12,4},... | collective-permute-start | bytes 98312 | tf_op jit(solution)/shard_map/ppermute | solution.py:167
  8.4 17.4 %collective-permute-start.4 = (bf16[32,4096]{1,0:T(8,128)(2,1)}, bf16[32,4096]{1,0:T(8,128)(2,1)S(1)}, u32[]{:S(2)}, u32[]{:S(2)}) collective-permute-start(bf16[32,4096]{1,0:T(8,128)(2,1)} %bitcast.37.refs_0_), channel_id=1, source_target_pairs={{0,192},{64,0},{128,64},{192,128},{1,193},{65,1},{129,65},{193,129... | collective-permute-start | bytes 786440 | tf_op jit(solution)/shard_map/ppermute | solution.py:161
  12.7 13.1 %collective-permute-start.3 = (bf16[32,4096]{1,0:T(8,128)(2,1)}, bf16[32,4096]{1,0:T(8,128)(2,1)S(1)}, u32[]{:S(2)}, u32[]{:S(2)}) collective-permute-start(bf16[32,4096]{1,0:T(8,128)(2,1)} %bitcast.37.refs_0_), channel_id=1, source_target_pairs={{0,64},{64,128},{128,192},{192,0},{1,65},{65,129},{129,193},{193,1... | collective-permute-start | bytes 786440 | tf_op jit(solution)/shard_map/ppermute | solution.py:161
  15.9 9.9 %collective-permute-start.2 = (f32[64,128]{1,0:T(8,128)S(1)}, f32[64,128]{1,0:T(8,128)S(1)}, u32[]{:S(2)}, u32[]{:S(2)}) collective-permute-start(f32[64,128]{1,0:T(8,128)S(1)} %add.436), channel_id=1, source_target_pairs={{0,48},{16,32},{32,16},{48,0},{1,49},{17,33},{33,17},{49,1},{2,50}... | collective-permute-start | bytes 98312 | tf_op jit(solution)/shard_map/ppermute | solution.py:167
  18.4 17.8 %collective-permute-start.10 = (bf16[32,4096]{1,0:T(8,128)(2,1)}, bf16[32,4096]{1,0:T(8,128)(2,1)S(1)}, u32[]{:S(2)}, u32[]{:S(2)}) collective-permute-start(bf16[32,4096]{1,0:T(8,128)(2,1)} %bitcast.37.refs_0_), channel_id=1, source_target_pairs={{0,32},{16,48},{32,0},{48,16},{1,33},{17,49},{33,1},{49,17},{2,34}... | collective-permute-start | bytes 786440 | tf_op jit(solution)/shard_map/ppermute | solution.py:161
  18.9 20.5 %collective-permute-start.9 = (bf16[32,4096]{1,0:T(8,128)(2,1)}, bf16[32,4096]{1,0:T(8,128)(2,1)}, u32[]{:S(2)}, u32[]{:S(2)}) collective-permute-start(bf16[32,4096]{1,0:T(8,128)(2,1)} %bitcast.37.refs_0_), channel_id=1, source_target_pairs={{0,48},{16,0},{32,16},{48,32},{1,49},{17,1},{33,17},{49,33},{2,50}... | collective-permute-start | bytes 786440 | tf_op jit(solution)/shard_map/ppermute | solution.py:161
  25.8 13.7 %collective-permute-start.8 = (bf16[32,4096]{1,0:T(8,128)(2,1)}, bf16[32,4096]{1,0:T(8,128)(2,1)S(1)}, u32[]{:S(2)}, u32[]{:S(2)}) collective-permute-start(bf16[32,4096]{1,0:T(8,128)(2,1)} %bitcast.37.refs_0_), channel_id=1, source_target_pairs={{0,16},{16,32},{32,48},{48,0},{1,17},{17,33},{33,49},{49,1},{2,18}... | collective-permute-start | bytes 786440 | tf_op jit(solution)/shard_map/ppermute | solution.py:161
  25.8 5.0 %collective-permute-start.5 = (f32[64,128]{1,0:T(8,128)S(1)}, f32[64,128]{1,0:T(8,128)S(1)}, u32[]{:S(2)}, u32[]{:S(2)}) collective-permute-start(f32[64,128]{1,0:T(8,128)S(1)} %add.437), channel_id=1, source_target_pairs={{0,64},{64,0},{128,192},{192,128},{1,65},{65,1},{129,193},{193,129... | collective-permute-start | bytes 98312 | tf_op jit(solution)/shard_map/ppermute | solution.py:167
  28.4 11.1 %collective-permute-start.7 = (bf16[16,4096]{1,0:T(8,128)(2,1)}, bf16[16,4096]{1,0:T(8,128)(2,1)}, u32[]{:S(2)}, u32[]{:S(2)}) collective-permute-start(bf16[16,4096]{1,0:T(8,128)(2,1)} %slice.19), channel_id=1, source_target_pairs={{0,192},{64,0},{128,64},{192,128},{1,193},{65,1},{129,65},{193,129... | collective-permute-start | bytes 393224 | tf_op jit(solution)/shard_map/ppermute | solution.py:161
  30.9 8.7 %collective-permute-start.6 = (bf16[16,4096]{1,0:T(8,128)(2,1)}, bf16[16,4096]{1,0:T(8,128)(2,1)}, u32[]{:S(2)}, u32[]{:S(2)}) collective-permute-start(bf16[16,4096]{1,0:T(8,128)(2,1)} %slice.18), channel_id=1, source_target_pairs={{0,64},{64,128},{128,192},{192,0},{1,65},{65,129},{129,193},{193,1... | collective-permute-start | bytes 393224 | tf_op jit(solution)/shard_map/ppermute | solution.py:161
  36.2 21.9 %collective-permute-start.13 = (bf16[64,4096]{1,0:T(8,128)(2,1)S(1)}, bf16[64,4096]{1,0:T(8,128)(2,1)S(1)}, u32[]{:S(2)}, u32[]{:S(2)}) collective-permute-start(bf16[64,4096]{1,0:T(8,128)(2,1)S(1)} %constant_dynamic-update-slice_fusion.refs_4_), channel_id=1, source_target_pairs={{0,48},{16,0},{32,16},{48,32},{1,49},{17,1},{33,17},{49,33},{2,50}... | collective-permute-start | bytes 1572872 | tf_op jit(solution)/shard_map/ppermute | solution.py:161
  39.4 18.7 %collective-permute-start.12 = (bf16[64,4096]{1,0:T(8,128)(2,1)S(1)}, bf16[64,4096]{1,0:T(8,128)(2,1)S(1)}, u32[]{:S(2)}, u32[]{:S(2)}) collective-permute-start(bf16[64,4096]{1,0:T(8,128)(2,1)S(1)} %constant_dynamic-update-slice_fusion.refs_4_), channel_id=1, source_target_pairs={{0,16},{16,32},{32,48},{48,0},{1,17},{17,33},{33,49},{49,1},{2,18}... | collective-permute-start | bytes 1572872 | tf_op jit(solution)/shard_map/ppermute | solution.py:161
  39.5 13.4 %collective-permute-start.11 = (f32[64,128]{1,0:T(8,128)S(1)}, f32[64,128]{1,0:T(8,128)S(1)}, u32[]{:S(2)}, u32[]{:S(2)}) collective-permute-start(f32[64,128]{1,0:T(8,128)S(1)} %add.438), channel_id=1, source_target_pairs={{0,192},{64,128},{128,64},{192,0},{1,193},{65,129},{129,65},{193,1... | collective-permute-start | bytes 98312 | tf_op jit(solution)/shard_map/ppermute | solution.py:167
  42.9 10.5 %collective-permute-start.14 = (bf16[32,4096]{1,0:T(8,128)(2,1)}, bf16[32,4096]{1,0:T(8,128)(2,1)}, u32[]{:S(2)}, u32[]{:S(2)}) collective-permute-start(bf16[32,4096]{1,0:T(8,128)(2,1)} %bitcast.37.refs_0_), channel_id=1, source_target_pairs={{0,8},{8,0},{1,9},{9,1},{2,10},{10,2},{3,11},{11,3},{4,12},{12,4},... | collective-permute-start | bytes 786440 | tf_op jit(solution)/shard_map/ppermute | solution.py:161
  52.9 5.2 %collective-permute-start.16 = (bf16[32,4096]{1,0:T(8,128)(2,1)}, bf16[32,4096]{1,0:T(8,128)(2,1)S(1)}, u32[]{:S(2)}, u32[]{:S(2)}) collective-permute-start(bf16[32,4096]{1,0:T(8,128)(2,1)} %collective-permute-done.9.refs_2_), channel_id=1, source_target_pairs={{0,8},{8,0},{1,9},{9,1},{2,10},{10,2},{3,11},{11,3},{4,12},{12,4},... | collective-permute-start | bytes 786440 | tf_op jit(solution)/shard_map/ppermute | solution.py:161
  53.4 4.7 %collective-permute-start.17 = (bf16[32,4096]{1,0:T(8,128)(2,1)}, bf16[32,4096]{1,0:T(8,128)(2,1)S(1)}, u32[]{:S(2)}, u32[]{:S(2)}) collective-permute-start(bf16[32,4096]{1,0:T(8,128)(2,1)} %copy-done.8), channel_id=1, source_target_pairs={{0,8},{8,0},{1,9},{9,1},{2,10},{10,2},{3,11},{11,3},{4,12},{12,4},... | collective-permute-start | bytes 786440 | tf_op jit(solution)/shard_map/ppermute | solution.py:161
  55.1 14.6 %collective-permute-start.19 = (bf16[32,4096]{1,0:T(8,128)(2,1)}, bf16[32,4096]{1,0:T(8,128)(2,1)S(1)}, u32[]{:S(2)}, u32[]{:S(2)}) collective-permute-start(bf16[32,4096]{1,0:T(8,128)(2,1)} %copy-done.6), channel_id=1, source_target_pairs={{0,48},{16,0},{32,16},{48,32},{1,49},{17,1},{33,17},{49,33},{2,50}... | collective-permute-start | bytes 786440 | tf_op jit(solution)/shard_map/ppermute | solution.py:161
  58.1 11.7 %collective-permute-start.18 = (bf16[32,4096]{1,0:T(8,128)(2,1)}, bf16[32,4096]{1,0:T(8,128)(2,1)}, u32[]{:S(2)}, u32[]{:S(2)}) collective-permute-start(bf16[32,4096]{1,0:T(8,128)(2,1)} %copy-done.6), channel_id=1, source_target_pairs={{0,16},{16,32},{32,48},{48,0},{1,17},{17,33},{33,49},{49,1},{2,18}... | collective-permute-start | bytes 786440 | tf_op jit(solution)/shard_map/ppermute | solution.py:161
  59.7 10.0 %collective-permute-start.21 = (bf16[32,4096]{1,0:T(8,128)(2,1)}, bf16[32,4096]{1,0:T(8,128)(2,1)}, u32[]{:S(2)}, u32[]{:S(2)}) collective-permute-start(bf16[32,4096]{1,0:T(8,128)(2,1)} %slice.21), channel_id=1, source_target_pairs={{0,48},{16,0},{32,16},{48,32},{1,49},{17,1},{33,17},{49,33},{2,50}... | collective-permute-start | bytes 786440 | tf_op jit(solution)/shard_map/ppermute | solution.py:161
  62.4 10.0 %collective-permute-start.20 = (bf16[32,4096]{1,0:T(8,128)(2,1)}, bf16[32,4096]{1,0:T(8,128)(2,1)}, u32[]{:S(2)}, u32[]{:S(2)}) collective-permute-start(bf16[32,4096]{1,0:T(8,128)(2,1)} %slice.20), channel_id=1, source_target_pairs={{0,16},{16,32},{32,48},{48,0},{1,17},{17,33},{33,49},{49,1},{2,18}... | collective-permute-start | bytes 786440 | tf_op jit(solution)/shard_map/ppermute | solution.py:161
  73.7 5.3 %collective-permute-start.22 = (bf16[16,4096]{1,0:T(8,128)(2,1)S(1)}, bf16[16,4096]{1,0:T(8,128)(2,1)S(1)}, u32[]{:S(2)}, u32[]{:S(2)}) collective-permute-start(bf16[16,4096]{1,0:T(8,128)(2,1)S(1)} %slice.22), channel_id=1, source_target_pairs={{0,16},{16,32},{32,48},{48,0},{1,17},{17,33},{33,49},{49,1},{2,18}... | collective-permute-start | bytes 393224 | tf_op jit(solution)/shard_map/ppermute | solution.py:161
  74.9 8.2 %collective-permute-start.27 = (bf16[32,4096]{1,0:T(8,128)(2,1)}, bf16[32,4096]{1,0:T(8,128)(2,1)S(1)}, u32[]{:S(2)}, u32[]{:S(2)}) collective-permute-start(bf16[32,4096]{1,0:T(8,128)(2,1)} %collective-permute-done.20.refs_7_), channel_id=1, source_target_pairs={{0,8},{8,0},{1,9},{9,1},{2,10},{10,2},{3,11},{11,3},{4,12},{12,4},... | collective-permute-start | bytes 786440 | tf_op jit(solution)/shard_map/ppermute | solution.py:161
  77.1 5.0 %collective-permute-start.33 = (bf16[16,4096]{1,0:T(8,128)(2,1)S(1)}, bf16[16,4096]{1,0:T(8,128)(2,1)S(1)}, u32[]{:S(2)}, u32[]{:S(2)}) collective-permute-start(bf16[16,4096]{1,0:T(8,128)(2,1)S(1)} %collective-permute-done.23.refs_13_), channel_id=1, source_target_pairs={{0,8},{8,0},{1,9},{9,1},{2,10},{10,2},{3,11},{11,3},{4,12},{12,4},... | collective-permute-start | bytes 393224 | tf_op jit(solution)/shard_map/ppermute | solution.py:161
  106.6 25.5 %all-to-all-start = ((bf16[8,128,768]{2,1,0:T(8,128)(2,1)}), bf16[8,128,768]{2,1,0:T(8,128)(2,1)}, u32[]{:S(2)}, u32[]{:S(2)}) async-start(bf16[8,128,768]{2,1,0:T(8,128)(2,1)} %bitcast.60), calls=%async_computation | async-start | bytes 3145728 | tf_op jit(solution)/shard_map/all_to_all | solution.py:246
  (32 other events, 189.5 us)

commit v4 on v3

v4 whole, which is shorter than its diff:
```python
import functools

import jax
import jax.numpy as jnp
from jax import lax
from jax.experimental import pallas as pl
from jax.experimental.pallas import tpu as pltpu
from jax.sharding import PartitionSpec as P

SEQ = 256
RANK = 64
PITCH = 72
DP = ("zh", "x", "core")
SECTION = ("zl", "y")

VMEM_BYTES = 60 * 2**20
LIGHT = pl.CostEstimate(flops=0, bytes_accessed=1024, transcendentals=0)


def params():
    return pltpu.CompilerParams(vmem_limit_bytes=VMEM_BYTES)


def shuffle_kernel(t_ref, *refs):
    x_ref, wide = refs[-2:]
    for j in range(t_ref.shape[1] // 128):
        turned = t_ref[:, 128 * j : 128 * j + 128].astype(jnp.float32).T
        wide[PITCH * 2 * j : PITCH * 2 * j + RANK, :] = turned[:RANK, :]
        wide[PITCH * (2 * j + 1) : PITCH * (2 * j + 1) + RANK, :] = turned[RANK:, :]
    for i in range(RANK):
        x_ref[0, RANK * i : RANK * i + RANK, :] = wide[pl.ds(i, RANK, stride=PITCH), :].astype(
            jnp.bfloat16
        )


def shuffle(t, first, count, held=None):
    n, width = t.shape
    specs = [pl.BlockSpec((128, width), lambda j: (j + first, 0))]
    return pl.pallas_call(
        shuffle_kernel,
        grid=(count,),
        in_specs=specs + ([] if held is None else [pl.BlockSpec(memory_space=pl.ANY)]),
        out_specs=pl.BlockSpec((1, width, 128), lambda j: (j + first, 0, 0)),
        out_shape=jax.ShapeDtypeStruct((n // 128, width, 128), jnp.bfloat16),
        input_output_aliases={} if held is None else {1: 0},
        scratch_shapes=[pltpu.VMEM((RANK * PITCH, 128), jnp.float32)],
        compiler_params=params(),
        cost_estimate=LIGHT,
    )(*((t,) if held is None else (t, held)))


def weigh_kernel(x_ref, a_ref, b_ref, y_ref, low, high):
    a, b = a_ref[...], b_ref[...]
    width = x_ref.shape[1]
    for g in range(width // 256):
        band = slice(256 * g, 256 * g + 256)
        x = jnp.concatenate([x_ref[0, band, :], x_ref[1, band, :]], axis=1)
        y = jnp.dot(a, x, preferred_element_type=jnp.float32)
        for r in range(4):
            spot = slice(PITCH * (4 * g + r), PITCH * (4 * g + r) + RANK)
            low[spot, :] = y[RANK * r : RANK * r + RANK, :128]
            high[spot, :] = y[RANK * r : RANK * r + RANK, 128:]
    for g in range(width // 256):
        parts = []
        for k in range(4 * g, 4 * g + 4):
            pair = [half[pl.ds(k, RANK, stride=PITCH), :] for half in (low, high)]
            parts.append(jnp.concatenate(pair, axis=1).astype(jnp.bfloat16))
        z = jnp.concatenate(parts, axis=0)
        y_ref[0, 256 * g : 256 * g + 256, :] = jnp.dot(
            b, z, preferred_element_type=jnp.float32
        ).astype(jnp.bfloat16)


def weigh(x, a, b):
    chunks, width, _ = x.shape
    small = pl.BlockSpec((256, 256), lambda j: (0, 0))
    return pl.pallas_call(
        weigh_kernel,
        grid=(chunks // 2,),
        in_specs=[pl.BlockSpec((2, width, 128), lambda j: (j, 0, 0)), small, small],
        out_specs=pl.BlockSpec((1, width, 256), lambda j: (j, 0, 0)),
        out_shape=jax.ShapeDtypeStruct((chunks // 2, width, 256), jnp.bfloat16),
        scratch_shapes=[pltpu.VMEM((RANK * PITCH, 128), jnp.float32)] * 2,
        compiler_params=params(),
        cost_estimate=LIGHT,
    )(x, a, b)


def score_kernel(moves, count, pos_ref, w_ref, *refs):
    pieces, y_ref, rows, sems = refs[:count], refs[count], refs[count + 1], refs[count + 2]
    first = pl.program_id(0) == 0

    @pl.when(first)
    def _():
        copies = []
        for n, (piece, start) in enumerate(moves):
            place = pl.multiple_of(pos_ref[n] * 32, 32)
            copies.append(
                pltpu.make_async_copy(
                    pieces[piece].at[pl.ds(start, 32)], rows.at[pl.ds(place, 32)], sems.at[n]
                )
            )
        for copy in copies:
            copy.start()
        for copy in copies:
            copy.wait()

    for g in range(rows.shape[0] // 256):
        band = slice(256 * g, 256 * g + 256)
        y_ref[band, :] = jnp.dot(
            rows[band, :], w_ref[0], preferred_element_type=jnp.float32
        ).astype(jnp.bfloat16)


def score(pieces, pos, weighed):
    chunks, width, _ = weighed.shape
    moves = [(k, n) for k, piece in enumerate(pieces) for n in range(0, piece.shape[0], 32)]
    total = 32 * len(moves)
    return pl.pallas_call(
        functools.partial(score_kernel, moves, len(pieces)),
        grid=(chunks,),
        in_specs=[
            pl.BlockSpec(memory_space=pltpu.SMEM),
            pl.BlockSpec((1, width, 256), lambda j: (j, 0, 0)),
        ]
        + [pl.BlockSpec(memory_space=pl.ANY)] * len(pieces),
        out_specs=pl.BlockSpec((total, 256), lambda j: (0, j)),
        out_shape=jax.ShapeDtypeStruct((total, chunks * 256), jnp.bfloat16),
        scratch_shapes=[
            pltpu.VMEM((total, width), jnp.bfloat16),
            pltpu.SemaphoreType.DMA((len(moves),)),
        ],
        compiler_params=params(),
        cost_estimate=LIGHT,
    )(pos, weighed, *pieces)


def add_kernel(part_ref, out_ref):
    total = part_ref[0].astype(jnp.float32)
    for k in range(1, part_ref.shape[0]):
        total = total + part_ref[k].astype(jnp.float32)
    out_ref[...] = total


def add_parts(parts):
    count, rows, n = parts.shape
    return pl.pallas_call(
        add_kernel,
        grid=(2,),
        in_specs=[pl.BlockSpec((count, rows // 2, n), lambda j: (0, j, 0))],
        out_specs=pl.BlockSpec((rows // 2, n), lambda j: (j, 0)),
        out_shape=jax.ShapeDtypeStruct((rows, n), jnp.float32),
        compiler_params=params(),
        cost_estimate=LIGHT,
    )(parts)


def blocks(m):
    four=jnp.concatenate([m]*4,axis=1)
    four=jnp.concatenate([four]*4,axis=0)
    r=lax.broadcasted_iota(jnp.int32,four.shape,0)//RANK
    c=lax.broadcasted_iota(jnp.int32,four.shape,1)//RANK
    return jnp.where(r==c,four,0.0).astype(jnp.bfloat16)
def inverse_kernel(tokens, s_ref, a_ref, b_ref):
    m = s_ref[...] / tokens
    row = lax.broadcasted_iota(jnp.int32, m.shape, 0)
    lane = lax.broadcasted_iota(jnp.int32, m.shape, 1)
    left = lane < RANK
    lane = jnp.where(left, lane, lane - RANK)
    diag = jnp.where(row == lane, m, 0.0)
    mean_left = jnp.sum(jnp.where(left, diag, 0.0)) / RANK
    mean_right = jnp.sum(jnp.where(left, 0.0, diag)) / RANK
    mean = jnp.where(left, mean_left, mean_right)
    m = m / mean + jnp.where(row == lane, 0.1, 0.0)
    first = left[:1]
    pick = lambda r, k: jnp.where(first, r[:, k : k + 1], r[:, RANK + k : RANK + k + 1])
    for k in range(0, RANK, 2):
        r0, r1 = m[k : k + 1, :], m[k + 1 : k + 2, :]
        c0 = jnp.where(left, m[:, k : k + 1], m[:, RANK + k : RANK + k + 1])
        c1 = jnp.where(left, m[:, k + 1 : k + 2], m[:, RANK + k + 1 : RANK + k + 2])
        d00, d01, d10, d11 = pick(r0, k), pick(r0, k + 1), pick(r1, k), pick(r1, k + 1)
        scale = 1.0 / (d00 * d11 - d01 * d10)
        at0, at1 = lane[:1] == k, lane[:1] == k + 1
        r0 = jnp.where(at0, 1.0, jnp.where(at1, 0.0, r0))
        r1 = jnp.where(at1, 1.0, jnp.where(at0, 0.0, r1))
        s0 = (d11 * r0 - d01 * r1) * scale
        s1 = (d00 * r1 - d10 * r0) * scale
        kept = jnp.where((lane == k) | (lane == k + 1), 0.0, m)
        m = kept - c0 * s0 - c1 * s1
        m = jnp.where(row == k, s0, jnp.where(row == k + 1, s1, m))
    m = m / mean
    a_ref[...] = blocks(m[:, RANK:].T)
    b_ref[...] = blocks(m[:, :RANK])


def inverses(s,tokens):
    return pl.pallas_call(functools.partial(inverse_kernel,tokens),
        out_shape=[jax.ShapeDtypeStruct((256,256),jnp.bfloat16)]*2,
        cost_estimate=LIGHT,
    )(s)


def swap(value, axis, way):
    last = lax.axis_size(axis) - 1
    pairs = [(i, i ^ 1 if way == 0 else last - i) for i in range(last + 1)]
    return value + lax.ppermute(value, axis, pairs)


def twin(value):
    return lax.ppermute(value, "core", [(0, 1), (1, 0)])


def onward(value, axis):
    pairs = []
    for zh in range(4):
        for x in range(4):
            for core in range(2):
                step = 1 - 2 * core
                to = ((zh + step) % 4, x) if axis == "zh" else (zh, (x + step) % 4)
                pairs.append(((zh * 4 + x) * 2 + core, (to[0] * 4 + to[1]) * 2 + core))
    return lax.ppermute(value, DP, pairs)


def pack_kernel(first, second, third, out):
    out[:32, :] = first[...]
    out[32:64, :] = second[...]
    out[64:, :] = third[...]


def pack(*parts):
    return pl.pallas_call(
        pack_kernel,
        out_shape=jax.ShapeDtypeStruct((96, parts[0].shape[1]), parts[0].dtype),
        compiler_params=params(),
        cost_estimate=LIGHT,
    )(*parts)


def block_ids():
    zh, x, core = (lax.axis_index(axis) for axis in DP)
    near, back = 3 - 2 * core, 1 + 2 * core
    mine = [(near, 0), (near, 1), (2, 0)]
    theirs = [(back, 1), (back, 0), (2, 1)]
    runs = [(0, [(0, 0)]), (0, [(0, 1)])]
    runs += [(near, [(0, 0)]), (near, [(0, 1)]), (2, [(0, 0)])]
    runs += [(back, [(0, 1)]), (back, [(0, 0)]), (2, [(0, 1)])]
    runs += [(0, mine), (0, theirs), (near, mine), (near, theirs), (2, mine)]
    runs += [(back, theirs), (back, mine), (2, theirs)]
    ids = []
    for turn, blocks in runs:
        for climb, other in blocks:
            ids.append((((zh + climb) % 4) * 4 + (x + turn) % 4) * 2 + (core + other) % 2)
    return jnp.stack(ids)


def on_device(layer_inputs, output_grads, proj_in, proj_out, train_log, queries, query_owner):
    local_tokens = layer_inputs.shape[1]
    total_tokens = local_tokens * lax.axis_size(DP)
    hold = lax.optimization_barrier
    own, train = queries[0], train_log[0]
    other = twin(own)
    up, up_other = onward(own, "zh"), onward(other, "zh")
    near, near_other = onward(own, "x"), onward(other, "x")

    acts = jnp.dot(layer_inputs[0], proj_in[0], preferred_element_type=jnp.float32).astype(
        jnp.bfloat16
    )
    grads = jnp.dot(output_grads[0], proj_out[0], preferred_element_type=jnp.float32).astype(
        jnp.bfloat16
    )
    down = (((0,), (0,)), ((), ()))
    in_sum = lax.dot_general(acts, acts, down, preferred_element_type=jnp.float32)
    out_sum = lax.dot_general(grads, grads, down, preferred_element_type=jnp.float32)
    sums = swap(jnp.concatenate([in_sum, out_sum], axis=1), "core", 0)
    sums, train = hold((swap(sums, "x", 0), train))
    turned = shuffle(train, 0, 2)
    sums, turned, up, up_other, near = hold(
        (swap(sums, "x", 1), turned, up, up_other, near)
    )
    far, near_far = onward(up, "zh"), onward(near, "x")
    turned = shuffle(train, 2, 2, turned)
    turned = shuffle(train, 4, 2, turned)
    sums, turned, far, near_far, near_other = hold((sums, turned, far, near_far, near_other))
    mine = pack(up, up_other, far)
    theirs = twin(mine)
    side, side_other = onward(mine, "x"), onward(theirs, "x")
    sums = swap(swap(sums, "zh", 0), "zh", 1)
    sums, turned = hold((sums, turned))
    out_blocks, in_blocks = inverses(sums, total_tokens)
    ring = [near, near_other, near_far]
    ring_twins = [twin(piece) for piece in ring]
    out_blocks, side, side_other, ring_twins = hold((out_blocks, side, side_other, ring_twins))
    side_far = onward(side, "x")
    weighed = weigh(turned, out_blocks, in_blocks)
    wide = [side, side_other]
    wide_twins = [twin(piece) for piece in wide]
    weighed, side_far, wide_twins = hold((weighed, side_far, wide_twins))
    pieces = [own, other] + ring + ring_twins + [mine, theirs] + wide + [side_far]
    pieces += wide_twins + [twin(side_far)]

    count = query_owner.shape[0]
    here = block_ids()[:, None] == query_owner[None, :]
    pos = jnp.sum(jnp.where(here, jnp.arange(count, dtype=jnp.int32)[None, :], 0), axis=1)
    ordered = score(pieces, pos, weighed)
    parts = lax.axis_size(SECTION)
    ordered = ordered.reshape(parts, ordered.shape[0] // parts, ordered.shape[1])
    arrived = lax.all_to_all(ordered, SECTION, split_axis=0, concat_axis=0, tiled=True)
    scores = add_parts(arrived)

    examples = local_tokens // SEQ
    per_example = lax.dot_general(
        grads.reshape(examples, SEQ, RANK),
        acts.reshape(examples, SEQ, RANK),
        (((1,), (1,)), ((0,), (0,))),
        preferred_element_type=jnp.float32,
    )
    fresh_grads = (per_example / SEQ).reshape(1, examples, RANK * RANK).astype(jnp.bfloat16)
    return (fresh_grads, scores)


def solution(mesh):
    fine = jax.sharding.Mesh(
        mesh.devices.reshape(4, 4, 2, 2, 4), ("zh", "x", "core", "zl", "y")
    )
    placed = (
        P(SECTION, DP, None),
        P(SECTION, DP, None),
        P(SECTION, None, None),
        P(SECTION, None, None),
        P(SECTION, DP, None),
        P(SECTION, DP, None),
        P(),
    )
    return jax.shard_map(
        on_device,
        mesh=fine,
        in_specs=placed,
        out_specs=(P(SECTION, DP, None), P(SECTION, DP)),
        check_vma=False,
    )
```

time: 135 us -> 122 us (0.904)
  starting transfers between devices: 48.8 us -> 39.1 us
  local copies, waits for them, and re-layouts: 9.07 us -> 2.47 us
  waiting for transfers between devices: 26 us -> 32.5 us
  other arithmetic: 3.94 us -> 1.49 us
    pallas_call x0 -> x3, Pallas kernels: none -> 13 us  [the longest x1 8.65 us: weigh(): pl.pallas_call(weigh_kernel, grid=(chunks // 2,), in_specs=[pl.BlockSpec(...]
    pallas_call x1, Pallas kernels: 20 us -> 13.2 us  [score(): pl.pallas_call(functools.partial(score_kernel, moves, len(pieces)), grid=...]
    ppermute x5, waiting for transfers between devices: 1.86 us -> 7.23 us  [swap(): return value + lax.ppermute(value, axis, pairs)]
    pallas_call x3, Pallas kernels: 15.4 us -> 10.3 us  [shuffle(): pl.pallas_call(shuffle_kernel, grid=(count,), in_specs=specs + ([] if hel...]
    ppermute x5, starting transfers between devices: 11.6 us -> 6.57 us  [swap(): return value + lax.ppermute(value, axis, pairs)]
    ppermute x29 -> x17, starting transfers between devices: 32.4 us -> 28.2 us  [the longest x9 17.8 us: onward(): return lax.ppermute(value, DP, pairs)]
    slice x6 -> x0, local copies, waits for them, and re-layouts: 3.84 us -> none  [forward(): return [shift(behind[:half], axis, 1), shift(ahead[half:], axis, -1)]]
    reduce_sum x1 -> x0, other arithmetic: 2.4 us -> none  [on_device(): scores = jnp.sum(arrived.astype(jnp.float32), axis=0)]
  transfers between devices with their start and end apart: 35 -> 23, of which waited for: 7 -> 9; matrix products, arithmetic and copies ran while one was open for 6% -> 4% of each run, Pallas kernels for 17% -> 20%
where the time goes in v4:
time: 122 us; the launch traced here: 121 us
  Pallas kernels  41.9 us (34%)
  starting transfers between devices  39.1 us (32%)
  waiting for transfers between devices  32.5 us (27%)
  matrix products  2.94 us (2%)
  local copies, waits for them, and re-layouts  2.47 us (2%)
  other arithmetic  1.49 us (1%)
    all_to_all x1, waiting for transfers between devices, on_device(): lax.all_to_all(ordered, SECTION, split_axis=0, concat_axis=0, tiled=True)  19.9 us
    ppermute x9, starting transfers between devices, onward(): return lax.ppermute(value, DP, pairs)  17.8 us
    pallas_call x1, Pallas kernels, score(): pl.pallas_call(functools.partial(score_kernel, moves, len(pieces)), grid=...  13.2 us
    ppermute x8, starting transfers between devices, twin(): return lax.ppermute(value, 'core', [(0, 1), (1, 0)])  10.5 us
    pallas_call x3, Pallas kernels, shuffle(): pl.pallas_call(shuffle_kernel, grid=(count,), in_specs=specs + ([] if hel...  10.3 us
    pallas_call x1, Pallas kernels, weigh(): pl.pallas_call(weigh_kernel, grid=(chunks // 2,), in_specs=[pl.BlockSpec(...  8.65 us
    ppermute x5, waiting for transfers between devices, swap(): return value + lax.ppermute(value, axis, pairs)  7.23 us
    ppermute x5, starting transfers between devices, swap(): return value + lax.ppermute(value, axis, pairs)  6.57 us
  transfers between devices with their start and end apart: 23, of which 9 were waited for; matrix products, arithmetic and copies ran while one was open for 4% of the time, Pallas kernels for 20%

profile of v4, /device:TPU:1, one launch (start us, length us, event | category | flops | bytes accessed | tf_op | source)
XLA Modules:
  0.0 121.2 jit_solution(9174583583038148229)
XLA Ops:
  0.7 3.3 %collective-permute-start.4 = (bf16[32,4096]{1,0:T(8,128)(2,1)}, bf16[32,4096]{1,0:T(8,128)(2,1)S(1)}, u32[]{:S(2)}, u32[]{:S(2)}) collective-permute-start(bf16[32,4096]{1,0:T(8,128)(2,1)} %bitcast.61), channel_id=1, source_target_pairs={{0,8},{8,0},{1,9},{9,1},{2,10},{10,2},{3,11},{11,3},{4,12},{12,4},... | collective-permute-start | bytes 786440 | tf_op jit(solution)/shard_map/ppermute | solution.py:210
  4.0 1.8 %fusion.7 = bf16[256,64]{0,1:T(8,128)(2,1)S(1)} fusion(bf16[1,256,4096]{2,1,0:T(8,128)(2,1)S(1)} %copy-done, bf16[1,4096,64]{1,2,0:T(8,128)(2,1)} %param.9), kind=kOutput, calls=%fused_computation.5 | convolution fusion | flops 134234112 | bytes 2654208 | tf_op jit(solution)/shard_map/dot_general | solution.py:265
  6.9 1.5 %collective-permute-start = (f32[64,128]{1,0:T(8,128)S(1)}, f32[64,128]{1,0:T(8,128)S(1)}, u32[]{:S(2)}, u32[]{:S(2)}) collective-permute-start(f32[64,128]{1,0:T(8,128)S(1)} %pad_maximum_fusion), channel_id=1, source_target_pairs={{0,8},{8,0},{1,9},{9,1},{2,10},{10,2},{3,11},{11,3},{4,12},{12,4},... | collective-permute-start | bytes 98312 | tf_op jit(solution)/shard_map/ppermute | solution.py:206
  9.2 6.0 %collective-permute-start.3 = (bf16[32,4096]{1,0:T(8,128)(2,1)S(1)}, bf16[32,4096]{1,0:T(8,128)(2,1)S(1)}, u32[]{:S(2)}, u32[]{:S(2)}) collective-permute-start(bf16[32,4096]{1,0:T(8,128)(2,1)S(1)} %bitcast.64), channel_id=1, source_target_pairs={{0,64},{8,200},{16,80},{24,216},{32,96},{40,232},{48,112},{56,248}... | collective-permute-start | bytes 786440 | tf_op jit(solution)/shard_map/ppermute | solution.py:221
  16.5 3.3 %collective-permute-done.1 = f32[64,128]{1,0:T(8,128)S(1)} collective-permute-done((f32[64,128]{1,0:T(8,128)S(1)}, f32[64,128]{1,0:T(8,128)S(1)}, u32[]{:S(2)}, u32[]{:S(2)}) %collective-permute-start.1) | collective-permute-done | bytes 32800 | tf_op jit(solution)/shard_map/ppermute | solution.py:206
  20.1 3.5 %shard_map.86.refs_0_ = bf16[6,4096,128]{2,1,0:T(8,128)(2,1)} custom-call(bf16[768,4096]{1,0:T(8,128)(2,1)} %bitcast.57), custom_call_target="tpu_custom_call" | custom-call | bytes 1024 | tf_op jit(solution)/shard_map/pallas_call | solution.py:39
  24.1 2.0 %collective-permute-start.9 = (bf16[32,4096]{1,0:T(8,128)(2,1)S(1)}, bf16[32,4096]{1,0:T(8,128)(2,1)}, u32[]{:S(2)}, u32[]{:S(2)}) collective-permute-start(bf16[32,4096]{1,0:T(8,128)(2,1)S(1)} %collective-permute-done.4.refs_1_), channel_id=1, source_target_pairs={{0,16},{8,56},{16,32},{24,8},{32,48},{40,24},{48,0},{56,40},{64,80... | collective-permute-start | bytes 786440 | tf_op jit(solution)/shard_map/ppermute | solution.py:221
  26.9 4.0 %collective-permute-start.7 = (bf16[32,4096]{1,0:T(8,128)(2,1)S(1)}, bf16[32,4096]{1,0:T(8,128)(2,1)S(1)}, u32[]{:S(2)}, u32[]{:S(2)}) collective-permute-start(bf16[32,4096]{1,0:T(8,128)(2,1)S(1)} %collective-permute-done.3.first), channel_id=1, source_target_pairs={{0,64},{8,200},{16,80},{24,216},{32,96},{40,232},{48,112},{56,248}... | collective-permute-start | bytes 786440 | tf_op jit(solution)/shard_map/ppermute | solution.py:221
  31.5 3.4 %shard_map.87.refs_0_ = bf16[6,4096,128]{2,1,0:T(8,128)(2,1)} custom-call(bf16[768,4096]{1,0:T(8,128)(2,1)} %bitcast.58, bf16[6,4096,128]{2,1,0:T(8,128)(2,1)} %shard_map.86.refs_0_), custom_call_target="tpu_custom_call", output_to_operand_aliasing={{}: (1, {})} | custom-call | bytes 1024 | tf_op jit(solution)/shard_map/pallas_call | solution.py:39
  34.9 3.4 %shard_map.88.x_ref = bf16[6,4096,128]{2,1,0:T(8,128)(2,1)} custom-call(bf16[768,4096]{1,0:T(8,128)(2,1)} %bitcast.59, bf16[6,4096,128]{2,1,0:T(8,128)(2,1)} %shard_map.87.refs_0_), custom_call_target="tpu_custom_call", output_to_operand_aliasing={{}: (1, {})} | custom-call | bytes 1024 | tf_op jit(solution)/shard_map/pallas_call | solution.py:39
  39.1 2.2 %shard_map.90.refs_8_ = bf16[96,4096]{1,0:T(8,128)(2,1)} custom-call(bf16[32,4096]{1,0:T(8,128)(2,1)} %copy-done.9, bf16[32,4096]{1,0:T(8,128)(2,1)} %copy-done.10, bf16[32,4096]{1,0:T(8,128)(2,1)} %copy-done.11), custom_call_target="tpu_custom_call" | custom-call | bytes 1024 | tf_op jit(solution)/shard_map/pallas_call | solution.py:231
  44.9 2.6 %collective-permute-start.10 = (f32[64,128]{1,0:T(8,128)S(1)}, f32[64,128]{1,0:T(8,128)S(1)}, u32[]{:S(2)}, u32[]{:S(2)}) collective-permute-start(f32[64,128]{1,0:T(8,128)S(1)} %add.441), channel_id=1, source_target_pairs={{0,64},{64,0},{128,192},{192,128},{1,65},{65,1},{129,193},{193,129... | collective-permute-start | bytes 98312 | tf_op jit(solution)/shard_map/ppermute | solution.py:206
  47.4 1.7 %collective-permute-done.10 = f32[64,128]{1,0:T(8,128)S(1)} collective-permute-done((f32[64,128]{1,0:T(8,128)S(1)}, f32[64,128]{1,0:T(8,128)S(1)}, u32[]{:S(2)}, u32[]{:S(2)}) %collective-permute-start.10) | collective-permute-done | bytes 32800 | tf_op jit(solution)/shard_map/ppermute | solution.py:206
  49.1 2.1 %collective-permute-start.11 = (f32[64,128]{1,0:T(8,128)S(1)}, f32[64,128]{1,0:T(8,128)S(1)}, u32[]{:S(2)}, u32[]{:S(2)}) collective-permute-start(f32[64,128]{1,0:T(8,128)S(1)} %add.442), channel_id=1, source_target_pairs={{0,192},{64,128},{128,64},{192,0},{1,193},{65,129},{129,65},{193,1... | collective-permute-start | bytes 98312 | tf_op jit(solution)/shard_map/ppermute | solution.py:206
  52.1 1.8 %collective-permute-done.11 = f32[64,128]{1,0:T(8,128)S(1)} collective-permute-done((f32[64,128]{1,0:T(8,128)S(1)}, f32[64,128]{1,0:T(8,128)S(1)}, u32[]{:S(2)}, u32[]{:S(2)}) %collective-permute-start.11) | collective-permute-done | bytes 32800 | tf_op jit(solution)/shard_map/ppermute | solution.py:206
  54.0 2.3 %collective-permute-start.17 = (bf16[32,4096]{1,0:T(8,128)(2,1)S(1)}, bf16[32,4096]{1,0:T(8,128)(2,1)}, u32[]{:S(2)}, u32[]{:S(2)}) collective-permute-start(bf16[32,4096]{1,0:T(8,128)(2,1)S(1)} %collective-permute-done.8.refs_4_), channel_id=1, source_target_pairs={{0,8},{8,0},{1,9},{9,1},{2,10},{10,2},{3,11},{11,3},{4,12},{12,4},... | collective-permute-start | bytes 786440 | tf_op jit(solution)/shard_map/ppermute | solution.py:210
  56.9 5.4 %shard_map.89 = (bf16[256,256]{1,0:T(8,128)(2,1)}, bf16[256,256]{1,0:T(8,128)(2,1)}) custom-call(f32[64,128]{1,0:T(8,128)} %add.443.s_ref), custom_call_target="tpu_custom_call" | custom-call | bytes 1024 | tf_op jit(solution)/shard_map/pallas_call | solution.py:197
  64.4 8.7 %shard_map.91.w_ref = bf16[3,4096,256]{2,1,0:T(8,128)(2,1)} custom-call(bf16[6,4096,128]{2,1,0:T(8,128)(2,1)} %shard_map.88.x_ref, bf16[256,256]{1,0:T(8,128)(2,1)} %get-tuple-element.43.a_ref, bf16[256,256]{1,0:T(8,128)(2,1)} %get-tuple-element.44.b_ref), custom_call_target="tpu_custom_call" | custom-call | bytes 1024 | tf_op jit(solution)/shard_map/pallas_call | solution.py:77
  73.1 2.1 %collective-permute-done.18.refs_12_ = bf16[96,4096]{1,0:T(8,128)(2,1)} collective-permute-done((bf16[96,4096]{1,0:T(8,128)(2,1)}, bf16[96,4096]{1,0:T(8,128)(2,1)}, u32[]{:S(2)}, u32[]{:S(2)}) %collective-permute-start.18) | collective-permute-done | bytes 786464 | tf_op jit(solution)/shard_map/ppermute | solution.py:221
  75.2 2.6 %collective-permute-start.21 = (bf16[96,4096]{1,0:T(8,128)(2,1)}, bf16[96,4096]{1,0:T(8,128)(2,1)S(1)}, u32[]{:S(2)}, u32[]{:S(2)}) collective-permute-start(bf16[96,4096]{1,0:T(8,128)(2,1)} %collective-permute-done.18.refs_12_), channel_id=1, source_target_pairs={{0,8},{8,0},{1,9},{9,1},{2,10},{10,2},{3,11},{11,3},{4,12},{12,4},... | collective-permute-start | bytes 2359304 | tf_op jit(solution)/shard_map/ppermute | solution.py:210
  80.8 13.2 %shard_map.92 = bf16[1024,768]{1,0:T(8,128)(2,1)} custom-call(s32[32]{0:T(128)} %select_reduce_fusion.pos_ref, bf16[3,4096,256]{2,1,0:T(8,128)(2,1)} %shard_map.91.w_ref, bf16[32,4096]{1,0:T(8,128)(2,1)} %bitcast.62, bf16[32,4096]{1,0:T(8,128)(2,1)} %copy-done.6, bf16[32,4096]{1,0:T(8,128)(2,1)} %collective-permute-done.6.refs_2_, ...), custom_call_target="tpu_custom_call" | custom-call | bytes 1024 | tf_op jit(solution)/shard_map/pallas_call | solution.py:119
  94.0 4.3 %all-to-all-start = ((bf16[8,128,768]{2,1,0:T(8,128)(2,1)}), bf16[8,128,768]{2,1,0:T(8,128)(2,1)}, u32[]{:S(2)}, u32[]{:S(2)}) async-start(bf16[8,128,768]{2,1,0:T(8,128)(2,1)} %bitcast.60), calls=%async_computation | async-start | bytes 3145728 | tf_op jit(solution)/shard_map/all_to_all | solution.py:307
  99.1 19.9 %all-to-all-done.part_ref = bf16[8,128,768]{2,1,0:T(8,128)(2,1)} async-done(((bf16[8,128,768]{2,1,0:T(8,128)(2,1)}), bf16[8,128,768]{2,1,0:T(8,128)(2,1)}, u32[]{:S(2)}, u32[]{:S(2)}) %all-to-all-start) | async-done | bytes 1572896 | tf_op jit(solution)/shard_map/all_to_all | solution.py:307
  119.1 2.1 %shard_map.93 = f32[128,768]{1,0:T(8,128)} custom-call(bf16[8,128,768]{2,1,0:T(8,128)(2,1)} %all-to-all-done.part_ref), custom_call_target="tpu_custom_call" | custom-call | bytes 1024 | tf_op jit(solution)/shard_map/pallas_call | solution.py:147
  (70 shorter events, 17.2 us)
Async XLA Ops:
  0.7 14.5 %collective-permute-start.4 = (bf16[32,4096]{1,0:T(8,128)(2,1)}, bf16[32,4096]{1,0:T(8,128)(2,1)S(1)}, u32[]{:S(2)}, u32[]{:S(2)}) collective-permute-start(bf16[32,4096]{1,0:T(8,128)(2,1)} %bitcast.61), channel_id=1, source_target_pairs={{0,8},{8,0},{1,9},{9,1},{2,10},{10,2},{3,11},{11,3},{4,12},{12,4},... | collective-permute-start | bytes 786440 | tf_op jit(solution)/shard_map/ppermute | solution.py:210
  6.9 9.5 %collective-permute-start = (f32[64,128]{1,0:T(8,128)S(1)}, f32[64,128]{1,0:T(8,128)S(1)}, u32[]{:S(2)}, u32[]{:S(2)}) collective-permute-start(f32[64,128]{1,0:T(8,128)S(1)} %pad_maximum_fusion), channel_id=1, source_target_pairs={{0,8},{8,0},{1,9},{9,1},{2,10},{10,2},{3,11},{11,3},{4,12},{12,4},... | collective-permute-start | bytes 98312 | tf_op jit(solution)/shard_map/ppermute | solution.py:206
  8.4 17.6 %collective-permute-start.6 = (bf16[32,4096]{1,0:T(8,128)(2,1)S(1)}, bf16[32,4096]{1,0:T(8,128)(2,1)}, u32[]{:S(2)}, u32[]{:S(2)}) collective-permute-start(bf16[32,4096]{1,0:T(8,128)(2,1)S(1)} %bitcast.63), channel_id=1, source_target_pairs={{0,16},{8,56},{16,32},{24,8},{32,48},{40,24},{48,0},{56,40},{64,80... | collective-permute-start | bytes 786440 | tf_op jit(solution)/shard_map/ppermute | solution.py:221
  9.2 16.9 %collective-permute-start.3 = (bf16[32,4096]{1,0:T(8,128)(2,1)S(1)}, bf16[32,4096]{1,0:T(8,128)(2,1)S(1)}, u32[]{:S(2)}, u32[]{:S(2)}) collective-permute-start(bf16[32,4096]{1,0:T(8,128)(2,1)S(1)} %bitcast.64), channel_id=1, source_target_pairs={{0,64},{8,200},{16,80},{24,216},{32,96},{40,232},{48,112},{56,248}... | collective-permute-start | bytes 786440 | tf_op jit(solution)/shard_map/ppermute | solution.py:221
  15.2 11.7 %collective-permute-start.5 = (bf16[32,4096]{1,0:T(8,128)(2,1)S(1)}, bf16[32,4096]{1,0:T(8,128)(2,1)S(1)}, u32[]{:S(2)}, u32[]{:S(2)}) collective-permute-start(bf16[32,4096]{1,0:T(8,128)(2,1)S(1)} %collective-permute-done.4.refs_1_), channel_id=1, source_target_pairs={{0,64},{8,200},{16,80},{24,216},{32,96},{40,232},{48,112},{56,248}... | collective-permute-start | bytes 786440 | tf_op jit(solution)/shard_map/ppermute | solution.py:221
  16.5 3.3 %collective-permute-start.1 = (f32[64,128]{1,0:T(8,128)S(1)}, f32[64,128]{1,0:T(8,128)S(1)}, u32[]{:S(2)}, u32[]{:S(2)}) collective-permute-start(f32[64,128]{1,0:T(8,128)S(1)} %fusion.21), channel_id=1, source_target_pairs={{0,16},{16,0},{32,48},{48,32},{1,17},{17,1},{33,49},{49,33},{2,18}... | collective-permute-start | bytes 98312 | tf_op jit(solution)/shard_map/ppermute | solution.py:206
  19.8 4.3 %collective-permute-start.2 = (f32[64,128]{1,0:T(8,128)S(1)}, f32[64,128]{1,0:T(8,128)S(1)}, u32[]{:S(2)}, u32[]{:S(2)}) collective-permute-start(f32[64,128]{1,0:T(8,128)S(1)} %add.440), channel_id=1, source_target_pairs={{0,48},{16,32},{32,16},{48,0},{1,49},{17,33},{33,17},{49,1},{2,50}... | collective-permute-start | bytes 98312 | tf_op jit(solution)/shard_map/ppermute | solution.py:206
  24.1 14.3 %collective-permute-start.9 = (bf16[32,4096]{1,0:T(8,128)(2,1)S(1)}, bf16[32,4096]{1,0:T(8,128)(2,1)}, u32[]{:S(2)}, u32[]{:S(2)}) collective-permute-start(bf16[32,4096]{1,0:T(8,128)(2,1)S(1)} %collective-permute-done.4.refs_1_), channel_id=1, source_target_pairs={{0,16},{8,56},{16,32},{24,8},{32,48},{40,24},{48,0},{56,40},{64,80... | collective-permute-start | bytes 786440 | tf_op jit(solution)/shard_map/ppermute | solution.py:221
  26.9 11.4 %collective-permute-start.7 = (bf16[32,4096]{1,0:T(8,128)(2,1)S(1)}, bf16[32,4096]{1,0:T(8,128)(2,1)S(1)}, u32[]{:S(2)}, u32[]{:S(2)}) collective-permute-start(bf16[32,4096]{1,0:T(8,128)(2,1)S(1)} %collective-permute-done.3.first), channel_id=1, source_target_pairs={{0,64},{8,200},{16,80},{24,216},{32,96},{40,232},{48,112},{56,248}... | collective-permute-start | bytes 786440 | tf_op jit(solution)/shard_map/ppermute | solution.py:221
  31.0 7.4 %collective-permute-start.8 = (bf16[32,4096]{1,0:T(8,128)(2,1)}, bf16[32,4096]{1,0:T(8,128)(2,1)S(1)}, u32[]{:S(2)}, u32[]{:S(2)}) collective-permute-start(bf16[32,4096]{1,0:T(8,128)(2,1)} %collective-permute-done.6.refs_2_), channel_id=1, source_target_pairs={{0,16},{8,56},{16,32},{24,8},{32,48},{40,24},{48,0},{56,40},{64,80... | collective-permute-start | bytes 786440 | tf_op jit(solution)/shard_map/ppermute | solution.py:221
  39.1 33.9 %copy-start.7 = (bf16[32,4096]{1,0:T(8,128)(2,1)}, bf16[32,4096]{1,0:T(8,128)(2,1)S(1)}, u32[]{:S(2)}) copy-start(bf16[32,4096]{1,0:T(8,128)(2,1)S(1)} %collective-permute-done.8.refs_4_) | copy-start | bytes 786436
  41.2 2.5 %collective-permute-start.13 = (bf16[96,4096]{1,0:T(8,128)(2,1)}, bf16[96,4096]{1,0:T(8,128)(2,1)S(1)}, u32[]{:S(2)}, u32[]{:S(2)}) collective-permute-start(bf16[96,4096]{1,0:T(8,128)(2,1)} %shard_map.90.refs_8_), channel_id=1, source_target_pairs={{0,8},{8,0},{1,9},{9,1},{2,10},{10,2},{3,11},{11,3},{4,12},{12,4},... | collective-permute-start | bytes 2359304 | tf_op jit(solution)/shard_map/ppermute | solution.py:210
  41.2 21.0 %collective-permute-start.12 = (bf16[96,4096]{1,0:T(8,128)(2,1)}, bf16[96,4096]{1,0:T(8,128)(2,1)}, u32[]{:S(2)}, u32[]{:S(2)}) collective-permute-start(bf16[96,4096]{1,0:T(8,128)(2,1)} %shard_map.90.refs_8_), channel_id=1, source_target_pairs={{0,16},{8,56},{16,32},{24,8},{32,48},{40,24},{48,0},{56,40},{64,80... | collective-permute-start | bytes 2359304 | tf_op jit(solution)/shard_map/ppermute | solution.py:221
  43.7 18.5 %collective-permute-start.14 = (bf16[96,4096]{1,0:T(8,128)(2,1)S(1)}, bf16[96,4096]{1,0:T(8,128)(2,1)}, u32[]{:S(2)}, u32[]{:S(2)}) collective-permute-start(bf16[96,4096]{1,0:T(8,128)(2,1)S(1)} %collective-permute-done.13.refs_9_), channel_id=1, source_target_pairs={{0,16},{8,56},{16,32},{24,8},{32,48},{40,24},{48,0},{56,40},{64,80... | collective-permute-start | bytes 2359304 | tf_op jit(solution)/shard_map/ppermute | solution.py:221
  44.9 4.2 %collective-permute-start.10 = (f32[64,128]{1,0:T(8,128)S(1)}, f32[64,128]{1,0:T(8,128)S(1)}, u32[]{:S(2)}, u32[]{:S(2)}) collective-permute-start(f32[64,128]{1,0:T(8,128)S(1)} %add.441), channel_id=1, source_target_pairs={{0,64},{64,0},{128,192},{192,128},{1,65},{65,1},{129,193},{193,129... | collective-permute-start | bytes 98312 | tf_op jit(solution)/shard_map/ppermute | solution.py:206
  49.1 4.9 %collective-permute-start.11 = (f32[64,128]{1,0:T(8,128)S(1)}, f32[64,128]{1,0:T(8,128)S(1)}, u32[]{:S(2)}, u32[]{:S(2)}) collective-permute-start(f32[64,128]{1,0:T(8,128)S(1)} %add.442), channel_id=1, source_target_pairs={{0,192},{64,128},{128,64},{192,0},{1,193},{65,129},{129,65},{193,1... | collective-permute-start | bytes 98312 | tf_op jit(solution)/shard_map/ppermute | solution.py:206
  51.2 11.0 %collective-permute-start.15 = (bf16[32,4096]{1,0:T(8,128)(2,1)}, bf16[32,4096]{1,0:T(8,128)(2,1)S(1)}, u32[]{:S(2)}, u32[]{:S(2)}) collective-permute-start(bf16[32,4096]{1,0:T(8,128)(2,1)} %collective-permute-done.6.refs_2_), channel_id=1, source_target_pairs={{0,8},{8,0},{1,9},{9,1},{2,10},{10,2},{3,11},{11,3},{4,12},{12,4},... | collective-permute-start | bytes 786440 | tf_op jit(solution)/shard_map/ppermute | solution.py:210
  52.1 10.1 %collective-permute-start.16 = (bf16[32,4096]{1,0:T(8,128)(2,1)}, bf16[32,4096]{1,0:T(8,128)(2,1)}, u32[]{:S(2)}, u32[]{:S(2)}) collective-permute-start(bf16[32,4096]{1,0:T(8,128)(2,1)} %collective-permute-done.9.refs_3_), channel_id=1, source_target_pairs={{0,8},{8,0},{1,9},{9,1},{2,10},{10,2},{3,11},{11,3},{4,12},{12,4},... | collective-permute-start | bytes 786440 | tf_op jit(solution)/shard_map/ppermute | solution.py:210
  54.0 8.3 %collective-permute-start.17 = (bf16[32,4096]{1,0:T(8,128)(2,1)S(1)}, bf16[32,4096]{1,0:T(8,128)(2,1)}, u32[]{:S(2)}, u32[]{:S(2)}) collective-permute-start(bf16[32,4096]{1,0:T(8,128)(2,1)S(1)} %collective-permute-done.8.refs_4_), channel_id=1, source_target_pairs={{0,8},{8,0},{1,9},{9,1},{2,10},{10,2},{3,11},{11,3},{4,12},{12,4},... | collective-permute-start | bytes 786440 | tf_op jit(solution)/shard_map/ppermute | solution.py:210
  62.3 10.7 %collective-permute-start.20 = (bf16[96,4096]{1,0:T(8,128)(2,1)}, bf16[96,4096]{1,0:T(8,128)(2,1)}, u32[]{:S(2)}, u32[]{:S(2)}) collective-permute-start(bf16[96,4096]{1,0:T(8,128)(2,1)} %collective-permute-done.14.refs_11_), channel_id=1, source_target_pairs={{0,8},{8,0},{1,9},{9,1},{2,10},{10,2},{3,11},{11,3},{4,12},{12,4},... | collective-permute-start | bytes 2359304 | tf_op jit(solution)/shard_map/ppermute | solution.py:210
  63.7 9.3 %collective-permute-start.19 = (bf16[96,4096]{1,0:T(8,128)(2,1)}, bf16[96,4096]{1,0:T(8,128)(2,1)}, u32[]{:S(2)}, u32[]{:S(2)}) collective-permute-start(bf16[96,4096]{1,0:T(8,128)(2,1)} %collective-permute-done.12.refs_10_), channel_id=1, source_target_pairs={{0,8},{8,0},{1,9},{9,1},{2,10},{10,2},{3,11},{11,3},{4,12},{12,4},... | collective-permute-start | bytes 2359304 | tf_op jit(solution)/shard_map/ppermute | solution.py:210
  63.7 11.5 %collective-permute-start.18 = (bf16[96,4096]{1,0:T(8,128)(2,1)}, bf16[96,4096]{1,0:T(8,128)(2,1)}, u32[]{:S(2)}, u32[]{:S(2)}) collective-permute-start(bf16[96,4096]{1,0:T(8,128)(2,1)} %collective-permute-done.12.refs_10_), channel_id=1, source_target_pairs={{0,16},{8,56},{16,32},{24,8},{32,48},{40,24},{48,0},{56,40},{64,80... | collective-permute-start | bytes 2359304 | tf_op jit(solution)/shard_map/ppermute | solution.py:221
  75.2 4.7 %collective-permute-start.21 = (bf16[96,4096]{1,0:T(8,128)(2,1)}, bf16[96,4096]{1,0:T(8,128)(2,1)S(1)}, u32[]{:S(2)}, u32[]{:S(2)}) collective-permute-start(bf16[96,4096]{1,0:T(8,128)(2,1)} %collective-permute-done.18.refs_12_), channel_id=1, source_target_pairs={{0,8},{8,0},{1,9},{9,1},{2,10},{10,2},{3,11},{11,3},{4,12},{12,4},... | collective-permute-start | bytes 2359304 | tf_op jit(solution)/shard_map/ppermute | solution.py:210
  94.0 25.1 %all-to-all-start = ((bf16[8,128,768]{2,1,0:T(8,128)(2,1)}), bf16[8,128,768]{2,1,0:T(8,128)(2,1)}, u32[]{:S(2)}, u32[]{:S(2)}) async-start(bf16[8,128,768]{2,1,0:T(8,128)(2,1)} %bitcast.60), calls=%async_computation | async-start | bytes 3145728 | tf_op jit(solution)/shard_map/all_to_all | solution.py:307
  (12 other events, 97.5 us)

commit v5 on v4

--- a/solution.py
+++ b/solution.py
@@ -221,16 +221,15 @@
     return lax.ppermute(value, DP, pairs)
 
 
-def pack_kernel(first, second, third, out):
+def pack_kernel(first, second, out):
     out[:32, :] = first[...]
-    out[32:64, :] = second[...]
-    out[64:, :] = third[...]
+    out[32:, :] = second[...]
 
 
 def pack(*parts):
     return pl.pallas_call(
         pack_kernel,
-        out_shape=jax.ShapeDtypeStruct((96, parts[0].shape[1]), parts[0].dtype),
+        out_shape=jax.ShapeDtypeStruct((64, parts[0].shape[1]), parts[0].dtype),
         compiler_params=params(),
         cost_estimate=LIGHT,
     )(*parts)
@@ -239,13 +238,15 @@
 def block_ids():
     zh, x, core = (lax.axis_index(axis) for axis in DP)
     near, back = 3 - 2 * core, 1 + 2 * core
-    mine = [(near, 0), (near, 1), (2, 0)]
-    theirs = [(back, 1), (back, 0), (2, 1)]
+    mine, theirs = [(near, 0), (near, 1)], [(back, 1), (back, 0)]
+    far, far_twin = [(2, 0)], [(2, 1)]
     runs = [(0, [(0, 0)]), (0, [(0, 1)])]
     runs += [(near, [(0, 0)]), (near, [(0, 1)]), (2, [(0, 0)])]
     runs += [(back, [(0, 1)]), (back, [(0, 0)]), (2, [(0, 1)])]
-    runs += [(0, mine), (0, theirs), (near, mine), (near, theirs), (2, mine)]
-    runs += [(back, theirs), (back, mine), (2, theirs)]
+    runs += [(0, mine), (0, theirs), (0, far), (0, far_twin)]
+    runs += [(near, mine), (near, theirs), (near, far), (near, far_twin)]
+    runs += [(back, theirs), (back, mine), (back, far_twin), (back, far)]
+    runs += [(2, mine), (2, far), (2, theirs), (2, far_twin)]
     ids = []
     for turn, blocks in runs:
         for climb, other in blocks:
@@ -272,35 +273,40 @@
     in_sum = lax.dot_general(acts, acts, down, preferred_element_type=jnp.float32)
     out_sum = lax.dot_general(grads, grads, down, preferred_element_type=jnp.float32)
     sums = swap(jnp.concatenate([in_sum, out_sum], axis=1), "core", 0)
-    sums, train = hold((swap(sums, "x", 0), train))
+    count = query_owner.shape[0]
+    here = block_ids()[:, None] == query_owner[None, :]
+    pos = jnp.sum(jnp.where(here, jnp.arange(count, dtype=jnp.int32)[None, :], 0), axis=1)
+    sums, train, pos = hold((swap(sums, "x", 0), train, pos))
     turned = shuffle(train, 0, 2)
     sums, turned, up, up_other, near = hold(
         (swap(sums, "x", 1), turned, up, up_other, near)
     )
     far, near_far = onward(up, "zh"), onward(near, "x")
+    pair = pack(up, up_other)
+    pair_twin = twin(pair)
+    side, side_other = onward(pair, "x"), onward(pair_twin, "x")
+    sums = swap(sums, "zh", 0)
     turned = shuffle(train, 2, 2, turned)
     turned = shuffle(train, 4, 2, turned)
     sums, turned, far, near_far, near_other = hold((sums, turned, far, near_far, near_other))
-    mine = pack(up, up_other, far)
-    theirs = twin(mine)
-    side, side_other = onward(mine, "x"), onward(theirs, "x")
-    sums = swap(swap(sums, "zh", 0), "zh", 1)
-    sums, turned = hold((sums, turned))
+    far_twin = twin(far)
+    far_side, far_side_other = onward(far, "x"), onward(far_twin, "x")
+    sums, side = hold((swap(sums, "zh", 1), side))
+    side_far = onward(side, "x")
     out_blocks, in_blocks = inverses(sums, total_tokens)
     ring = [near, near_other, near_far]
     ring_twins = [twin(piece) for piece in ring]
-    out_blocks, side, side_other, ring_twins = hold((out_blocks, side, side_other, ring_twins))
-    side_far = onward(side, "x")
+    out_blocks, far_side, far_side_other, side_other, ring_twins = hold(
+        (out_blocks, far_side, far_side_other, side_other, ring_twins)
+    )
+    last = [side_far, onward(far_side, "x")]
     weighed = weigh(turned, out_blocks, in_blocks)
-    wide = [side, side_other]
+    wide = [side, side_other, far_side, far_side_other]
     wide_twins = [twin(piece) for piece in wide]
-    weighed, side_far, wide_twins = hold((weighed, side_far, wide_twins))
-    pieces = [own, other] + ring + ring_twins + [mine, theirs] + wide + [side_far]
-    pieces += wide_twins + [twin(side_far)]
-
-    count = query_owner.shape[0]
-    here = block_ids()[:, None] == query_owner[None, :]
-    pos = jnp.sum(jnp.where(here, jnp.arange(count, dtype=jnp.int32)[None, :], 0), axis=1)
+    weighed, last, wide_twins = hold((weighed, last, wide_twins))
+    pieces = [own, other] + ring + ring_twins + [pair, pair_twin, far, far_twin]
+    pieces += wide + wide_twins + last + [twin(piece) for piece in last]
+
     ordered = score(pieces, pos, weighed)
     parts = lax.axis_size(SECTION)
     ordered = ordered.reshape(parts, ordered.shape[0] // parts, ordered.shape[1])

time: 122 us -> 120 us (0.984)
  waiting for transfers between devices: 32.5 us -> 29.4 us
  local copies, waits for them, and re-layouts: 2.47 us -> 3.82 us
    ppermute x5, waiting for transfers between devices: 7.23 us -> 3.91 us  [swap(): return value + lax.ppermute(value, axis, pairs)]
    ppermute x5, starting transfers between devices: 6.57 us -> 3.86 us  [swap(): return value + lax.ppermute(value, axis, pairs)]
    ppermute x9 -> x12, starting transfers between devices: 17.8 us -> 20.1 us  [onward(): return lax.ppermute(value, DP, pairs)]
    unnamed x26 -> x30, local copies, waits for them, and re-layouts: 1.65 us -> 3.01 us
    ppermute x9 -> x12, waiting for transfers between devices: 3 us -> 3.57 us  [onward(): return lax.ppermute(value, DP, pairs)]
    ppermute x8 -> x12, starting transfers between devices: 10.5 us -> 10.7 us  [twin(): return lax.ppermute(value, 'core', [(0, 1), (1, 0)])]
  transfers between devices with their start and end apart: 23 -> 30, of which waited for: 9 -> 7; matrix products, arithmetic and copies ran while one was open for 4% -> 4% of each run, Pallas kernels for 20% -> 20%
where the time goes in v5:
time: 120 us; the launch traced here: 119 us
  Pallas kernels  41.6 us (35%)
  starting transfers between devices  39 us (32%)
  waiting for transfers between devices  29.4 us (24%)
  local copies, waits for them, and re-layouts  3.82 us (3%)
  matrix products  2.94 us (2%)
  other arithmetic  1.5 us (1%)
    ppermute x12, starting transfers between devices, onward(): return lax.ppermute(value, DP, pairs)  20.1 us
    all_to_all x1, waiting for transfers between devices, on_device(): lax.all_to_all(ordered, SECTION, split_axis=0, concat_axis=0, tiled=True)  19.9 us
    pallas_call x1, Pallas kernels, score(): pl.pallas_call(functools.partial(score_kernel, moves, len(pieces)), grid=...  13.2 us
    ppermute x12, starting transfers between devices, twin(): return lax.ppermute(value, 'core', [(0, 1), (1, 0)])  10.7 us
    pallas_call x3, Pallas kernels, shuffle(): pl.pallas_call(shuffle_kernel, grid=(count,), in_specs=specs + ([] if hel...  10.3 us
    pallas_call x1, Pallas kernels, weigh(): pl.pallas_call(weigh_kernel, grid=(chunks // 2,), in_specs=[pl.BlockSpec(...  8.66 us
    pallas_call x1, Pallas kernels, inverses(): pl.pallas_call(functools.partial(inverse_kernel, tokens), out_shape=[jax....  5.39 us
    all_to_all x1, starting transfers between devices, on_device(): lax.all_to_all(ordered, SECTION, split_axis=0, concat_axis=0, tiled=True)  4.31 us
  transfers between devices with their start and end apart: 30, of which 7 were waited for; matrix products, arithmetic and copies ran while one was open for 4% of the time, Pallas kernels for 20%

profile of v5, /device:TPU:1, one launch (start us, length us, event | category | flops | bytes accessed | tf_op | source)
XLA Modules:
  0.0 119.2 jit_solution(9606236697387774216)
XLA Ops:
  0.7 3.3 %collective-permute-start.4 = (bf16[32,4096]{1,0:T(8,128)(2,1)}, bf16[32,4096]{1,0:T(8,128)(2,1)}, u32[]{:S(2)}, u32[]{:S(2)}) collective-permute-start(bf16[32,4096]{1,0:T(8,128)(2,1)} %bitcast.61), channel_id=1, source_target_pairs={{0,8},{8,0},{1,9},{9,1},{2,10},{10,2},{3,11},{11,3},{4,12},{12,4},... | collective-permute-start | bytes 786440 | tf_op jit(solution)/shard_map/ppermute | solution.py:210
  4.0 1.8 %fusion.7 = bf16[256,64]{0,1:T(8,128)(2,1)S(1)} fusion(bf16[1,256,4096]{2,1,0:T(8,128)(2,1)S(1)} %copy-done, bf16[1,4096,64]{1,2,0:T(8,128)(2,1)} %param.9), kind=kOutput, calls=%fused_computation.5 | convolution fusion | flops 134234112 | bytes 2654208 | tf_op jit(solution)/shard_map/dot_general | solution.py:266
  6.9 1.5 %collective-permute-start = (f32[64,128]{1,0:T(8,128)S(1)}, f32[64,128]{1,0:T(8,128)S(1)}, u32[]{:S(2)}, u32[]{:S(2)}) collective-permute-start(f32[64,128]{1,0:T(8,128)S(1)} %pad_maximum_fusion), channel_id=1, source_target_pairs={{0,8},{8,0},{1,9},{9,1},{2,10},{10,2},{3,11},{11,3},{4,12},{12,4},... | collective-permute-start | bytes 98312 | tf_op jit(solution)/shard_map/ppermute | solution.py:206
  9.2 6.0 %collective-permute-start.3 = (bf16[32,4096]{1,0:T(8,128)(2,1)S(1)}, bf16[32,4096]{1,0:T(8,128)(2,1)S(1)}, u32[]{:S(2)}, u32[]{:S(2)}) collective-permute-start(bf16[32,4096]{1,0:T(8,128)(2,1)S(1)} %bitcast.64), channel_id=1, source_target_pairs={{0,64},{8,200},{16,80},{24,216},{32,96},{40,232},{48,112},{56,248}... | collective-permute-start | bytes 786440 | tf_op jit(solution)/shard_map/ppermute | solution.py:221
  17.4 2.6 %collective-permute-done.1 = f32[64,128]{1,0:T(8,128)S(1)} collective-permute-done((f32[64,128]{1,0:T(8,128)S(1)}, f32[64,128]{1,0:T(8,128)S(1)}, u32[]{:S(2)}, u32[]{:S(2)}) %collective-permute-start.1) | collective-permute-done | bytes 32800 | tf_op jit(solution)/shard_map/ppermute | solution.py:206
  20.3 3.5 %shard_map.86.refs_0_ = bf16[6,4096,128]{2,1,0:T(8,128)(2,1)} custom-call(bf16[768,4096]{1,0:T(8,128)(2,1)} %bitcast.57), custom_call_target="tpu_custom_call" | custom-call | bytes 1024 | tf_op jit(solution)/shard_map/pallas_call | solution.py:39
  24.3 2.8 %collective-permute-done.5.second = bf16[32,4096]{1,0:T(8,128)(2,1)S(1)} collective-permute-done((bf16[32,4096]{1,0:T(8,128)(2,1)}, bf16[32,4096]{1,0:T(8,128)(2,1)S(1)}, u32[]{:S(2)}, u32[]{:S(2)}) %collective-permute-start.5) | collective-permute-done | bytes 262176 | tf_op jit(solution)/shard_map/ppermute | solution.py:221
  27.8 1.9 %shard_map.89.refs_8_ = bf16[64,4096]{1,0:T(8,128)(2,1)} custom-call(bf16[32,4096]{1,0:T(8,128)(2,1)} %copy-done.12, bf16[32,4096]{1,0:T(8,128)(2,1)} %copy-done.13), custom_call_target="tpu_custom_call" | custom-call | bytes 1024 | tf_op jit(solution)/shard_map/pallas_call | solution.py:230
  29.7 1.5 %collective-permute-start.7 = (f32[64,128]{1,0:T(8,128)S(1)}, f32[64,128]{1,0:T(8,128)S(1)}, u32[]{:S(2)}, u32[]{:S(2)}) collective-permute-start(f32[64,128]{1,0:T(8,128)S(1)} %add.441), channel_id=1, source_target_pairs={{0,64},{64,0},{128,192},{192,128},{1,65},{65,1},{129,193},{193,129... | collective-permute-start | bytes 98312 | tf_op jit(solution)/shard_map/ppermute | solution.py:206
  32.2 4.2 %collective-permute-start.8 = (bf16[32,4096]{1,0:T(8,128)(2,1)}, bf16[32,4096]{1,0:T(8,128)(2,1)}, u32[]{:S(2)}, u32[]{:S(2)}) collective-permute-start(bf16[32,4096]{1,0:T(8,128)(2,1)} %copy-done.12), channel_id=1, source_target_pairs={{0,64},{8,200},{16,80},{24,216},{32,96},{40,232},{48,112},{56,248}... | collective-permute-start | bytes 786440 | tf_op jit(solution)/shard_map/ppermute | solution.py:221
  36.4 1.3 %collective-permute-start.9 = (bf16[32,4096]{1,0:T(8,128)(2,1)}, bf16[32,4096]{1,0:T(8,128)(2,1)}, u32[]{:S(2)}, u32[]{:S(2)}) collective-permute-start(bf16[32,4096]{1,0:T(8,128)(2,1)} %collective-permute-done.6.refs_2_), channel_id=1, source_target_pairs={{0,16},{8,56},{16,32},{24,8},{32,48},{40,24},{48,0},{56,40},{64,80... | collective-permute-start | bytes 786440 | tf_op jit(solution)/shard_map/ppermute | solution.py:221
  38.2 3.4 %shard_map.87.refs_0_ = bf16[6,4096,128]{2,1,0:T(8,128)(2,1)} custom-call(bf16[768,4096]{1,0:T(8,128)(2,1)} %bitcast.58, bf16[6,4096,128]{2,1,0:T(8,128)(2,1)} %shard_map.86.refs_0_), custom_call_target="tpu_custom_call", output_to_operand_aliasing={{}: (1, {})} | custom-call | bytes 1024 | tf_op jit(solution)/shard_map/pallas_call | solution.py:39
  41.6 3.4 %shard_map.88.x_ref = bf16[6,4096,128]{2,1,0:T(8,128)(2,1)} custom-call(bf16[768,4096]{1,0:T(8,128)(2,1)} %bitcast.59, bf16[6,4096,128]{2,1,0:T(8,128)(2,1)} %shard_map.87.refs_0_), custom_call_target="tpu_custom_call", output_to_operand_aliasing={{}: (1, {})} | custom-call | bytes 1024 | tf_op jit(solution)/shard_map/pallas_call | solution.py:39
  45.7 2.9 %collective-permute-start.18 = (bf16[32,4096]{1,0:T(8,128)(2,1)}, bf16[32,4096]{1,0:T(8,128)(2,1)S(1)}, u32[]{:S(2)}, u32[]{:S(2)}) collective-permute-start(bf16[32,4096]{1,0:T(8,128)(2,1)} %collective-permute-done.6.refs_2_), channel_id=1, source_target_pairs={{0,8},{8,0},{1,9},{9,1},{2,10},{10,2},{3,11},{11,3},{4,12},{12,4},... | collective-permute-start | bytes 786440 | tf_op jit(solution)/shard_map/ppermute | solution.py:210
  51.4 1.4 %collective-permute-start.13 = (bf16[32,4096]{1,0:T(8,128)(2,1)}, bf16[32,4096]{1,0:T(8,128)(2,1)}, u32[]{:S(2)}, u32[]{:S(2)}) collective-permute-start(bf16[32,4096]{1,0:T(8,128)(2,1)} %collective-permute-done.8.refs_10_), channel_id=1, source_target_pairs={{0,16},{8,56},{16,32},{24,8},{32,48},{40,24},{48,0},{56,40},{64,80... | collective-permute-start | bytes 786440 | tf_op jit(solution)/shard_map/ppermute | solution.py:221
  54.0 5.4 %shard_map.90 = (bf16[256,256]{1,0:T(8,128)(2,1)}, bf16[256,256]{1,0:T(8,128)(2,1)}) custom-call(f32[64,128]{1,0:T(8,128)} %add.443.s_ref), custom_call_target="tpu_custom_call" | custom-call | bytes 1024 | tf_op jit(solution)/shard_map/pallas_call | solution.py:197
  59.4 2.5 %collective-permute-start.21 = (bf16[64,4096]{1,0:T(8,128)(2,1)S(1)}, bf16[64,4096]{1,0:T(8,128)(2,1)S(1)}, u32[]{:S(2)}, u32[]{:S(2)}) collective-permute-start(bf16[64,4096]{1,0:T(8,128)(2,1)S(1)} %collective-permute-done.12.refs_12_), channel_id=1, source_target_pairs={{0,16},{8,56},{16,32},{24,8},{32,48},{40,24},{48,0},{56,40},{64,80... | collective-permute-start | bytes 1572872 | tf_op jit(solution)/shard_map/ppermute | solution.py:221
  62.7 2.5 %collective-permute-start.24 = (bf16[64,4096]{1,0:T(8,128)(2,1)}, bf16[64,4096]{1,0:T(8,128)(2,1)}, u32[]{:S(2)}, u32[]{:S(2)}) collective-permute-start(bf16[64,4096]{1,0:T(8,128)(2,1)} %collective-permute-done.17.refs_13_), channel_id=1, source_target_pairs={{0,8},{8,0},{1,9},{9,1},{2,10},{10,2},{3,11},{11,3},{4,12},{12,4},... | collective-permute-start | bytes 1572872 | tf_op jit(solution)/shard_map/ppermute | solution.py:210
  65.7 8.7 %shard_map.91.w_ref = bf16[3,4096,256]{2,1,0:T(8,128)(2,1)} custom-call(bf16[6,4096,128]{2,1,0:T(8,128)(2,1)} %shard_map.88.x_ref, bf16[256,256]{1,0:T(8,128)(2,1)} %get-tuple-element.48.a_ref, bf16[256,256]{1,0:T(8,128)(2,1)} %get-tuple-element.49.b_ref), custom_call_target="tpu_custom_call" | custom-call | bytes 1024 | tf_op jit(solution)/shard_map/pallas_call | solution.py:77
  75.2 2.0 %collective-permute-done.28.refs_23_ = bf16[32,4096]{1,0:T(8,128)(2,1)S(1)} collective-permute-done((bf16[32,4096]{1,0:T(8,128)(2,1)}, bf16[32,4096]{1,0:T(8,128)(2,1)S(1)}, u32[]{:S(2)}, u32[]{:S(2)}) %collective-permute-start.28) | collective-permute-done | bytes 262176 | tf_op jit(solution)/shard_map/ppermute | solution.py:210
  78.7 13.2 %shard_map.92 = bf16[1024,768]{1,0:T(8,128)(2,1)} custom-call(s32[32]{0:T(128)} %select_reduce_fusion.pos_ref, bf16[3,4096,256]{2,1,0:T(8,128)(2,1)} %shard_map.91.w_ref, bf16[32,4096]{1,0:T(8,128)(2,1)} %bitcast.62, bf16[32,4096]{1,0:T(8,128)(2,1)} %collective-permute-done.4.refs_1_, bf16[32,4096]{1,0:T(8,128)(2,1)} %collective-permute-done.6.refs_2_, ...), custom_call_target="tpu_custom_call" | custom-call | bytes 1024 | tf_op jit(solution)/shard_map/pallas_call | solution.py:119
  92.0 4.3 %all-to-all-start = ((bf16[8,128,768]{2,1,0:T(8,128)(2,1)}), bf16[8,128,768]{2,1,0:T(8,128)(2,1)}, u32[]{:S(2)}, u32[]{:S(2)}) async-start(bf16[8,128,768]{2,1,0:T(8,128)(2,1)} %bitcast.60), calls=%async_computation | async-start | bytes 3145728 | tf_op jit(solution)/shard_map/all_to_all | solution.py:313
  97.1 19.9 %all-to-all-done.part_ref = bf16[8,128,768]{2,1,0:T(8,128)(2,1)} async-done(((bf16[8,128,768]{2,1,0:T(8,128)(2,1)}), bf16[8,128,768]{2,1,0:T(8,128)(2,1)}, u32[]{:S(2)}, u32[]{:S(2)}) %all-to-all-start) | async-done | bytes 1572896 | tf_op jit(solution)/shard_map/all_to_all | solution.py:313
  117.1 2.1 %shard_map.93 = f32[128,768]{1,0:T(8,128)} custom-call(bf16[8,128,768]{2,1,0:T(8,128)(2,1)} %all-to-all-done.part_ref), custom_call_target="tpu_custom_call" | custom-call | bytes 1024 | tf_op jit(solution)/shard_map/pallas_call | solution.py:147
  (88 shorter events, 16.3 us)
Async XLA Ops:
  0.7 14.7 %collective-permute-start.4 = (bf16[32,4096]{1,0:T(8,128)(2,1)}, bf16[32,4096]{1,0:T(8,128)(2,1)}, u32[]{:S(2)}, u32[]{:S(2)}) collective-permute-start(bf16[32,4096]{1,0:T(8,128)(2,1)} %bitcast.61), channel_id=1, source_target_pairs={{0,8},{8,0},{1,9},{9,1},{2,10},{10,2},{3,11},{11,3},{4,12},{12,4},... | collective-permute-start | bytes 786440 | tf_op jit(solution)/shard_map/ppermute | solution.py:210
  6.9 9.6 %collective-permute-start = (f32[64,128]{1,0:T(8,128)S(1)}, f32[64,128]{1,0:T(8,128)S(1)}, u32[]{:S(2)}, u32[]{:S(2)}) collective-permute-start(f32[64,128]{1,0:T(8,128)S(1)} %pad_maximum_fusion), channel_id=1, source_target_pairs={{0,8},{8,0},{1,9},{9,1},{2,10},{10,2},{3,11},{11,3},{4,12},{12,4},... | collective-permute-start | bytes 98312 | tf_op jit(solution)/shard_map/ppermute | solution.py:206
  8.4 15.8 %collective-permute-start.6 = (bf16[32,4096]{1,0:T(8,128)(2,1)S(1)}, bf16[32,4096]{1,0:T(8,128)(2,1)}, u32[]{:S(2)}, u32[]{:S(2)}) collective-permute-start(bf16[32,4096]{1,0:T(8,128)(2,1)S(1)} %bitcast.63), channel_id=1, source_target_pairs={{0,16},{8,56},{16,32},{24,8},{32,48},{40,24},{48,0},{56,40},{64,80... | collective-permute-start | bytes 786440 | tf_op jit(solution)/shard_map/ppermute | solution.py:221
  9.2 15.1 %collective-permute-start.3 = (bf16[32,4096]{1,0:T(8,128)(2,1)S(1)}, bf16[32,4096]{1,0:T(8,128)(2,1)S(1)}, u32[]{:S(2)}, u32[]{:S(2)}) collective-permute-start(bf16[32,4096]{1,0:T(8,128)(2,1)S(1)} %bitcast.64), channel_id=1, source_target_pairs={{0,64},{8,200},{16,80},{24,216},{32,96},{40,232},{48,112},{56,248}... | collective-permute-start | bytes 786440 | tf_op jit(solution)/shard_map/ppermute | solution.py:221
  15.3 11.8 %collective-permute-start.5 = (bf16[32,4096]{1,0:T(8,128)(2,1)}, bf16[32,4096]{1,0:T(8,128)(2,1)S(1)}, u32[]{:S(2)}, u32[]{:S(2)}) collective-permute-start(bf16[32,4096]{1,0:T(8,128)(2,1)} %collective-permute-done.4.refs_1_), channel_id=1, source_target_pairs={{0,64},{8,200},{16,80},{24,216},{32,96},{40,232},{48,112},{56,248}... | collective-permute-start | bytes 786440 | tf_op jit(solution)/shard_map/ppermute | solution.py:221
  29.7 18.8 %collective-permute-start.16 = (bf16[64,4096]{1,0:T(8,128)(2,1)}, bf16[64,4096]{1,0:T(8,128)(2,1)S(1)}, u32[]{:S(2)}, u32[]{:S(2)}) collective-permute-start(bf16[64,4096]{1,0:T(8,128)(2,1)} %shard_map.89.refs_8_), channel_id=1, source_target_pairs={{0,8},{8,0},{1,9},{9,1},{2,10},{10,2},{3,11},{11,3},{4,12},{12,4},... | collective-permute-start | bytes 1572872 | tf_op jit(solution)/shard_map/ppermute | solution.py:210
  29.7 8.0 %collective-permute-start.7 = (f32[64,128]{1,0:T(8,128)S(1)}, f32[64,128]{1,0:T(8,128)S(1)}, u32[]{:S(2)}, u32[]{:S(2)}) collective-permute-start(f32[64,128]{1,0:T(8,128)S(1)} %add.441), channel_id=1, source_target_pairs={{0,64},{64,0},{128,192},{192,128},{1,65},{65,1},{129,193},{193,129... | collective-permute-start | bytes 98312 | tf_op jit(solution)/shard_map/ppermute | solution.py:206
  31.2 13.9 %collective-permute-start.10 = (bf16[32,4096]{1,0:T(8,128)(2,1)}, bf16[32,4096]{1,0:T(8,128)(2,1)S(1)}, u32[]{:S(2)}, u32[]{:S(2)}) collective-permute-start(bf16[32,4096]{1,0:T(8,128)(2,1)} %collective-permute-done.4.refs_1_), channel_id=1, source_target_pairs={{0,16},{8,56},{16,32},{24,8},{32,48},{40,24},{48,0},{56,40},{64,80... | collective-permute-start | bytes 786440 | tf_op jit(solution)/shard_map/ppermute | solution.py:221
  32.2 12.9 %collective-permute-start.8 = (bf16[32,4096]{1,0:T(8,128)(2,1)}, bf16[32,4096]{1,0:T(8,128)(2,1)}, u32[]{:S(2)}, u32[]{:S(2)}) collective-permute-start(bf16[32,4096]{1,0:T(8,128)(2,1)} %copy-done.12), channel_id=1, source_target_pairs={{0,64},{8,200},{16,80},{24,216},{32,96},{40,232},{48,112},{56,248}... | collective-permute-start | bytes 786440 | tf_op jit(solution)/shard_map/ppermute | solution.py:221
  36.4 8.7 %collective-permute-start.9 = (bf16[32,4096]{1,0:T(8,128)(2,1)}, bf16[32,4096]{1,0:T(8,128)(2,1)}, u32[]{:S(2)}, u32[]{:S(2)}) collective-permute-start(bf16[32,4096]{1,0:T(8,128)(2,1)} %collective-permute-done.6.refs_2_), channel_id=1, source_target_pairs={{0,16},{8,56},{16,32},{24,8},{32,48},{40,24},{48,0},{56,40},{64,80... | collective-permute-start | bytes 786440 | tf_op jit(solution)/shard_map/ppermute | solution.py:221
  37.7 13.4 %collective-permute-start.12 = (bf16[64,4096]{1,0:T(8,128)(2,1)}, bf16[64,4096]{1,0:T(8,128)(2,1)S(1)}, u32[]{:S(2)}, u32[]{:S(2)}) collective-permute-start(bf16[64,4096]{1,0:T(8,128)(2,1)} %shard_map.89.refs_8_), channel_id=1, source_target_pairs={{0,16},{8,56},{16,32},{24,8},{32,48},{40,24},{48,0},{56,40},{64,80... | collective-permute-start | bytes 1572872 | tf_op jit(solution)/shard_map/ppermute | solution.py:221
  45.1 5.1 %collective-permute-start.11 = (f32[64,128]{1,0:T(8,128)S(1)}, f32[64,128]{1,0:T(8,128)S(1)}, u32[]{:S(2)}, u32[]{:S(2)}) collective-permute-start(f32[64,128]{1,0:T(8,128)S(1)} %add.442), channel_id=1, source_target_pairs={{0,192},{64,128},{128,64},{192,0},{1,193},{65,129},{129,65},{193,1... | collective-permute-start | bytes 98312 | tf_op jit(solution)/shard_map/ppermute | solution.py:206
  45.7 5.8 %collective-permute-start.18 = (bf16[32,4096]{1,0:T(8,128)(2,1)}, bf16[32,4096]{1,0:T(8,128)(2,1)S(1)}, u32[]{:S(2)}, u32[]{:S(2)}) collective-permute-start(bf16[32,4096]{1,0:T(8,128)(2,1)} %collective-permute-done.6.refs_2_), channel_id=1, source_target_pairs={{0,8},{8,0},{1,9},{9,1},{2,10},{10,2},{3,11},{11,3},{4,12},{12,4},... | collective-permute-start | bytes 786440 | tf_op jit(solution)/shard_map/ppermute | solution.py:210
  48.5 14.1 %collective-permute-start.17 = (bf16[64,4096]{1,0:T(8,128)(2,1)S(1)}, bf16[64,4096]{1,0:T(8,128)(2,1)}, u32[]{:S(2)}, u32[]{:S(2)}) collective-permute-start(bf16[64,4096]{1,0:T(8,128)(2,1)S(1)} %collective-permute-done.16.refs_9_), channel_id=1, source_target_pairs={{0,16},{8,56},{16,32},{24,8},{32,48},{40,24},{48,0},{56,40},{64,80... | collective-permute-start | bytes 1572872 | tf_op jit(solution)/shard_map/ppermute | solution.py:221
  51.1 8.3 %collective-permute-start.20 = (bf16[32,4096]{1,0:T(8,128)(2,1)}, bf16[32,4096]{1,0:T(8,128)(2,1)}, u32[]{:S(2)}, u32[]{:S(2)}) collective-permute-start(bf16[32,4096]{1,0:T(8,128)(2,1)} %collective-permute-done.9.refs_4_), channel_id=1, source_target_pairs={{0,8},{8,0},{1,9},{9,1},{2,10},{10,2},{3,11},{11,3},{4,12},{12,4},... | collective-permute-start | bytes 786440 | tf_op jit(solution)/shard_map/ppermute | solution.py:210
  51.4 10.5 %collective-permute-start.13 = (bf16[32,4096]{1,0:T(8,128)(2,1)}, bf16[32,4096]{1,0:T(8,128)(2,1)}, u32[]{:S(2)}, u32[]{:S(2)}) collective-permute-start(bf16[32,4096]{1,0:T(8,128)(2,1)} %collective-permute-done.8.refs_10_), channel_id=1, source_target_pairs={{0,16},{8,56},{16,32},{24,8},{32,48},{40,24},{48,0},{56,40},{64,80... | collective-permute-start | bytes 786440 | tf_op jit(solution)/shard_map/ppermute | solution.py:221
  52.8 9.8 %collective-permute-start.15 = (bf16[32,4096]{1,0:T(8,128)(2,1)}, bf16[32,4096]{1,0:T(8,128)(2,1)}, u32[]{:S(2)}, u32[]{:S(2)}) collective-permute-start(bf16[32,4096]{1,0:T(8,128)(2,1)} %collective-permute-done.14.refs_11_), channel_id=1, source_target_pairs={{0,16},{8,56},{16,32},{24,8},{32,48},{40,24},{48,0},{56,40},{64,80... | collective-permute-start | bytes 786440 | tf_op jit(solution)/shard_map/ppermute | solution.py:221
  53.9 11.8 %collective-permute-start.23 = (bf16[64,4096]{1,0:T(8,128)(2,1)S(1)}, bf16[64,4096]{1,0:T(8,128)(2,1)}, u32[]{:S(2)}, u32[]{:S(2)}) collective-permute-start(bf16[64,4096]{1,0:T(8,128)(2,1)S(1)} %collective-permute-done.12.refs_12_), channel_id=1, source_target_pairs={{0,8},{8,0},{1,9},{9,1},{2,10},{10,2},{3,11},{11,3},{4,12},{12,4},... | collective-permute-start | bytes 1572872 | tf_op jit(solution)/shard_map/ppermute | solution.py:210
  59.4 14.9 %collective-permute-start.21 = (bf16[64,4096]{1,0:T(8,128)(2,1)S(1)}, bf16[64,4096]{1,0:T(8,128)(2,1)S(1)}, u32[]{:S(2)}, u32[]{:S(2)}) collective-permute-start(bf16[64,4096]{1,0:T(8,128)(2,1)S(1)} %collective-permute-done.12.refs_12_), channel_id=1, source_target_pairs={{0,16},{8,56},{16,32},{24,8},{32,48},{40,24},{48,0},{56,40},{64,80... | collective-permute-start | bytes 1572872 | tf_op jit(solution)/shard_map/ppermute | solution.py:221
  62.7 11.7 %collective-permute-start.24 = (bf16[64,4096]{1,0:T(8,128)(2,1)}, bf16[64,4096]{1,0:T(8,128)(2,1)}, u32[]{:S(2)}, u32[]{:S(2)}) collective-permute-start(bf16[64,4096]{1,0:T(8,128)(2,1)} %collective-permute-done.17.refs_13_), channel_id=1, source_target_pairs={{0,8},{8,0},{1,9},{9,1},{2,10},{10,2},{3,11},{11,3},{4,12},{12,4},... | collective-permute-start | bytes 1572872 | tf_op jit(solution)/shard_map/ppermute | solution.py:210
  65.2 9.2 %collective-permute-start.26 = (bf16[32,4096]{1,0:T(8,128)(2,1)}, bf16[32,4096]{1,0:T(8,128)(2,1)}, u32[]{:S(2)}, u32[]{:S(2)}) collective-permute-start(bf16[32,4096]{1,0:T(8,128)(2,1)} %collective-permute-done.15.refs_15_), channel_id=1, source_target_pairs={{0,8},{8,0},{1,9},{9,1},{2,10},{10,2},{3,11},{11,3},{4,12},{12,4},... | collective-permute-start | bytes 786440 | tf_op jit(solution)/shard_map/ppermute | solution.py:210
  65.2 9.2 %collective-permute-start.25 = (bf16[32,4096]{1,0:T(8,128)(2,1)}, bf16[32,4096]{1,0:T(8,128)(2,1)}, u32[]{:S(2)}, u32[]{:S(2)}) collective-permute-start(bf16[32,4096]{1,0:T(8,128)(2,1)} %collective-permute-done.13.refs_14_), channel_id=1, source_target_pairs={{0,8},{8,0},{1,9},{9,1},{2,10},{10,2},{3,11},{11,3},{4,12},{12,4},... | collective-permute-start | bytes 786440 | tf_op jit(solution)/shard_map/ppermute | solution.py:210
  65.7 8.7 %collective-permute-start.22 = (bf16[32,4096]{1,0:T(8,128)(2,1)}, bf16[32,4096]{1,0:T(8,128)(2,1)}, u32[]{:S(2)}, u32[]{:S(2)}) collective-permute-start(bf16[32,4096]{1,0:T(8,128)(2,1)} %collective-permute-done.13.refs_14_), channel_id=1, source_target_pairs={{0,16},{8,56},{16,32},{24,8},{32,48},{40,24},{48,0},{56,40},{64,80... | collective-permute-start | bytes 786440 | tf_op jit(solution)/shard_map/ppermute | solution.py:221
  92.0 25.1 %all-to-all-start = ((bf16[8,128,768]{2,1,0:T(8,128)(2,1)}), bf16[8,128,768]{2,1,0:T(8,128)(2,1)}, u32[]{:S(2)}, u32[]{:S(2)}) async-start(bf16[8,128,768]{2,1,0:T(8,128)(2,1)} %bitcast.60), calls=%async_computation | async-start | bytes 3145728 | tf_op jit(solution)/shard_map/all_to_all | solution.py:313
  (21 other events, 136.2 us)

commit v6 on v5

--- a/solution.py
+++ b/solution.py
@@ -87,29 +87,49 @@
 
 
 def score_kernel(moves, count, pos_ref, w_ref, *refs):
-    pieces, y_ref, rows, sems = refs[:count], refs[count], refs[count + 1], refs[count + 2]
+    pieces, y_ref = refs[:count], refs[count]
+    rows, partial, sems = refs[count + 1 :]
+    half = rows.shape[1] // 2
     first = pl.program_id(0) == 0
+    bands = [slice(256 * g, 256 * g + 256) for g in range(rows.shape[0] // 256)]
+
+    def dot(band, depth):
+        return jnp.dot(
+            rows[band, depth], w_ref[0, depth, :], preferred_element_type=jnp.float32
+        )
 
     @pl.when(first)
     def _():
-        copies = []
-        for n, (piece, start) in enumerate(moves):
-            place = pl.multiple_of(pos_ref[n] * 32, 32)
-            copies.append(
-                pltpu.make_async_copy(
-                    pieces[piece].at[pl.ds(start, 32)], rows.at[pl.ds(place, 32)], sems.at[n]
+        sides = []
+        for side in range(2):
+            columns = pl.ds(side * half, half)
+            copies = []
+            for n, (piece, start) in enumerate(moves):
+                place = pl.multiple_of(pos_ref[n] * 32, 32)
+                copies.append(
+                    pltpu.make_async_copy(
+                        pieces[piece].at[pl.ds(start, 32), columns],
+                        rows.at[pl.ds(place, 32), columns],
+                        sems.at[side * len(moves) + n],
+                    )
                 )
-            )
-        for copy in copies:
+            sides.append(copies)
+        for copy in sides[0] + sides[1]:
             copy.start()
-        for copy in copies:
+        for copy in sides[0]:
             copy.wait()
-
-    for g in range(rows.shape[0] // 256):
-        band = slice(256 * g, 256 * g + 256)
-        y_ref[band, :] = jnp.dot(
-            rows[band, :], w_ref[0], preferred_element_type=jnp.float32
-        ).astype(jnp.bfloat16)
+        for band in bands:
+            partial[band, :] = dot(band, slice(0, half))
+        for copy in sides[1]:
+            copy.wait()
+        for band in bands:
+            total = partial[band, :] + dot(band, slice(half, 2 * half))
+            y_ref[band, :] = total.astype(jnp.bfloat16)
+
+    @pl.when(jnp.logical_not(first))
+    def _():
+        for band in bands:
+            y_ref[band, :] = dot(band, slice(0, 2 * half)).astype(jnp.bfloat16)
 
 
 def score(pieces, pos, weighed):
@@ -128,7 +148,8 @@
         out_shape=jax.ShapeDtypeStruct((total, chunks * 256), jnp.bfloat16),
         scratch_shapes=[
             pltpu.VMEM((total, width), jnp.bfloat16),
-            pltpu.SemaphoreType.DMA((len(moves),)),
+            pltpu.VMEM((total, 256), jnp.float32),
+            pltpu.SemaphoreType.DMA((2 * len(moves),)),
         ],
         compiler_params=params(),
         cost_estimate=LIGHT,

time: 120 us -> 119 us (level)
  transfers between devices with their start and end apart: 30 -> 30, of which waited for: 7 -> 7; matrix products, arithmetic and copies ran while one was open for 4% -> 4% of each run, Pallas kernels for 20% -> 21%
where the time goes in v6:
time: 119 us; the launch traced here: 118 us
  Pallas kernels  40.9 us (34%)
  starting transfers between devices  39 us (33%)
  waiting for transfers between devices  29.4 us (25%)
  local copies, waits for them, and re-layouts  3.82 us (3%)
  matrix products  2.94 us (2%)
  other arithmetic  1.5 us (1%)
    ppermute x12, starting transfers between devices, onward(): return lax.ppermute(value, DP, pairs)  20.1 us
    all_to_all x1, waiting for transfers between devices, on_device(): lax.all_to_all(ordered, SECTION, split_axis=0, concat_axis=0, tiled=True)  19.9 us
    pallas_call x1, Pallas kernels, score(): pl.pallas_call(functools.partial(score_kernel, moves, len(pieces)), grid=...  12.4 us
    ppermute x12, starting transfers between devices, twin(): return lax.ppermute(value, 'core', [(0, 1), (1, 0)])  10.7 us
    pallas_call x3, Pallas kernels, shuffle(): pl.pallas_call(shuffle_kernel, grid=(count,), in_specs=specs + ([] if hel...  10.3 us
    pallas_call x1, Pallas kernels, weigh(): pl.pallas_call(weigh_kernel, grid=(chunks // 2,), in_specs=[pl.BlockSpec(...  8.66 us
    pallas_call x1, Pallas kernels, inverses(): pl.pallas_call(functools.partial(inverse_kernel, tokens), out_shape=[jax....  5.39 us
    all_to_all x1, starting transfers between devices, on_device(): lax.all_to_all(ordered, SECTION, split_axis=0, concat_axis=0, tiled=True)  4.31 us
  transfers between devices with their start and end apart: 30, of which 7 were waited for; matrix products, arithmetic and copies ran while one was open for 4% of the time, Pallas kernels for 21%

profile of v6, /device:TPU:1, one launch (start us, length us, event | category | flops | bytes accessed | tf_op | source)
XLA Modules:
  0.0 118.5 jit_solution(1187813427090162338)
XLA Ops:
  0.7 3.3 %collective-permute-start.4 = (bf16[32,4096]{1,0:T(8,128)(2,1)}, bf16[32,4096]{1,0:T(8,128)(2,1)}, u32[]{:S(2)}, u32[]{:S(2)}) collective-permute-start(bf16[32,4096]{1,0:T(8,128)(2,1)} %bitcast.61), channel_id=1, source_target_pairs={{0,8},{8,0},{1,9},{9,1},{2,10},{10,2},{3,11},{11,3},{4,12},{12,4},... | collective-permute-start | bytes 786440 | tf_op jit(solution)/shard_map/ppermute | solution.py:231
  4.0 1.8 %fusion.7 = bf16[256,64]{0,1:T(8,128)(2,1)S(1)} fusion(bf16[1,256,4096]{2,1,0:T(8,128)(2,1)S(1)} %copy-done, bf16[1,4096,64]{1,2,0:T(8,128)(2,1)} %param.9), kind=kOutput, calls=%fused_computation.5 | convolution fusion | flops 134234112 | bytes 2654208 | tf_op jit(solution)/shard_map/dot_general | solution.py:287
  6.9 1.5 %collective-permute-start = (f32[64,128]{1,0:T(8,128)S(1)}, f32[64,128]{1,0:T(8,128)S(1)}, u32[]{:S(2)}, u32[]{:S(2)}) collective-permute-start(f32[64,128]{1,0:T(8,128)S(1)} %pad_maximum_fusion), channel_id=1, source_target_pairs={{0,8},{8,0},{1,9},{9,1},{2,10},{10,2},{3,11},{11,3},{4,12},{12,4},... | collective-permute-start | bytes 98312 | tf_op jit(solution)/shard_map/ppermute | solution.py:227
  9.2 6.0 %collective-permute-start.3 = (bf16[32,4096]{1,0:T(8,128)(2,1)S(1)}, bf16[32,4096]{1,0:T(8,128)(2,1)S(1)}, u32[]{:S(2)}, u32[]{:S(2)}) collective-permute-start(bf16[32,4096]{1,0:T(8,128)(2,1)S(1)} %bitcast.64), channel_id=1, source_target_pairs={{0,64},{8,200},{16,80},{24,216},{32,96},{40,232},{48,112},{56,248}... | collective-permute-start | bytes 786440 | tf_op jit(solution)/shard_map/ppermute | solution.py:242
  17.4 2.6 %collective-permute-done.1 = f32[64,128]{1,0:T(8,128)S(1)} collective-permute-done((f32[64,128]{1,0:T(8,128)S(1)}, f32[64,128]{1,0:T(8,128)S(1)}, u32[]{:S(2)}, u32[]{:S(2)}) %collective-permute-start.1) | collective-permute-done | bytes 32800 | tf_op jit(solution)/shard_map/ppermute | solution.py:227
  20.3 3.5 %shard_map.86.refs_0_ = bf16[6,4096,128]{2,1,0:T(8,128)(2,1)} custom-call(bf16[768,4096]{1,0:T(8,128)(2,1)} %bitcast.57), custom_call_target="tpu_custom_call" | custom-call | bytes 1024 | tf_op jit(solution)/shard_map/pallas_call | solution.py:39
  24.3 2.8 %collective-permute-done.5.second = bf16[32,4096]{1,0:T(8,128)(2,1)S(1)} collective-permute-done((bf16[32,4096]{1,0:T(8,128)(2,1)}, bf16[32,4096]{1,0:T(8,128)(2,1)S(1)}, u32[]{:S(2)}, u32[]{:S(2)}) %collective-permute-start.5) | collective-permute-done | bytes 262176 | tf_op jit(solution)/shard_map/ppermute | solution.py:242
  27.8 1.9 %shard_map.89.refs_8_ = bf16[64,4096]{1,0:T(8,128)(2,1)} custom-call(bf16[32,4096]{1,0:T(8,128)(2,1)} %copy-done.12, bf16[32,4096]{1,0:T(8,128)(2,1)} %copy-done.13), custom_call_target="tpu_custom_call" | custom-call | bytes 1024 | tf_op jit(solution)/shard_map/pallas_call | solution.py:251
  29.7 1.5 %collective-permute-start.7 = (f32[64,128]{1,0:T(8,128)S(1)}, f32[64,128]{1,0:T(8,128)S(1)}, u32[]{:S(2)}, u32[]{:S(2)}) collective-permute-start(f32[64,128]{1,0:T(8,128)S(1)} %add.441), channel_id=1, source_target_pairs={{0,64},{64,0},{128,192},{192,128},{1,65},{65,1},{129,193},{193,129... | collective-permute-start | bytes 98312 | tf_op jit(solution)/shard_map/ppermute | solution.py:227
  32.2 4.2 %collective-permute-start.8 = (bf16[32,4096]{1,0:T(8,128)(2,1)}, bf16[32,4096]{1,0:T(8,128)(2,1)}, u32[]{:S(2)}, u32[]{:S(2)}) collective-permute-start(bf16[32,4096]{1,0:T(8,128)(2,1)} %copy-done.12), channel_id=1, source_target_pairs={{0,64},{8,200},{16,80},{24,216},{32,96},{40,232},{48,112},{56,248}... | collective-permute-start | bytes 786440 | tf_op jit(solution)/shard_map/ppermute | solution.py:242
  36.4 1.3 %collective-permute-start.9 = (bf16[32,4096]{1,0:T(8,128)(2,1)}, bf16[32,4096]{1,0:T(8,128)(2,1)}, u32[]{:S(2)}, u32[]{:S(2)}) collective-permute-start(bf16[32,4096]{1,0:T(8,128)(2,1)} %collective-permute-done.6.refs_2_), channel_id=1, source_target_pairs={{0,16},{8,56},{16,32},{24,8},{32,48},{40,24},{48,0},{56,40},{64,80... | collective-permute-start | bytes 786440 | tf_op jit(solution)/shard_map/ppermute | solution.py:242
  38.2 3.4 %shard_map.87.refs_0_ = bf16[6,4096,128]{2,1,0:T(8,128)(2,1)} custom-call(bf16[768,4096]{1,0:T(8,128)(2,1)} %bitcast.58, bf16[6,4096,128]{2,1,0:T(8,128)(2,1)} %shard_map.86.refs_0_), custom_call_target="tpu_custom_call", output_to_operand_aliasing={{}: (1, {})} | custom-call | bytes 1024 | tf_op jit(solution)/shard_map/pallas_call | solution.py:39
  41.6 3.4 %shard_map.88.x_ref = bf16[6,4096,128]{2,1,0:T(8,128)(2,1)} custom-call(bf16[768,4096]{1,0:T(8,128)(2,1)} %bitcast.59, bf16[6,4096,128]{2,1,0:T(8,128)(2,1)} %shard_map.87.refs_0_), custom_call_target="tpu_custom_call", output_to_operand_aliasing={{}: (1, {})} | custom-call | bytes 1024 | tf_op jit(solution)/shard_map/pallas_call | solution.py:39
  45.7 2.9 %collective-permute-start.18 = (bf16[32,4096]{1,0:T(8,128)(2,1)}, bf16[32,4096]{1,0:T(8,128)(2,1)S(1)}, u32[]{:S(2)}, u32[]{:S(2)}) collective-permute-start(bf16[32,4096]{1,0:T(8,128)(2,1)} %collective-permute-done.6.refs_2_), channel_id=1, source_target_pairs={{0,8},{8,0},{1,9},{9,1},{2,10},{10,2},{3,11},{11,3},{4,12},{12,4},... | collective-permute-start | bytes 786440 | tf_op jit(solution)/shard_map/ppermute | solution.py:231
  51.4 1.4 %collective-permute-start.13 = (bf16[32,4096]{1,0:T(8,128)(2,1)}, bf16[32,4096]{1,0:T(8,128)(2,1)}, u32[]{:S(2)}, u32[]{:S(2)}) collective-permute-start(bf16[32,4096]{1,0:T(8,128)(2,1)} %collective-permute-done.8.refs_10_), channel_id=1, source_target_pairs={{0,16},{8,56},{16,32},{24,8},{32,48},{40,24},{48,0},{56,40},{64,80... | collective-permute-start | bytes 786440 | tf_op jit(solution)/shard_map/ppermute | solution.py:242
  54.0 5.4 %shard_map.90 = (bf16[256,256]{1,0:T(8,128)(2,1)}, bf16[256,256]{1,0:T(8,128)(2,1)}) custom-call(f32[64,128]{1,0:T(8,128)} %add.443.s_ref), custom_call_target="tpu_custom_call" | custom-call | bytes 1024 | tf_op jit(solution)/shard_map/pallas_call | solution.py:218
  59.4 2.5 %collective-permute-start.21 = (bf16[64,4096]{1,0:T(8,128)(2,1)S(1)}, bf16[64,4096]{1,0:T(8,128)(2,1)S(1)}, u32[]{:S(2)}, u32[]{:S(2)}) collective-permute-start(bf16[64,4096]{1,0:T(8,128)(2,1)S(1)} %collective-permute-done.12.refs_12_), channel_id=1, source_target_pairs={{0,16},{8,56},{16,32},{24,8},{32,48},{40,24},{48,0},{56,40},{64,80... | collective-permute-start | bytes 1572872 | tf_op jit(solution)/shard_map/ppermute | solution.py:242
  62.7 2.5 %collective-permute-start.24 = (bf16[64,4096]{1,0:T(8,128)(2,1)}, bf16[64,4096]{1,0:T(8,128)(2,1)}, u32[]{:S(2)}, u32[]{:S(2)}) collective-permute-start(bf16[64,4096]{1,0:T(8,128)(2,1)} %collective-permute-done.17.refs_13_), channel_id=1, source_target_pairs={{0,8},{8,0},{1,9},{9,1},{2,10},{10,2},{3,11},{11,3},{4,12},{12,4},... | collective-permute-start | bytes 1572872 | tf_op jit(solution)/shard_map/ppermute | solution.py:231
  65.7 8.7 %shard_map.91.w_ref = bf16[3,4096,256]{2,1,0:T(8,128)(2,1)} custom-call(bf16[6,4096,128]{2,1,0:T(8,128)(2,1)} %shard_map.88.x_ref, bf16[256,256]{1,0:T(8,128)(2,1)} %get-tuple-element.48.a_ref, bf16[256,256]{1,0:T(8,128)(2,1)} %get-tuple-element.49.b_ref), custom_call_target="tpu_custom_call" | custom-call | bytes 1024 | tf_op jit(solution)/shard_map/pallas_call | solution.py:77
  75.2 2.0 %collective-permute-done.28.refs_23_ = bf16[32,4096]{1,0:T(8,128)(2,1)S(1)} collective-permute-done((bf16[32,4096]{1,0:T(8,128)(2,1)}, bf16[32,4096]{1,0:T(8,128)(2,1)S(1)}, u32[]{:S(2)}, u32[]{:S(2)}) %collective-permute-start.28) | collective-permute-done | bytes 262176 | tf_op jit(solution)/shard_map/ppermute | solution.py:231
  78.7 12.4 %shard_map.92 = bf16[1024,768]{1,0:T(8,128)(2,1)} custom-call(s32[32]{0:T(128)} %select_reduce_fusion.pos_ref, bf16[3,4096,256]{2,1,0:T(8,128)(2,1)} %shard_map.91.w_ref, bf16[32,4096]{1,0:T(8,128)(2,1)} %bitcast.62, bf16[32,4096]{1,0:T(8,128)(2,1)} %collective-permute-done.4.refs_1_, bf16[32,4096]{1,0:T(8,128)(2,1)} %collective-permute-done.6.refs_2_, ...), custom_call_target="tpu_custom_call" | custom-call | bytes 1024 | tf_op jit(solution)/shard_map/pallas_call | solution.py:139
  91.2 4.3 %all-to-all-start = ((bf16[8,128,768]{2,1,0:T(8,128)(2,1)}), bf16[8,128,768]{2,1,0:T(8,128)(2,1)}, u32[]{:S(2)}, u32[]{:S(2)}) async-start(bf16[8,128,768]{2,1,0:T(8,128)(2,1)} %bitcast.60), calls=%async_computation | async-start | bytes 3145728 | tf_op jit(solution)/shard_map/all_to_all | solution.py:334
  96.4 19.9 %all-to-all-done.part_ref = bf16[8,128,768]{2,1,0:T(8,128)(2,1)} async-done(((bf16[8,128,768]{2,1,0:T(8,128)(2,1)}), bf16[8,128,768]{2,1,0:T(8,128)(2,1)}, u32[]{:S(2)}, u32[]{:S(2)}) %all-to-all-start) | async-done | bytes 1572896 | tf_op jit(solution)/shard_map/all_to_all | solution.py:334
  116.3 2.1 %shard_map.93 = f32[128,768]{1,0:T(8,128)} custom-call(bf16[8,128,768]{2,1,0:T(8,128)(2,1)} %all-to-all-done.part_ref), custom_call_target="tpu_custom_call" | custom-call | bytes 1024 | tf_op jit(solution)/shard_map/pallas_call | solution.py:168
  (88 shorter events, 16.3 us)
Async XLA Ops:
  0.7 14.7 %collective-permute-start.4 = (bf16[32,4096]{1,0:T(8,128)(2,1)}, bf16[32,4096]{1,0:T(8,128)(2,1)}, u32[]{:S(2)}, u32[]{:S(2)}) collective-permute-start(bf16[32,4096]{1,0:T(8,128)(2,1)} %bitcast.61), channel_id=1, source_target_pairs={{0,8},{8,0},{1,9},{9,1},{2,10},{10,2},{3,11},{11,3},{4,12},{12,4},... | collective-permute-start | bytes 786440 | tf_op jit(solution)/shard_map/ppermute | solution.py:231
  6.9 9.6 %collective-permute-start = (f32[64,128]{1,0:T(8,128)S(1)}, f32[64,128]{1,0:T(8,128)S(1)}, u32[]{:S(2)}, u32[]{:S(2)}) collective-permute-start(f32[64,128]{1,0:T(8,128)S(1)} %pad_maximum_fusion), channel_id=1, source_target_pairs={{0,8},{8,0},{1,9},{9,1},{2,10},{10,2},{3,11},{11,3},{4,12},{12,4},... | collective-permute-start | bytes 98312 | tf_op jit(solution)/shard_map/ppermute | solution.py:227
  8.4 15.8 %collective-permute-start.6 = (bf16[32,4096]{1,0:T(8,128)(2,1)S(1)}, bf16[32,4096]{1,0:T(8,128)(2,1)}, u32[]{:S(2)}, u32[]{:S(2)}) collective-permute-start(bf16[32,4096]{1,0:T(8,128)(2,1)S(1)} %bitcast.63), channel_id=1, source_target_pairs={{0,16},{8,56},{16,32},{24,8},{32,48},{40,24},{48,0},{56,40},{64,80... | collective-permute-start | bytes 786440 | tf_op jit(solution)/shard_map/ppermute | solution.py:242
  9.2 15.1 %collective-permute-start.3 = (bf16[32,4096]{1,0:T(8,128)(2,1)S(1)}, bf16[32,4096]{1,0:T(8,128)(2,1)S(1)}, u32[]{:S(2)}, u32[]{:S(2)}) collective-permute-start(bf16[32,4096]{1,0:T(8,128)(2,1)S(1)} %bitcast.64), channel_id=1, source_target_pairs={{0,64},{8,200},{16,80},{24,216},{32,96},{40,232},{48,112},{56,248}... | collective-permute-start | bytes 786440 | tf_op jit(solution)/shard_map/ppermute | solution.py:242
  15.3 11.8 %collective-permute-start.5 = (bf16[32,4096]{1,0:T(8,128)(2,1)}, bf16[32,4096]{1,0:T(8,128)(2,1)S(1)}, u32[]{:S(2)}, u32[]{:S(2)}) collective-permute-start(bf16[32,4096]{1,0:T(8,128)(2,1)} %collective-permute-done.4.refs_1_), channel_id=1, source_target_pairs={{0,64},{8,200},{16,80},{24,216},{32,96},{40,232},{48,112},{56,248}... | collective-permute-start | bytes 786440 | tf_op jit(solution)/shard_map/ppermute | solution.py:242
  29.7 18.8 %collective-permute-start.16 = (bf16[64,4096]{1,0:T(8,128)(2,1)}, bf16[64,4096]{1,0:T(8,128)(2,1)S(1)}, u32[]{:S(2)}, u32[]{:S(2)}) collective-permute-start(bf16[64,4096]{1,0:T(8,128)(2,1)} %shard_map.89.refs_8_), channel_id=1, source_target_pairs={{0,8},{8,0},{1,9},{9,1},{2,10},{10,2},{3,11},{11,3},{4,12},{12,4},... | collective-permute-start | bytes 1572872 | tf_op jit(solution)/shard_map/ppermute | solution.py:231
  29.7 8.0 %collective-permute-start.7 = (f32[64,128]{1,0:T(8,128)S(1)}, f32[64,128]{1,0:T(8,128)S(1)}, u32[]{:S(2)}, u32[]{:S(2)}) collective-permute-start(f32[64,128]{1,0:T(8,128)S(1)} %add.441), channel_id=1, source_target_pairs={{0,64},{64,0},{128,192},{192,128},{1,65},{65,1},{129,193},{193,129... | collective-permute-start | bytes 98312 | tf_op jit(solution)/shard_map/ppermute | solution.py:227
  31.2 13.9 %collective-permute-start.10 = (bf16[32,4096]{1,0:T(8,128)(2,1)}, bf16[32,4096]{1,0:T(8,128)(2,1)S(1)}, u32[]{:S(2)}, u32[]{:S(2)}) collective-permute-start(bf16[32,4096]{1,0:T(8,128)(2,1)} %collective-permute-done.4.refs_1_), channel_id=1, source_target_pairs={{0,16},{8,56},{16,32},{24,8},{32,48},{40,24},{48,0},{56,40},{64,80... | collective-permute-start | bytes 786440 | tf_op jit(solution)/shard_map/ppermute | solution.py:242
  32.2 12.9 %collective-permute-start.8 = (bf16[32,4096]{1,0:T(8,128)(2,1)}, bf16[32,4096]{1,0:T(8,128)(2,1)}, u32[]{:S(2)}, u32[]{:S(2)}) collective-permute-start(bf16[32,4096]{1,0:T(8,128)(2,1)} %copy-done.12), channel_id=1, source_target_pairs={{0,64},{8,200},{16,80},{24,216},{32,96},{40,232},{48,112},{56,248}... | collective-permute-start | bytes 786440 | tf_op jit(solution)/shard_map/ppermute | solution.py:242
  36.4 8.7 %collective-permute-start.9 = (bf16[32,4096]{1,0:T(8,128)(2,1)}, bf16[32,4096]{1,0:T(8,128)(2,1)}, u32[]{:S(2)}, u32[]{:S(2)}) collective-permute-start(bf16[32,4096]{1,0:T(8,128)(2,1)} %collective-permute-done.6.refs_2_), channel_id=1, source_target_pairs={{0,16},{8,56},{16,32},{24,8},{32,48},{40,24},{48,0},{56,40},{64,80... | collective-permute-start | bytes 786440 | tf_op jit(solution)/shard_map/ppermute | solution.py:242
  37.7 13.4 %collective-permute-start.12 = (bf16[64,4096]{1,0:T(8,128)(2,1)}, bf16[64,4096]{1,0:T(8,128)(2,1)S(1)}, u32[]{:S(2)}, u32[]{:S(2)}) collective-permute-start(bf16[64,4096]{1,0:T(8,128)(2,1)} %shard_map.89.refs_8_), channel_id=1, source_target_pairs={{0,16},{8,56},{16,32},{24,8},{32,48},{40,24},{48,0},{56,40},{64,80... | collective-permute-start | bytes 1572872 | tf_op jit(solution)/shard_map/ppermute | solution.py:242
  45.1 5.1 %collective-permute-start.11 = (f32[64,128]{1,0:T(8,128)S(1)}, f32[64,128]{1,0:T(8,128)S(1)}, u32[]{:S(2)}, u32[]{:S(2)}) collective-permute-start(f32[64,128]{1,0:T(8,128)S(1)} %add.442), channel_id=1, source_target_pairs={{0,192},{64,128},{128,64},{192,0},{1,193},{65,129},{129,65},{193,1... | collective-permute-start | bytes 98312 | tf_op jit(solution)/shard_map/ppermute | solution.py:227
  45.7 5.8 %collective-permute-start.18 = (bf16[32,4096]{1,0:T(8,128)(2,1)}, bf16[32,4096]{1,0:T(8,128)(2,1)S(1)}, u32[]{:S(2)}, u32[]{:S(2)}) collective-permute-start(bf16[32,4096]{1,0:T(8,128)(2,1)} %collective-permute-done.6.refs_2_), channel_id=1, source_target_pairs={{0,8},{8,0},{1,9},{9,1},{2,10},{10,2},{3,11},{11,3},{4,12},{12,4},... | collective-permute-start | bytes 786440 | tf_op jit(solution)/shard_map/ppermute | solution.py:231
  48.5 14.1 %collective-permute-start.17 = (bf16[64,4096]{1,0:T(8,128)(2,1)S(1)}, bf16[64,4096]{1,0:T(8,128)(2,1)}, u32[]{:S(2)}, u32[]{:S(2)}) collective-permute-start(bf16[64,4096]{1,0:T(8,128)(2,1)S(1)} %collective-permute-done.16.refs_9_), channel_id=1, source_target_pairs={{0,16},{8,56},{16,32},{24,8},{32,48},{40,24},{48,0},{56,40},{64,80... | collective-permute-start | bytes 1572872 | tf_op jit(solution)/shard_map/ppermute | solution.py:242
  51.1 8.3 %collective-permute-start.20 = (bf16[32,4096]{1,0:T(8,128)(2,1)}, bf16[32,4096]{1,0:T(8,128)(2,1)}, u32[]{:S(2)}, u32[]{:S(2)}) collective-permute-start(bf16[32,4096]{1,0:T(8,128)(2,1)} %collective-permute-done.9.refs_4_), channel_id=1, source_target_pairs={{0,8},{8,0},{1,9},{9,1},{2,10},{10,2},{3,11},{11,3},{4,12},{12,4},... | collective-permute-start | bytes 786440 | tf_op jit(solution)/shard_map/ppermute | solution.py:231
  51.4 10.5 %collective-permute-start.13 = (bf16[32,4096]{1,0:T(8,128)(2,1)}, bf16[32,4096]{1,0:T(8,128)(2,1)}, u32[]{:S(2)}, u32[]{:S(2)}) collective-permute-start(bf16[32,4096]{1,0:T(8,128)(2,1)} %collective-permute-done.8.refs_10_), channel_id=1, source_target_pairs={{0,16},{8,56},{16,32},{24,8},{32,48},{40,24},{48,0},{56,40},{64,80... | collective-permute-start | bytes 786440 | tf_op jit(solution)/shard_map/ppermute | solution.py:242
  52.8 9.8 %collective-permute-start.15 = (bf16[32,4096]{1,0:T(8,128)(2,1)}, bf16[32,4096]{1,0:T(8,128)(2,1)}, u32[]{:S(2)}, u32[]{:S(2)}) collective-permute-start(bf16[32,4096]{1,0:T(8,128)(2,1)} %collective-permute-done.14.refs_11_), channel_id=1, source_target_pairs={{0,16},{8,56},{16,32},{24,8},{32,48},{40,24},{48,0},{56,40},{64,80... | collective-permute-start | bytes 786440 | tf_op jit(solution)/shard_map/ppermute | solution.py:242
  53.9 11.8 %collective-permute-start.23 = (bf16[64,4096]{1,0:T(8,128)(2,1)S(1)}, bf16[64,4096]{1,0:T(8,128)(2,1)}, u32[]{:S(2)}, u32[]{:S(2)}) collective-permute-start(bf16[64,4096]{1,0:T(8,128)(2,1)S(1)} %collective-permute-done.12.refs_12_), channel_id=1, source_target_pairs={{0,8},{8,0},{1,9},{9,1},{2,10},{10,2},{3,11},{11,3},{4,12},{12,4},... | collective-permute-start | bytes 1572872 | tf_op jit(solution)/shard_map/ppermute | solution.py:231
  59.4 14.9 %collective-permute-start.21 = (bf16[64,4096]{1,0:T(8,128)(2,1)S(1)}, bf16[64,4096]{1,0:T(8,128)(2,1)S(1)}, u32[]{:S(2)}, u32[]{:S(2)}) collective-permute-start(bf16[64,4096]{1,0:T(8,128)(2,1)S(1)} %collective-permute-done.12.refs_12_), channel_id=1, source_target_pairs={{0,16},{8,56},{16,32},{24,8},{32,48},{40,24},{48,0},{56,40},{64,80... | collective-permute-start | bytes 1572872 | tf_op jit(solution)/shard_map/ppermute | solution.py:242
  62.7 11.7 %collective-permute-start.24 = (bf16[64,4096]{1,0:T(8,128)(2,1)}, bf16[64,4096]{1,0:T(8,128)(2,1)}, u32[]{:S(2)}, u32[]{:S(2)}) collective-permute-start(bf16[64,4096]{1,0:T(8,128)(2,1)} %collective-permute-done.17.refs_13_), channel_id=1, source_target_pairs={{0,8},{8,0},{1,9},{9,1},{2,10},{10,2},{3,11},{11,3},{4,12},{12,4},... | collective-permute-start | bytes 1572872 | tf_op jit(solution)/shard_map/ppermute | solution.py:231
  65.2 9.2 %collective-permute-start.26 = (bf16[32,4096]{1,0:T(8,128)(2,1)}, bf16[32,4096]{1,0:T(8,128)(2,1)}, u32[]{:S(2)}, u32[]{:S(2)}) collective-permute-start(bf16[32,4096]{1,0:T(8,128)(2,1)} %collective-permute-done.15.refs_15_), channel_id=1, source_target_pairs={{0,8},{8,0},{1,9},{9,1},{2,10},{10,2},{3,11},{11,3},{4,12},{12,4},... | collective-permute-start | bytes 786440 | tf_op jit(solution)/shard_map/ppermute | solution.py:231
  65.2 9.2 %collective-permute-start.25 = (bf16[32,4096]{1,0:T(8,128)(2,1)}, bf16[32,4096]{1,0:T(8,128)(2,1)}, u32[]{:S(2)}, u32[]{:S(2)}) collective-permute-start(bf16[32,4096]{1,0:T(8,128)(2,1)} %collective-permute-done.13.refs_14_), channel_id=1, source_target_pairs={{0,8},{8,0},{1,9},{9,1},{2,10},{10,2},{3,11},{11,3},{4,12},{12,4},... | collective-permute-start | bytes 786440 | tf_op jit(solution)/shard_map/ppermute | solution.py:231
  65.7 8.7 %collective-permute-start.22 = (bf16[32,4096]{1,0:T(8,128)(2,1)}, bf16[32,4096]{1,0:T(8,128)(2,1)}, u32[]{:S(2)}, u32[]{:S(2)}) collective-permute-start(bf16[32,4096]{1,0:T(8,128)(2,1)} %collective-permute-done.13.refs_14_), channel_id=1, source_target_pairs={{0,16},{8,56},{16,32},{24,8},{32,48},{40,24},{48,0},{56,40},{64,80... | collective-permute-start | bytes 786440 | tf_op jit(solution)/shard_map/ppermute | solution.py:242
  91.2 25.1 %all-to-all-start = ((bf16[8,128,768]{2,1,0:T(8,128)(2,1)}), bf16[8,128,768]{2,1,0:T(8,128)(2,1)}, u32[]{:S(2)}, u32[]{:S(2)}) async-start(bf16[8,128,768]{2,1,0:T(8,128)(2,1)} %bitcast.60), calls=%async_computation | async-start | bytes 3145728 | tf_op jit(solution)/shard_map/all_to_all | solution.py:334
  (21 other events, 136.2 us)
